TPU v7x, 32 devices: a whole 2x2x4 slice. The times are simulated.
32 devices in a mesh: sp: 4 (over z), fsdp: 8 (over y, x, core).
Axes of the slice: x: 2, y: 2, z: 4, core: 2. Of those that a mesh axis runs over, the one named last changes fastest.
Arguments:
- tokens: bfloat16 [16384, 1024], P(('fsdp', 'sp')), may hold values from -72 to 72
- documents: int32 [16384], replicated, may hold values from 0 to 14, as said below
- expert_routes: int32 [16384, 8], P(('fsdp', 'sp')), may hold values from 0 to 31, all different within a row
- drop_rank: int32 [16384, 8], P(('fsdp', 'sp')), may hold values from 0 to 4095, as said below
- norm1_gain: bfloat16 [1024], P('fsdp'), may hold values from 0.5 to 1.5
- query_weight: bfloat16 [1024, 1024], P('fsdp'), may hold values from -0.75 to 0.75
- key_weight: bfloat16 [1024, 512], P('fsdp'), may hold values from -0.75 to 0.75
- value_weight: bfloat16 [1024, 512], P('fsdp'), may hold values from -0.1875 to 0.1875
- out_weight: bfloat16 [1024, 1024], P('fsdp'), may hold values from -2 to 2
- norm2_gain: bfloat16 [1024], P('fsdp'), may hold values from 0.5 to 1.5
- router_weight: bfloat16 [1024, 32], P('fsdp'), may hold values from -0.09375 to 0.09375
- gate_weight: bfloat16 [32, 1024, 512], P('fsdp'), may hold values from -0.1875 to 0.1875
- up_weight: bfloat16 [32, 1024, 512], P('fsdp'), may hold values from -0.1875 to 0.1875
- down_weight: bfloat16 [32, 512, 1024], P('fsdp'), may hold values from -4 to 4
- output_grad: bfloat16 [16384, 1024], P(('fsdp', 'sp')), may hold values from -6 to 6
Outputs:
- output: bfloat16 [16384, 1024], P(('fsdp', 'sp'))
- input_grad: bfloat16 [16384, 1024], P(('fsdp', 'sp'))
- grad_norm1: float32 [1024], P('fsdp')
- grad_query: float32 [1024, 1024], P('fsdp')
- grad_key: float32 [1024, 512], P('fsdp')
- grad_value: float32 [1024, 512], P('fsdp')
- grad_out: float32 [1024, 1024], P('fsdp')
- grad_norm2: float32 [1024], P('fsdp')
- grad_router: float32 [1024, 32], P('fsdp')
- grad_gate: float32 [32, 1024, 512], P('fsdp')
- grad_up: float32 [32, 1024, 512], P('fsdp')
- grad_down: float32 [32, 512, 1024], P('fsdp')
Inputs may be any that keep to these rules, and one draw needn't show every extreme that they name: `documents`: document numbers start at 0, never fall and rise by at most one from a token to the next; a document holds at most 2048 tokens and one holds exactly 2048; no document begins at a positive multiple of 2048. `expert_routes`: each row names 8 different experts. `drop_rank`: within each aligned block of 512 rows the entries are the numbers 0 to 4095, each once.
All inputs are finite; a program needn't handle non-finite values.
Results may differ from a plain program's by a relative error of at most 0.02.
Values may be sent and summed in bfloat16 or wider, within the bound.
No kernel may reach another device: no remote copies, remote signals or barrier semaphores. Data moves between devices by JAX's collectives and lax.ppermute only.
A program may use at most 256 MiB of HBM per device.

v0:
```python
import jax
import jax.numpy as jnp
from jax import lax
from jax.sharding import PartitionSpec as P

HD = 64
DOC_CAP = 2048


attend_scale = 0.015625
branch_scale = 0.22
norm_eps = 1e-06
rope_base = 10000.0
masked_score = -1e30


def from_behind(value, axis, steps):
    count = lax.axis_size(axis)
    initial, last = (max(0, -steps), min(count, count - steps))
    return lax.ppermute(value, axis, [(source, source + steps) for source in range(initial, last)])


def doc_position(documents):
    length = documents.shape[0]
    place = jnp.arange(length, dtype=jnp.int32)
    fresh = jnp.concatenate([jnp.ones((1,), dtype=bool), documents[1:] != documents[:-1]])
    opening = lax.cummax(jnp.where(fresh, place, 0), axis=0)
    return place - opening


def rope_tables(position, head_size):
    half_size = head_size // 2
    spacing = jnp.arange(half_size, dtype=jnp.float32)
    inverse = rope_base ** (-2.0 * spacing / head_size)
    angle = position.astype(jnp.float32)[:, None] * inverse[None, :]
    return (jnp.tile(jnp.cos(angle), (1, 2)), jnp.tile(jnp.sin(angle), (1, 2)))


def rotate(values, cosine, sine_table):
    half_size = values.shape[-1] // 2
    turned = jnp.concatenate([-values[..., half_size:], values[..., :half_size]], axis=-1)
    return values * cosine[:, None, :] + turned * sine_table[:, None, :]


def route_slots(routes, rank_table, experts, capacity):
    flat_routes = routes.reshape(-1)
    flat_ranks = rank_table.reshape(-1)
    ordered = flat_routes[jnp.argsort(flat_ranks)]
    onehot = (ordered[:, None] == jnp.arange(experts, dtype=jnp.int32)[None, :]).astype(jnp.int32)
    earlier = jnp.cumsum(onehot, axis=0) - onehot
    slot_sorted = jnp.sum(earlier * onehot, axis=1)
    slot_number = slot_sorted[flat_ranks].reshape(routes.shape)
    kept_pair = slot_number < capacity
    return (jnp.where(kept_pair, routes * capacity + slot_number, -1), kept_pair)


def to_owner(values):
    return lax.all_to_all(values, "fsdp", split_axis=0, concat_axis=1, tiled=True)


def from_owner(values):
    return lax.all_to_all(values, "fsdp", split_axis=1, concat_axis=0, tiled=True)


def expert_forward(slot_rows, gate_mats, up_mats, down_mats):
    gate_lin = jnp.einsum("nrd,ndf->nrf", slot_rows, gate_mats, preferred_element_type=jnp.float32)
    up_lin = jnp.einsum("nrd,ndf->nrf", slot_rows, up_mats, preferred_element_type=jnp.float32)
    inner = (gate_lin * jax.nn.sigmoid(gate_lin) * up_lin).astype(jnp.bfloat16)
    result = jnp.einsum(
        "nrf,nfd->nrd", inner, down_mats, preferred_element_type=jnp.float32
    ).astype(jnp.bfloat16)
    return (gate_lin, up_lin, result)


def expert_backward(slot_rows, gate_lin, up_lin, result_grad, gate_mats, up_mats, down_mats):
    sigma = jax.nn.sigmoid(gate_lin)
    swished = gate_lin * sigma
    inner = (swished * up_lin).astype(jnp.bfloat16)
    inner_grad = jnp.einsum(
        "nrd,nfd->nrf", result_grad, down_mats, preferred_element_type=jnp.float32
    )
    gate_grad = (inner_grad * up_lin * sigma * (1.0 + gate_lin * (1.0 - sigma))).astype(
        jnp.bfloat16
    )
    up_grad = (inner_grad * swished).astype(jnp.bfloat16)
    rows_grad = jnp.einsum("nrf,ndf->nrd", gate_grad, gate_mats, preferred_element_type=jnp.float32)
    rows_grad = (
        rows_grad + jnp.einsum("nrf,ndf->nrd", up_grad, up_mats, preferred_element_type=jnp.float32)
    ).astype(jnp.bfloat16)
    gate_part = jnp.einsum("nrd,nrf->ndf", slot_rows, gate_grad, preferred_element_type=jnp.float32)
    up_part = jnp.einsum("nrd,nrf->ndf", slot_rows, up_grad, preferred_element_type=jnp.float32)
    down_part = jnp.einsum("nrf,nrd->nfd", inner, result_grad, preferred_element_type=jnp.float32)
    return (rows_grad, gate_part, up_part, down_part)


def local(
    tokens,
    documents,
    expert_routes,
    drop_rank,
    norm1_gain,
    query_weight,
    key_weight,
    value_weight,
    out_weight,
    norm2_gain,
    router_weight,
    gate_weight,
    up_weight,
    down_weight,
    output_grad,
):
    rows_dev, model_width = tokens.shape
    heads_query = query_weight.shape[1] // HD
    heads_kv = key_weight.shape[1] // HD
    repeat = heads_query // heads_kv
    experts = router_weight.shape[1]
    top_count = expert_routes.shape[1]
    seq_parts = lax.axis_size("sp")
    span_rows = seq_parts * rows_dev
    query_block = min(512, span_rows)
    block_count = span_rows // query_block
    doc_most = min(DOC_CAP, span_rows)
    window = doc_most + query_block
    capacity = (9 * rows_dev * top_count + 8 * experts - 1) // (8 * experts)
    slot_total = experts * capacity
    block_start = lax.axis_index("fsdp") * span_rows
    row_start = block_start + lax.axis_index("sp") * rows_dev
    position = lax.dynamic_slice_in_dim(doc_position(documents), row_start, rows_dev)
    cosine, sine_table = rope_tables(position, HD)
    gain_first, query_mat, key_mat, value_mat, out_mat, gain_second, router_mat = (
        lax.all_gather(norm1_gain, "fsdp", axis=0, tiled=True),
        lax.all_gather(query_weight, "fsdp", axis=0, tiled=True),
        lax.all_gather(key_weight, "fsdp", axis=0, tiled=True),
        lax.all_gather(value_weight, "fsdp", axis=0, tiled=True),
        lax.all_gather(out_weight, "fsdp", axis=0, tiled=True),
        lax.all_gather(norm2_gain, "fsdp", axis=0, tiled=True),
        lax.all_gather(router_weight, "fsdp", axis=0, tiled=True),
    )
    stream = tokens.astype(jnp.float32)
    inverse_one = lax.rsqrt(jnp.mean(stream * stream, axis=-1, keepdims=True) + norm_eps)
    gain_one = gain_first.astype(jnp.float32)
    normed_one = (stream * inverse_one * gain_one).astype(jnp.bfloat16)
    query_lin = jnp.dot(normed_one, query_mat, preferred_element_type=jnp.float32).reshape(
        rows_dev, heads_query, HD
    )
    key_lin = jnp.dot(normed_one, key_mat, preferred_element_type=jnp.float32).reshape(
        rows_dev, heads_kv, HD
    )
    value_low = (
        jnp.dot(normed_one, value_mat, preferred_element_type=jnp.float32)
        .astype(jnp.bfloat16)
        .reshape(rows_dev, heads_kv, HD)
    )
    query_low = (
        rotate(query_lin, cosine, sine_table)
        .astype(jnp.bfloat16)
        .reshape(rows_dev, heads_kv, repeat * HD)
    )
    key_low = rotate(key_lin, cosine, sine_table).astype(jnp.bfloat16)
    packed = jnp.concatenate([query_low, key_low, value_low], axis=-1)
    by_heads = lax.all_to_all(packed, "sp", split_axis=1, concat_axis=0, tiled=True)
    groups = by_heads.shape[1]
    query_heads = by_heads[:, :, : repeat * HD]
    pair_heads = by_heads[:, :, repeat * HD :]
    halo_rows = from_behind(pair_heads[span_rows - doc_most :], "fsdp", 1)
    near_pairs = jnp.concatenate([halo_rows, pair_heads], axis=0)
    query_docs = lax.dynamic_slice_in_dim(documents, block_start, span_rows)
    near_docs = lax.dynamic_slice_in_dim(
        jnp.concatenate([jnp.full((doc_most,), -1, jnp.int32), documents]),
        block_start,
        doc_most + span_rows,
    )
    causal = jnp.arange(window)[None, :] <= jnp.arange(query_block)[:, None] + doc_most

    def block_scores(block_index):
        first_row = block_index * query_block
        query_part = lax.dynamic_slice_in_dim(query_heads, first_row, query_block).reshape(
            query_block, groups, repeat, HD
        )
        pair_part = lax.dynamic_slice_in_dim(near_pairs, first_row, window)
        key_part = pair_part[:, :, :HD]
        value_part = pair_part[:, :, HD:]
        own_docs = lax.dynamic_slice_in_dim(query_docs, first_row, query_block)
        seen_docs = lax.dynamic_slice_in_dim(near_docs, first_row, window)
        allowed = (seen_docs[None, :] == own_docs[:, None]) & causal
        scores = attend_scale * jnp.einsum(
            "rgjd,cgd->gjrc", query_part, key_part, preferred_element_type=jnp.float32
        )
        return (query_part, key_part, value_part, jnp.where(allowed, scores, masked_score))

    def attend_block(block_index):
        query_part, key_part, value_part, scores = block_scores(block_index)
        row_max = jnp.max(scores, axis=-1, keepdims=True)
        exponent = jnp.exp(scores - row_max)
        row_total = jnp.sum(exponent, axis=-1, keepdims=True)
        softmaxed = (exponent / row_total).astype(jnp.bfloat16)
        blended = jnp.einsum(
            "gjrc,cgd->rgjd", softmaxed, value_part, preferred_element_type=jnp.float32
        )
        return (
            blended.astype(jnp.bfloat16).reshape(query_block, groups, repeat * HD),
            (row_max + jnp.log(row_total))[..., 0],
        )

    blended_all, log_totals = lax.map(attend_block, jnp.arange(block_count, dtype=jnp.int32))
    attended = lax.all_to_all(
        blended_all.reshape(span_rows, groups, repeat * HD),
        "sp",
        split_axis=0,
        concat_axis=1,
        tiled=True,
    ).reshape(rows_dev, heads_query * HD)
    branch = jnp.dot(attended, out_mat, preferred_element_type=jnp.float32)
    hidden_one = stream + branch_scale * branch
    inverse_two = lax.rsqrt(jnp.mean(hidden_one * hidden_one, axis=-1, keepdims=True) + norm_eps)
    gain_two = gain_second.astype(jnp.float32)
    normed_two = (hidden_one * inverse_two * gain_two).astype(jnp.bfloat16)
    logits = jnp.dot(normed_two, router_mat, preferred_element_type=jnp.float32)
    route_hot = expert_routes[:, :, None] == jnp.arange(experts, dtype=jnp.int32)[None, None, :]
    chosen = jnp.sum(jnp.where(route_hot, logits[:, None, :], 0.0), axis=-1)
    chosen_max = jnp.max(chosen, axis=-1, keepdims=True)
    gate_exp = jnp.exp(chosen - chosen_max)
    gates = gate_exp / jnp.sum(gate_exp, axis=-1, keepdims=True)
    gate_low = gates.astype(jnp.bfloat16)
    slot_index, kept_pair = route_slots(expert_routes, drop_rank, experts, capacity)
    columns = jnp.arange(slot_total, dtype=jnp.int32)[None, :]
    dispatch = jnp.zeros((rows_dev, slot_total), dtype=bool)
    combine = jnp.zeros((rows_dev, slot_total), dtype=jnp.bfloat16)
    for route_slot in range(top_count):
        landing = slot_index[:, route_slot : route_slot + 1] == columns
        dispatch = dispatch | landing
        combine = combine + jnp.where(
            landing, gate_low[:, route_slot : route_slot + 1], jnp.zeros((), jnp.bfloat16)
        )
    dispatch_low = dispatch.astype(jnp.bfloat16)
    expert_in = (
        jnp.einsum("tc,td->cd", dispatch_low, normed_two, preferred_element_type=jnp.float32)
        .astype(jnp.bfloat16)
        .reshape(experts, capacity, model_width)
    )
    owned_in = to_owner(expert_in)
    gate_lin, up_lin, owned_out = expert_forward(owned_in, gate_weight, up_weight, down_weight)
    expert_out = from_owner(owned_out)
    mixture = jnp.dot(
        combine, expert_out.reshape(slot_total, model_width), preferred_element_type=jnp.float32
    )
    output = (hidden_one + branch_scale * mixture).astype(jnp.bfloat16)
    cotangent = output_grad.astype(jnp.float32)
    mixture_grad = (branch_scale * cotangent).astype(jnp.bfloat16)
    out_grad = (
        jnp.einsum("tc,td->cd", combine, mixture_grad, preferred_element_type=jnp.float32)
        .astype(jnp.bfloat16)
        .reshape(experts, capacity, model_width)
    )
    taken = jnp.take(
        expert_out.reshape(slot_total, model_width), jnp.clip(slot_index, 0, slot_total - 1), axis=0
    )
    gate_grad = jnp.where(
        kept_pair,
        jnp.einsum("tkd,td->tk", taken, mixture_grad, preferred_element_type=jnp.float32),
        0.0,
    )
    chosen_grad = gates * (gate_grad - jnp.sum(gates * gate_grad, axis=-1, keepdims=True))
    logit_grad = jnp.sum(jnp.where(route_hot, chosen_grad[:, :, None], 0.0), axis=1).astype(
        jnp.bfloat16
    )
    router_grad = jnp.einsum(
        "td,te->de", normed_two, logit_grad, preferred_element_type=jnp.float32
    )
    normed_two_grad = jnp.einsum(
        "te,de->td", logit_grad, router_mat, preferred_element_type=jnp.float32
    )
    owned_grad = to_owner(out_grad)
    owned_in_grad, expert_gate_grad, expert_up_grad, expert_down_grad = expert_backward(
        owned_in, gate_lin, up_lin, owned_grad, gate_weight, up_weight, down_weight
    )
    expert_in_grad = from_owner(owned_in_grad)
    normed_two_grad = normed_two_grad + jnp.dot(
        dispatch_low,
        expert_in_grad.reshape(slot_total, model_width),
        preferred_element_type=jnp.float32,
    )
    scaled_two = normed_two_grad * gain_two
    hidden_grad = (
        cotangent
        + inverse_two * scaled_two
        - hidden_one * inverse_two**3 * jnp.mean(hidden_one * scaled_two, axis=-1, keepdims=True)
    )
    norm_two_grad = jnp.sum(normed_two_grad * hidden_one * inverse_two, axis=0)
    branch_grad = (branch_scale * hidden_grad).astype(jnp.bfloat16)
    out_mat_grad = jnp.einsum(
        "tk,td->kd", attended, branch_grad, preferred_element_type=jnp.float32
    )
    attended_grad = jnp.einsum(
        "td,kd->tk", branch_grad, out_mat, preferred_element_type=jnp.float32
    ).astype(jnp.bfloat16)
    grad_heads = lax.all_to_all(
        attended_grad.reshape(rows_dev, heads_kv, repeat * HD),
        "sp",
        split_axis=1,
        concat_axis=0,
        tiled=True,
    )

    def attend_back(accumulated, block_item):
        block_index, log_total = block_item
        query_part, key_part, value_part, scores = block_scores(block_index)
        first_row = block_index * query_block
        softmaxed = jnp.exp(scores - log_total[..., None])
        incoming = lax.dynamic_slice_in_dim(grad_heads, first_row, query_block).reshape(
            query_block, groups, repeat, HD
        )
        softmax_grad = jnp.einsum(
            "rgjd,cgd->gjrc", incoming, value_part, preferred_element_type=jnp.float32
        )
        centred = jnp.sum(softmaxed * softmax_grad, axis=-1, keepdims=True)
        score_grad = (softmaxed * (softmax_grad - centred)).astype(jnp.bfloat16)
        query_grad = attend_scale * jnp.einsum(
            "gjrc,cgd->rgjd", score_grad, key_part, preferred_element_type=jnp.float32
        )
        key_grad = attend_scale * jnp.einsum(
            "gjrc,rgjd->cgd", score_grad, query_part, preferred_element_type=jnp.float32
        )
        value_grad = jnp.einsum(
            "gjrc,rgjd->cgd",
            softmaxed.astype(jnp.bfloat16),
            incoming,
            preferred_element_type=jnp.float32,
        )
        current = lax.dynamic_slice_in_dim(accumulated, first_row, window)
        updated = lax.dynamic_update_slice_in_dim(
            accumulated, current + jnp.concatenate([key_grad, value_grad], axis=-1), first_row, 0
        )
        return (updated, query_grad.reshape(query_block, groups, repeat * HD))

    pair_grad, query_grads = lax.scan(
        attend_back,
        jnp.zeros((doc_most + span_rows, groups, 2 * HD), jnp.float32),
        (jnp.arange(block_count, dtype=jnp.int32), log_totals),
    )
    returned = from_behind(pair_grad[:doc_most].astype(jnp.bfloat16), "fsdp", -1).astype(
        jnp.float32
    )
    own_grad = pair_grad[doc_most:]
    own_grad = jnp.concatenate(
        [own_grad[: span_rows - doc_most], own_grad[span_rows - doc_most :] + returned], axis=0
    )
    packed_grad = jnp.concatenate(
        [
            query_grads.reshape(span_rows, groups, repeat * HD).astype(jnp.bfloat16),
            own_grad.astype(jnp.bfloat16),
        ],
        axis=-1,
    )
    by_tokens = lax.all_to_all(packed_grad, "sp", split_axis=0, concat_axis=1, tiled=True)
    query_rot_grad = (
        by_tokens[:, :, : repeat * HD].astype(jnp.float32).reshape(rows_dev, heads_query, HD)
    )
    key_rot_grad = by_tokens[:, :, repeat * HD : (repeat + 1) * HD].astype(jnp.float32)
    value_grad_low = by_tokens[:, :, (repeat + 1) * HD :].reshape(rows_dev, heads_kv * HD)
    query_lin_grad = (
        rotate(query_rot_grad, cosine, -sine_table)
        .astype(jnp.bfloat16)
        .reshape(rows_dev, heads_query * HD)
    )
    key_lin_grad = (
        rotate(key_rot_grad, cosine, -sine_table)
        .astype(jnp.bfloat16)
        .reshape(rows_dev, heads_kv * HD)
    )
    query_mat_grad = jnp.einsum(
        "td,tk->dk", normed_one, query_lin_grad, preferred_element_type=jnp.float32
    )
    key_mat_grad = jnp.einsum(
        "td,tk->dk", normed_one, key_lin_grad, preferred_element_type=jnp.float32
    )
    value_mat_grad = jnp.einsum(
        "td,tk->dk", normed_one, value_grad_low, preferred_element_type=jnp.float32
    )
    normed_one_grad = jnp.einsum(
        "tk,dk->td", query_lin_grad, query_mat, preferred_element_type=jnp.float32
    )
    normed_one_grad = normed_one_grad + jnp.einsum(
        "tk,dk->td", key_lin_grad, key_mat, preferred_element_type=jnp.float32
    )
    normed_one_grad = normed_one_grad + jnp.einsum(
        "tk,dk->td", value_grad_low, value_mat, preferred_element_type=jnp.float32
    )
    scaled_one = normed_one_grad * gain_one
    input_grad = (
        hidden_grad
        + inverse_one * scaled_one
        - stream * inverse_one**3 * jnp.mean(stream * scaled_one, axis=-1, keepdims=True)
    ).astype(jnp.bfloat16)
    norm_one_grad = jnp.sum(normed_one_grad * stream * inverse_one, axis=0)
    shard_norm_one, shard_query, shard_key, shard_value, shard_out, shard_norm_two, shard_router = (
        lax.psum_scatter(
            norm_one_grad.astype(jnp.bfloat16), "fsdp", scatter_dimension=0, tiled=True
        ).astype(jnp.float32),
        lax.psum_scatter(
            query_mat_grad.astype(jnp.bfloat16), "fsdp", scatter_dimension=0, tiled=True
        ).astype(jnp.float32),
        lax.psum_scatter(
            key_mat_grad.astype(jnp.bfloat16), "fsdp", scatter_dimension=0, tiled=True
        ).astype(jnp.float32),
        lax.psum_scatter(
            value_mat_grad.astype(jnp.bfloat16), "fsdp", scatter_dimension=0, tiled=True
        ).astype(jnp.float32),
        lax.psum_scatter(
            out_mat_grad.astype(jnp.bfloat16), "fsdp", scatter_dimension=0, tiled=True
        ).astype(jnp.float32),
        lax.psum_scatter(
            norm_two_grad.astype(jnp.bfloat16), "fsdp", scatter_dimension=0, tiled=True
        ).astype(jnp.float32),
        lax.psum_scatter(
            router_grad.astype(jnp.bfloat16), "fsdp", scatter_dimension=0, tiled=True
        ).astype(jnp.float32),
    )
    (
        summed_norm_one,
        summed_query,
        summed_key,
        summed_value,
        summed_out,
        summed_norm_two,
        summed_router,
        summed_gate,
        summed_up,
        summed_down,
    ) = (
        lax.psum(shard_norm_one.astype(jnp.bfloat16), "sp").astype(jnp.float32),
        lax.psum(shard_query.astype(jnp.bfloat16), "sp").astype(jnp.float32),
        lax.psum(shard_key.astype(jnp.bfloat16), "sp").astype(jnp.float32),
        lax.psum(shard_value.astype(jnp.bfloat16), "sp").astype(jnp.float32),
        lax.psum(shard_out.astype(jnp.bfloat16), "sp").astype(jnp.float32),
        lax.psum(shard_norm_two.astype(jnp.bfloat16), "sp").astype(jnp.float32),
        lax.psum(shard_router.astype(jnp.bfloat16), "sp").astype(jnp.float32),
        lax.psum(expert_gate_grad.astype(jnp.bfloat16), "sp").astype(jnp.float32),
        lax.psum(expert_up_grad.astype(jnp.bfloat16), "sp").astype(jnp.float32),
        lax.psum(expert_down_grad.astype(jnp.bfloat16), "sp").astype(jnp.float32),
    )
    return (
        output,
        input_grad,
        summed_norm_one,
        summed_query,
        summed_key,
        summed_value,
        summed_out,
        summed_norm_two,
        summed_router,
        summed_gate,
        summed_up,
        summed_down,
    )


def solution(mesh):
    placed = (
        P(("fsdp", "sp"), None),
        P(),
        P(("fsdp", "sp"), None),
        P(("fsdp", "sp"), None),
        P("fsdp"),
        P("fsdp", None),
        P("fsdp", None),
        P("fsdp", None),
        P("fsdp", None),
        P("fsdp"),
        P("fsdp", None),
        P("fsdp", None, None),
        P("fsdp", None, None),
        P("fsdp", None, None),
        P(("fsdp", "sp"), None),
    )
    return jax.shard_map(
        local,
        mesh=mesh,
        in_specs=placed,
        out_specs=(
            P(("fsdp", "sp"), None),
            P(("fsdp", "sp"), None),
            P("fsdp"),
            P("fsdp", None),
            P("fsdp", None),
            P("fsdp", None),
            P("fsdp", None),
            P("fsdp"),
            P("fsdp", None),
            P("fsdp", None, None),
            P("fsdp", None, None),
            P("fsdp", None, None),
        ),
        check_vma=False,
    )
```

profile of v0, /device:TPU:0, one launch (start us, length us, event | category | flops | bytes accessed | tf_op | source)
XLA Modules:
  0.0 1995.6 jit_solution(6760143309941025577)
XLA Ops:
  39.1 22.5 %all-gather.11.cloned.1.call-done = bf16[1024,512]{1,0:T(8,128)(2,1)} async-done(((bf16[128,512]{1,0:T(8,128)(2,1)}), bf16[1024,512]{1,0:T(8,128)(2,1)}) %all-gather.11.cloned.1.call-update) | async-done | bytes 1048592 | tf_op jit(solution)/shard_map/all_gather | solution.py:135
  63.6 27.7 %all-gather.7.cloned.1.call-done = bf16[1024,1024]{1,0:T(8,128)(2,1)} async-done(((bf16[128,1024]{1,0:T(8,128)(2,1)}), bf16[1024,1024]{1,0:T(8,128)(2,1)}) %all-gather.7.cloned.1.call-update) | async-done | bytes 2097168 | tf_op jit(solution)/shard_map/all_gather | solution.py:133
  108.7 42.0 %all-to-all-done = bf16[512,8,256]{0,2,1:T(8,128)(2,1)S(1)} async-done(((bf16[512,8,256]{0,2,1:T(8,128)(2,1)}), bf16[512,8,256]{0,2,1:T(8,128)(2,1)S(1)}, u32[]{:S(2)}, u32[]{:S(2)}) %all-to-all-start) | async-done | bytes 2097184 | tf_op jit(solution)/shard_map/all_to_all | solution.py:162
  155.1 15.2 all-gather.1
  171.2 23.3 %gather_fusion = s32[4096]{0:T(1024)S(1)} fusion(s32[4096]{0:T(1024)S(1)} %reshape.337, s32[4096]{0:T(1024)S(1)} %fusion.88), kind=kCustom, calls=%fused_computation | custom fusion | bytes 49152 | tf_op jit(solution)/shard_map/gather | solution.py:48
  208.7 83.9 %while.26 = (s32[]{:T(128)}, bf16[4,512,2,128]{3,1,0,2:T(8,128)(2,1)S(1)}, f32[4,2,2,512]{3,2,1,0:T(2,128)}, s32[4]{0:T(128)S(1)}, bf16[4096,2,128]{0,2,1:T(8,12...) while((s32[]{:T(128)}, ...), condition=%wide.region_6.7_spmd.clone, body=%wide.region_3.6_spmd.clone.sunk | while | flops 1409153024 | bytes 71670032 | solution.py:206
  305.8 23.0 %gather_fusion.1 = s32[4096]{0:T(1024)S(1)} fusion(s32[4096]{0:T(1024)S(1)} %copy-done, s32[4096]{0:T(1024)S(1)} %broadcast_clamp_fusion.1), kind=kCustom, calls=%fused_computation.1 | custom fusion | bytes 49152 | tf_op jit(solution)/shard_map/gather | solution.py:52
  347.0 17.7 convolution_convert_fusion.1
  385.0 90.2 %all-to-all-done.4 = bf16[32,144,1024]{2,1,0:T(8,128)(2,1)} async-done(((bf16[32,144,1024]{2,1,0:T(8,128)(2,1)}), bf16[32,144,1024]{2,1,0:T(8,128)(2,1)}, u32[]{:S(2)}, u32[]{:S(2)}) %all-to-all-start.4) | async-done | bytes 9437216 | tf_op jit(solution)/shard_map/all_to_all | solution.py:58
  489.7 96.3 %all-to-all-done.2 = bf16[32,144,1024]{2,1,0:T(8,128)(2,1)} async-done(((bf16[32,144,1024]{2,1,0:T(8,128)(2,1)}), bf16[32,144,1024]{2,1,0:T(8,128)(2,1)}, u32[]{:S(2)}, u32[]{:S(2)}) %all-to-all-start.2) | async-done | bytes 9437216 | tf_op jit(solution)/shard_map/all_to_all | solution.py:58
  614.4 18.2 multiply_convert_fusion
  640.9 25.5 %copy.203 = bf16[4,1152,1024]{2,0,1:T(4,128)(2,1)} copy(bf16[4,1152,1024]{2,1,0:T(8,128)(2,1)S(1)} %convolution_convert_fusion) | data formatting | bytes 18874368 | tf_op jit(solution)/shard_map/convert_element_type | solution.py:71
  710.5 66.2 %all-to-all-done.3 = bf16[4,1152,1024]{2,0,1:T(4,128)(2,1)} async-done(((bf16[4,1152,1024]{2,0,1:T(4,128)(2,1)}), bf16[4,1152,1024]{2,0,1:T(4,128)(2,1)}, u32[]{:S(2)}, u32[]{:S(2)}) %all-to-all-start.3) | async-done | bytes 9437216 | tf_op jit(solution)/shard_map/all_to_all | solution.py:62
  793.7 25.7 %gather_fusion.2 = bf16[4096,1024]{1,0:T(8,128)(2,1)} fusion(bf16[4608,1024]{1,0:T(8,128)(2,1)} %bitcast.326, s32[4096]{0:T(1024)S(1)} %broadcast_clamp_fusion), kind=kCustom, calls=%fused_computation.2 | custom fusion | bytes 16793600 | tf_op jit(solution)/shard_map/jit(_take)/gather | solution.py:256
  828.3 59.0 %all-to-all-done.5 = bf16[4,1152,1024]{2,0,1:T(4,128)(2,1)} async-done(((bf16[4,1152,1024]{2,0,1:T(4,128)(2,1)}), bf16[4,1152,1024]{2,0,1:T(4,128)(2,1)}, u32[]{:S(2)}, u32[]{:S(2)}) %all-to-all-start.5) | async-done | bytes 9437216 | tf_op jit(solution)/shard_map/all_to_all | solution.py:62
  907.1 15.2 fusion.109
  932.9 22.8 %all-to-all-done.6 = bf16[512,8,128]{2,0,1:T(8,128)(2,1)S(1)} async-done(((bf16[512,8,128]{2,0,1:T(8,128)(2,1)}), bf16[512,8,128]{2,0,1:T(8,128)(2,1)S(1)}, u32[]{:S(2)}, u32[]{:S(2)}) %all-to-all-start.6) | async-done | bytes 1048608 | tf_op jit(solution)/shard_map/all_to_all | solution.py:298
  960.5 291.2 %while.27 = (s32[]{:T(128)}, f32[4096,2,128]{2,0,1:T(8,128)}, bf16[4,512,2,128]{3,1,0,2:T(8,128)(2,1)}, s32[4]{0:T(128)S(1)}, bf16[2048,2,128]{0,2,1:T(8,128)(2,...) while((s32[]{:T(128)}, f32[4096,2,128]{2,0,1:T(8,128)}, ...), condition=%wide.region_20.21_spmd.clone, body=%wide.region_18.20_spmd.clone.sunk | while | flops 3439917056 | bytes 209942864 | solution.py:337
  1281.4 40.2 %all-to-all-done.7 = bf16[2048,2,256]{2,1,0:T(2,128)(2,1)} async-done(((bf16[2048,2,256]{2,1,0:T(2,128)(2,1)}), bf16[2048,2,256]{2,1,0:T(2,128)(2,1)}, u32[]{:S(2)}, u32[]{:S(2)}) %all-to-all-start.7) | async-done | bytes 2097184 | tf_op jit(solution)/shard_map/all_to_all | solution.py:356
  1382.8 40.1 %reduce-scatter.10.cloned.1.call-done = bf16[128,512]{1,0:T(8,128)(2,1)} async-done(((bf16[1024,512]{1,0:T(8,128)(2,1)}), bf16[128,512]{1,0:T(8,128)(2,1)}) %reduce-scatter.10.cloned.1.call-update) | async-done | bytes 131088 | tf_op jit(solution)/shard_map/reduce_scatter | solution.py:404
  1422.9 44.9 %reduce-scatter.8.cloned.1.call-done = bf16[128,1024]{1,0:T(8,128)(2,1)} async-done(((bf16[1024,1024]{1,0:T(8,128)(2,1)}), bf16[128,1024]{1,0:T(8,128)(2,1)}) %reduce-scatter.8.cloned.1.call-update) | async-done | bytes 262160 | tf_op jit(solution)/shard_map/reduce_scatter | solution.py:401
  1469.8 17.5 add_convert_fusion.1
  1487.4 17.7 reduce-scatter.16.cloned.1.call-done
  1545.1 420.4 %all-reduce.8.cloned.1.call-done = (bf16[128,1024]{1,0:T(8,128)(2,1)}, bf16[128,512]{1,0:T(8,128)(2,1)}, bf16[128,512]{1,0:T(8,128)(2,1)}, bf16[128,1024]{1,0:T(...) async-done(((bf16[128,1024]{1,0:T(8,128)(2,1)}, bf16[128,512]{1,0:T(8,128)(2,1)}, ...) | async-done | bytes 13369360 | tf_op jit(solution)/shard_map/psum | solution.py:433
  (534 shorter events, 800.9 us)
Async XLA Ops:
  7.2 29.0 %all-gather.9.cloned.1.call-start = ((), (), s32[]{:S(2)}) async-start(), calls=%async_computation.14 | async-start | bytes 1179648 | tf_op jit(solution)/shard_map/all_gather | solution.py:134
  7.9 53.6 %all-gather.11.cloned.1.call-start = ((), (), s32[]{:S(2)}) async-start(), calls=%async_computation.15 | async-start | bytes 1179648 | tf_op jit(solution)/shard_map/all_gather | solution.py:135
  8.7 82.7 %all-gather.7.cloned.1.call-start = ((), (), s32[]{:S(2)}) async-start(), calls=%async_computation.13 | async-start | bytes 2359296 | tf_op jit(solution)/shard_map/all_gather | solution.py:133
  19.7 71.6 %copy-start.55 = (f32[8,1,128]{2,1,0:T(1,128)}, f32[8,1,128]{2,1,0:T(1,128)S(1)}, u32[]{:S(2)}) copy-start(f32[8,1,128]{2,1,0:T(1,128)S(1)} %convert_element_type.251) | copy-start | bytes 12292
  97.5 53.2 %all-to-all-start = ((bf16[512,8,256]{0,2,1:T(8,128)(2,1)}), bf16[512,8,256]{0,2,1:T(8,128)(2,1)S(1)}, u32[]{:S(2)}, u32[]{:S(2)}) async-start(bf16[512,8,256]{0,2,1:T(8,128)(2,1)} %pad_maximum_fusion), calls=%async_computation | async-start | bytes 4194304 | tf_op jit(solution)/shard_map/all_to_all | solution.py:162
  102.1 238.8 %all-gather.13.cloned.1.call-start = ((), (), s32[]{:S(2)}) async-start(), calls=%async_computation.16 | async-start | bytes 2359296 | tf_op jit(solution)/shard_map/all_gather | solution.py:136
  152.1 53.9 %collective-permute-start = (bf16[2048,2,128]{0,2,1:T(8,128)(2,1)S(1)}, bf16[2048,2,128]{0,2,1:T(8,128)(2,1)}, u32[]{:S(2)}, u32[]{:S(2)}) collective-permute-start(bf16[2048,2,128]{0,2,1:T(8,128)(2,1)S(1)} %get-tuple-element.250), channel_id=1, source_target_pairs={{0,1},{1,2},{2,3},{3,4},{4,5},{5,6},{6,7},{8,9},{9,10},{10,11},{11... | collective-permute-start | bytes 3145736 | tf_op jit(solution)/shard_map/ppermute | solution.py:20
  302.2 36.7 %all-to-all-start.1 = ((bf16[2048,2,128]{2,1,0:T(2,128)(2,1)}), bf16[2048,2,128]{2,1,0:T(2,128)(2,1)S(1)}, u32[]{:S(2)}, u32[]{:S(2)}) async-start(bf16[2048,2,128]{2,1,0:T(2,128)(2,1)} %copy.194), calls=%async_computation.1 | async-start | bytes 2097152 | tf_op jit(solution)/shard_map/all_to_all | solution.py:207
  364.8 110.4 %all-to-all-start.4 = ((bf16[32,144,1024]{2,1,0:T(8,128)(2,1)}), bf16[32,144,1024]{2,1,0:T(8,128)(2,1)}, u32[]{:S(2)}, u32[]{:S(2)}) async-start(bf16[32,144,1024]{2,1,0:T(8,128)(2,1)} %bitcast.345), calls=%async_computation.4 | async-start | bytes 18874368 | tf_op jit(solution)/shard_map/all_to_all | solution.py:58
  475.2 110.8 %all-to-all-start.2 = ((bf16[32,144,1024]{2,1,0:T(8,128)(2,1)}), bf16[32,144,1024]{2,1,0:T(8,128)(2,1)}, u32[]{:S(2)}, u32[]{:S(2)}) async-start(bf16[32,144,1024]{2,1,0:T(8,128)(2,1)} %bitcast.344), calls=%async_computation.2 | async-start | bytes 18874368 | tf_op jit(solution)/shard_map/all_to_all | solution.py:58
  666.4 110.4 %all-to-all-start.3 = ((bf16[4,1152,1024]{2,0,1:T(4,128)(2,1)}), bf16[4,1152,1024]{2,0,1:T(4,128)(2,1)}, u32[]{:S(2)}, u32[]{:S(2)}) async-start(bf16[4,1152,1024]{2,0,1:T(4,128)(2,1)} %copy.203), calls=%async_computation.3 | async-start | bytes 18874368 | tf_op jit(solution)/shard_map/all_to_all | solution.py:62
  710.5 71.5 %copy-start.64 = (pred[512,8]{0,1:T(8,128)(4,1)S(1)}, pred[512,8]{0,1:T(8,128)(4,1)}, u32[]{:S(2)}) copy-start(pred[512,8]{0,1:T(8,128)(4,1)} %get-tuple-element.234) | copy-start | bytes 12292
  710.5 71.7 %copy-start.49 = (s32[512,8]{0,1:T(8,128)S(1)}, s32[512,8]{0,1:T(8,128)}, u32[]{:S(2)}) copy-start(s32[512,8]{0,1:T(8,128)} %copy-done.48) | copy-start | bytes 49156
  776.8 110.6 %all-to-all-start.5 = ((bf16[4,1152,1024]{2,0,1:T(4,128)(2,1)}), bf16[4,1152,1024]{2,0,1:T(4,128)(2,1)}, u32[]{:S(2)}, u32[]{:S(2)}) async-start(bf16[4,1152,1024]{2,0,1:T(4,128)(2,1)} %copy.208), calls=%async_computation.5 | async-start | bytes 18874368 | tf_op jit(solution)/shard_map/all_to_all | solution.py:62
  828.3 94.1 %copy-start.39 = (bf16[512,32]{0,1:T(8,128)(2,1)}, bf16[512,32]{0,1:T(8,128)(2,1)S(1)}, u32[]{:S(2)}) copy-start(bf16[512,32]{0,1:T(8,128)(2,1)S(1)} %select_reduce_fusion) | copy-start | bytes 98308
  927.9 27.8 %all-to-all-start.6 = ((bf16[512,8,128]{2,0,1:T(8,128)(2,1)}), bf16[512,8,128]{2,0,1:T(8,128)(2,1)S(1)}, u32[]{:S(2)}, u32[]{:S(2)}) async-start(bf16[512,8,128]{2,0,1:T(8,128)(2,1)} %bitcast.258), calls=%async_computation.6 | async-start | bytes 2097152 | tf_op jit(solution)/shard_map/all_to_all | solution.py:298
  1253.5 4.6 collective-permute-start.1
  1274.2 47.4 %all-to-all-start.7 = ((bf16[2048,2,256]{2,1,0:T(2,128)(2,1)}), bf16[2048,2,256]{2,1,0:T(2,128)(2,1)}, u32[]{:S(2)}, u32[]{:S(2)}) async-start(bf16[2048,2,256]{2,1,0:T(2,128)(2,1)} %copy.216), calls=%async_computation.7 | async-start | bytes 4194304 | tf_op jit(solution)/shard_map/all_to_all | solution.py:356
  1278.6 96.9 %reduce-scatter.14.cloned.1.call-start = ((), (), s32[]{:S(2)}) async-start(), calls=%async_computation.20 | async-start | bytes 2359296 | tf_op jit(solution)/shard_map/reduce_scatter | solution.py:410
  1281.3 101.4 %reduce-scatter.12.cloned.1.call-start = ((), (), s32[]{:S(2)}) async-start(), calls=%async_computation.19 | async-start | bytes 1179648 | tf_op jit(solution)/shard_map/reduce_scatter | solution.py:407
  1330.2 92.7 %reduce-scatter.10.cloned.1.call-start = ((), (), s32[]{:S(2)}) async-start(), calls=%async_computation.18 | async-start | bytes 1179648 | tf_op jit(solution)/shard_map/reduce_scatter | solution.py:404
  1334.7 133.1 %reduce-scatter.8.cloned.1.call-start = ((), (), s32[]{:S(2)}) async-start(), calls=%async_computation.17 | async-start | bytes 2359296 | tf_op jit(solution)/shard_map/reduce_scatter | solution.py:401
  1339.9 165.2 %reduce-scatter.16.cloned.1.call-start = ((), (), s32[]{:S(2)}) async-start(), calls=%async_computation.21 | async-start | bytes 294912
  1364.2 601.3 %all-reduce.8.cloned.1.call-start = ((), (), s32[]{:S(2)}) async-start(), calls=%async_computation.22 | async-start | bytes 26738688 | tf_op jit(solution)/shard_map/psum | solution.py:433
  (111 other events, 1464.7 us)
Sparse Core Ops, SparseCore 0:
  9.9 26.1 all-gather.8
  38.0 23.4 all-gather.10
  63.4 27.8 all-gather.6
  104.5 28.3 all-gather.12
  1282.5 54.8 reduce-scatter.13
  1340.7 42.0 reduce-scatter.11
  1386.8 36.0 reduce-scatter.9
  1426.5 41.1 reduce-scatter.7
  1471.4 33.6 reduce-scatter.15
  1509.3 456.1 all-reduce.7
where the time goes:
time: 2010 us; the launch traced here: 2000 us
  waiting for transfers between devices  1020 us (51%)
  matrix products  419 us (21%)
  local copies, waits for them, and re-layouts  274 us (14%)
  other arithmetic  161 us (8%)
  blocking collectives  60.1 us (3%)
  starting transfers between devices  42.4 us (2%)
    psum x1, waiting for transfers between devices, local(): lax.psum(shard_query.astype(jnp.bfloat16), 'sp').astype(jnp.float32)  420 us
    all_to_all x2, waiting for transfers between devices, to_owner(): lax.all_to_all(values, 'fsdp', split_axis=0, concat_axis=1, tiled=True)  186 us
    all_to_all x2, waiting for transfers between devices, from_owner(): lax.all_to_all(values, 'fsdp', split_axis=1, concat_axis=0, tiled=True)  125 us
    dot_general x8, matrix products, block_scores(): jnp.einsum('rgjd,cgd->gjrc', query_part, key_part, preferred_element_type...  59.1 us
    convert_element_type x4, other arithmetic, attend_back(): score_grad = (softmaxed * (softmax_grad - centred)).astype(jnp.bfloat16)  58.4 us
    dot_general x4, matrix products, attend_back(): jnp.einsum('rgjd,cgd->gjrc', incoming, value_part, preferred_element_type...  57.8 us
    reduce_scatter x1, waiting for transfers between devices, local(): lax.psum_scatter(query_mat_grad.astype(jnp.bfloat16), 'fsdp', scatter_dim...  44.9 us
    all_to_all x1, waiting for transfers between devices, local(): lax.all_to_all(packed, 'sp', split_axis=1, concat_axis=0, tiled=True)  42 us
  transfers between devices with their start and end apart: 20, of which 16 were waited for; matrix products, arithmetic and copies ran while one was open for 18% of the time, Pallas kernels for 0%

commit v1 on v0

--- a/solution.py
+++ b/solution.py
@@ -1,7 +1,11 @@
+import functools
+
 import jax
 import jax.numpy as jnp
 from jax import lax
 from jax.sharding import PartitionSpec as P
+from jax.experimental import pallas as pl
+from jax.experimental.pallas import tpu as pltpu
 
 HD = 64
 DOC_CAP = 2048
@@ -456,6 +460,989 @@
     )
 
 
+BF = jnp.bfloat16
+F32 = jnp.float32
+LOG2E = 1.4426950408889634
+QB = 512
+KB = 512
+HALO = 2048
+VMEM_MOST = 60 * 1024 * 1024
+
+
+def in_vmem(count):
+    return [pl.BlockSpec(memory_space=pltpu.VMEM)] * count
+
+
+def in_hbm(count):
+    return [pl.BlockSpec(memory_space=pl.ANY)] * count
+
+
+def in_smem():
+    return pl.BlockSpec(memory_space=pltpu.SMEM)
+
+
+def shaped(shape, kind):
+    return jax.ShapeDtypeStruct(shape, kind)
+
+
+def params():
+    return pltpu.CompilerParams(vmem_limit_bytes=VMEM_MOST)
+
+
+def cost(flops, moved, transcendentals=0):
+    return pl.CostEstimate(
+        flops=int(flops), bytes_accessed=int(moved), transcendentals=int(transcendentals)
+    )
+
+
+def nn(left, right):
+    return lax.dot_general(left, right, (((1,), (0,)), ((), ())), preferred_element_type=F32)
+
+
+def nt(left, right):
+    return lax.dot_general(left, right, (((1,), (1,)), ((), ())), preferred_element_type=F32)
+
+
+def tn(left, right):
+    return lax.dot_general(left, right, (((0,), (0,)), ((), ())), preferred_element_type=F32)
+
+
+def flip(value, bit):
+    return lax.ppermute(value, "fsdp", [(place, place ^ bit) for place in range(8)])
+
+
+def half_rows(rows):
+    return (rows // 2 + 15) // 16 * 16
+
+
+def plan_of(rows):
+    half = half_rows(rows)
+    return (
+        (0, 0, rows),
+        (1, 0, rows),
+        (2, 0, rows),
+        (3, 0, rows),
+        (4, 0, rows),
+        (5, 0, rows),
+        (6, 0, half),
+        (6, half, rows - half),
+        (7, 0, half),
+        (7, half, rows - half),
+    )
+
+
+def spread(own):
+    half = half_rows(own.shape[0])
+    along_x = flip(own, 2)
+    along_y = flip(own, 4)
+    low = flip(along_y[:half], 2)
+    high = flip(along_x[half:], 4)
+    return (
+        own,
+        flip(own, 1),
+        along_x,
+        flip(along_x, 1),
+        along_y,
+        flip(along_y, 1),
+        low,
+        high,
+        flip(low, 1),
+        flip(high, 1),
+    )
+
+
+def add_low(left, right):
+    return (left.astype(F32) + right.astype(F32)).astype(BF)
+
+
+def collect(odd, even):
+    half = half_rows(even.shape[1])
+    received = flip(odd, 1)
+    own = add_low(even[0], received[0])
+    diagonal_low = flip(add_low(even[3, :half], received[3, :half]), 2)
+    diagonal_high = flip(add_low(even[3, half:], received[3, half:]), 4)
+    for_y = even[2].astype(F32) + received[2].astype(F32)
+    for_x = even[1].astype(F32) + received[1].astype(F32)
+    for_y = jnp.concatenate([for_y[:half] + diagonal_low.astype(F32), for_y[half:]]).astype(BF)
+    for_x = jnp.concatenate([for_x[:half], for_x[half:] + diagonal_high.astype(F32)]).astype(BF)
+    return (own, flip(for_x, 2), flip(for_y, 4))
+
+
+def start_fetch(me, plan, sources, target, block_rows, sems):
+    copies = []
+    for number, (partner, first, rows) in enumerate(plan):
+        start = pl.multiple_of((me ^ partner) * block_rows + first, 64)
+        copies.append(
+            pltpu.make_async_copy(sources[number], target.at[pl.ds(start, rows)], sems.at[number])
+        )
+        copies[-1].start()
+    return copies
+
+
+def start_fetch_heads(me, plan, sources, target, sems):
+    copies = []
+    for number, (partner, first, rows) in enumerate(plan):
+        for offset in range(0, rows, HD):
+            head = (me ^ partner) * 2 + (first + offset) // HD
+            head = (head & ~3) | ((head & 1) << 1) | ((head >> 1) & 1)
+            copies.append(
+                pltpu.make_async_copy(
+                    sources[number].at[pl.ds(offset, HD)],
+                    target.at[pl.ds(pl.multiple_of(head * HD, HD), HD)],
+                    sems.at[len(copies)],
+                )
+            )
+            copies[-1].start()
+    return copies
+
+
+def turn(values, cosine, sine):
+    lane = lax.broadcasted_iota(jnp.int32, values.shape, 1)
+    other = jnp.where(
+        lane % HD < HD // 2, pltpu.roll(values, 128 - HD // 2, 1), pltpu.roll(values, HD // 2, 1)
+    )
+    return values * cosine + other * sine
+
+
+def project_kernel(plan, me_ref, tokens_ref, cos_ref, sin_ref, *refs):
+    count = len(plan)
+    query_ref, pair_ref, extra_ref, mats, sems = refs[count:]
+    copies = start_fetch(me_ref[0], plan, refs[:count], mats, 128, sems)
+    stream = tokens_ref[...].astype(F32)
+    scaled = stream * lax.rsqrt(jnp.mean(stream * stream, axis=-1, keepdims=True) + norm_eps)
+    for copy in copies:
+        copy.wait()
+    extra = mats[:, 2048:2176].astype(F32).T
+    extra_ref[...] = extra[:48].astype(BF)
+    normed = (scaled * extra[32:33]).astype(BF)
+    cosine, sine = cos_ref[...], sin_ref[...]
+    for part in range(4):
+        query = nn(normed, mats[:, part * 256 : part * 256 + 256])
+        for half in range(2):
+            columns = slice(half * 128, half * 128 + 128)
+            query_ref[part, :, columns] = turn(query[:, columns], cosine, sine).astype(BF)
+        key = nn(normed, mats[:, 1024 + part * 128 : 1152 + part * 128])
+        pair_ref[part, :, :128] = turn(key, cosine, sine).astype(BF)
+        pair_ref[part, :, 128:] = nn(
+            normed, mats[:, 1536 + part * 128 : 1664 + part * 128]
+        ).astype(BF)
+
+
+def project(me, tokens, cosine, sine, pieces):
+    plan = plan_of(128)
+    return pl.pallas_call(
+        functools.partial(project_kernel, plan),
+        out_shape=(
+            shaped((4, 512, 256), BF),
+            shaped((4, 512, 256), BF),
+            shaped((48, 1024), BF),
+        ),
+        in_specs=[in_smem()] + in_vmem(3) + in_hbm(len(plan)),
+        out_specs=tuple(in_vmem(3)),
+        scratch_shapes=[pltpu.VMEM((1024, 2176), BF), pltpu.SemaphoreType.DMA((len(plan),))],
+        compiler_params=params(),
+        cost_estimate=cost(2 * 512 * 1024 * 2048, 9e6),
+        name="project",
+    )(me, tokens, cosine, sine, *pieces)
+
+
+def lane_half(values, group):
+    lane = lax.broadcasted_iota(jnp.int32, values.shape, 1)
+    return jnp.where((lane < HD) == (group == 0), values, jnp.zeros((), values.dtype))
+
+
+def allowed_pairs(block, step, start):
+    key_at = block * KB + lax.broadcasted_iota(jnp.int32, (KB, QB), 0)
+    query_at = HALO + step * QB + lax.broadcasted_iota(jnp.int32, (KB, QB), 1)
+    return (key_at >= start) & (key_at <= query_at)
+
+
+def attend_kernel(
+    low_ref, query_ref, own_ref, halo_ref, start_ref, out_ref, log_ref,
+    keys, values_t, most, total, blend,
+):
+    step = pl.program_id(0)
+
+    @pl.when(step == 0)
+    def _():
+        for first in range(0, HALO, 512):
+            rows = slice(first, first + 512)
+            keys[first : first + 512, :] = halo_ref[rows, :128]
+            keys[HALO + first : HALO + first + 512, :] = own_ref[rows, :128]
+            values_t[:, first : first + 512] = halo_ref[rows, 128:].astype(F32).T.astype(BF)
+            values_t[:, HALO + first : HALO + first + 512] = (
+                own_ref[rows, 128:].astype(F32).T.astype(BF)
+            )
+
+    start = start_ref[0]
+    picks = [
+        lane_half(query_ref[:, half * 128 : half * 128 + 128], group)
+        for half in range(2)
+        for group in range(2)
+    ]
+    most[...] = jnp.full(most.shape, masked_score, F32)
+    total[...] = jnp.zeros(total.shape, F32)
+    blend[...] = jnp.zeros(blend.shape, F32)
+
+    def visit(block, carry):
+        first = pl.multiple_of(block * KB, KB)
+        allowed = allowed_pairs(block, step, start)
+        key = keys[pl.ds(first, KB), :]
+        for number in range(4):
+            scores = nt(key, picks[number]) * (attend_scale * LOG2E)
+            scores = jnp.where(allowed, scores, masked_score)
+            before = most[number : number + 1, :]
+            top = jnp.maximum(before, jnp.max(scores, axis=0, keepdims=True))
+            weight = jnp.exp2(scores - top)
+            fade = jnp.exp2(before - top)
+            most[number : number + 1, :] = top
+            total[number : number + 1, :] = total[number : number + 1, :] * fade + jnp.sum(
+                weight, axis=0, keepdims=True
+            )
+            group = number % 2
+            value = values_t[group * HD : group * HD + HD, pl.ds(first, KB)]
+            rows = slice(number * HD, number * HD + HD)
+            blend[rows, :] = blend[rows, :] * fade + nn(value, weight.astype(BF))
+        return carry
+
+    lax.fori_loop(low_ref[step], step + HALO // KB + 1, visit, 0)
+    for number in range(4):
+        rows = slice(number * HD, number * HD + HD)
+        blend[rows, :] = blend[rows, :] / total[number : number + 1, :]
+    for half in range(2):
+        out_ref[:, half * 128 : half * 128 + 128] = (
+            blend[half * 128 : half * 128 + 128, :].T.astype(BF)
+        )
+    log_ref[0:4, :] = most[0:4, :] + jnp.log2(total[0:4, :])
+    log_ref[4:8, :] = jnp.zeros((4, QB), F32)
+
+
+def attend(low_block, query, own, halo, start):
+    steps = query.shape[0] // QB
+    spec = lambda shape, index: pl.BlockSpec(shape, index)
+    return pl.pallas_call(
+        attend_kernel,
+        out_shape=(shaped((2048, 256), BF), shaped((8, 2048), F32)),
+        grid_spec=pltpu.PrefetchScalarGridSpec(
+            num_scalar_prefetch=1,
+            grid=(steps,),
+            in_specs=[
+                spec((QB, 256), lambda i, low: (i, 0)),
+                spec((2048, 256), lambda i, low: (0, 0)),
+                spec((2048, 256), lambda i, low: (0, 0)),
+                spec((1, 1, QB), lambda i, low: (i, 0, 0)),
+            ],
+            out_specs=(
+                spec((QB, 256), lambda i, low: (i, 0)),
+                spec((8, QB), lambda i, low: (0, i)),
+            ),
+            scratch_shapes=[
+                pltpu.VMEM((2 * HALO, 128), BF),
+                pltpu.VMEM((128, 2 * HALO), BF),
+                pltpu.VMEM((8, QB), F32),
+                pltpu.VMEM((8, QB), F32),
+                pltpu.VMEM((256, QB), F32),
+            ],
+        ),
+        compiler_params=params(),
+        cost_estimate=cost(25e9, 6e6),
+        name="attend",
+    )(low_block, query, own, halo, start)
+
+
+def attend_back_kernel(
+    low_ref, query_ref, own_ref, halo_ref, start_ref, out_ref, grad_ref, log_ref,
+    query_grad_ref, own_grad_ref, halo_grad_ref,
+    keys, values, keys_t, key_grad, value_grad, blend,
+):
+    step = pl.program_id(0)
+
+    @pl.when(step == 0)
+    def _():
+        for first in range(0, HALO, 512):
+            rows = slice(first, first + 512)
+            late = slice(HALO + first, HALO + first + 512)
+            keys[rows, :] = halo_ref[rows, :128]
+            keys[late, :] = own_ref[rows, :128]
+            values[rows, :] = halo_ref[rows, 128:]
+            values[late, :] = own_ref[rows, 128:]
+            keys_t[:, rows] = halo_ref[rows, :128].astype(F32).T.astype(BF)
+            keys_t[:, late] = own_ref[rows, :128].astype(F32).T.astype(BF)
+        key_grad[...] = jnp.zeros(key_grad.shape, F32)
+        value_grad[...] = jnp.zeros(value_grad.shape, F32)
+
+    start = start_ref[0]
+    picks, incoming, centres = [], [], []
+    for half in range(2):
+        columns = slice(half * 128, half * 128 + 128)
+        product = (out_ref[:, columns].astype(F32) * grad_ref[:, columns].astype(F32)).T
+        for group in range(2):
+            picks.append(lane_half(query_ref[:, columns], group))
+            incoming.append(lane_half(grad_ref[:, columns], group))
+            centres.append(
+                jnp.sum(product[group * HD : group * HD + HD, :], axis=0, keepdims=True)
+            )
+    blend[...] = jnp.zeros(blend.shape, F32)
+
+    def visit(block, carry):
+        first = pl.multiple_of(block * KB, KB)
+        allowed = allowed_pairs(block, step, start)
+        here = pl.ds(first, KB)
+        key, value = keys[here, :], values[here, :]
+        for number in range(4):
+            scores = nt(key, picks[number]) * (attend_scale * LOG2E)
+            weight = jnp.where(
+                allowed, jnp.exp2(scores - log_ref[number : number + 1, :]), 0.0
+            )
+            weight_grad = nt(value, incoming[number])
+            score_grad = (weight * (weight_grad - centres[number])).astype(BF)
+            value_grad[here, :] += nn(weight.astype(BF), incoming[number])
+            key_grad[here, :] += nn(score_grad, picks[number])
+            group = number % 2
+            rows = slice(number * HD, number * HD + HD)
+            blend[rows, :] += nn(keys_t[group * HD : group * HD + HD, here], score_grad)
+        return carry
+
+    lax.fori_loop(low_ref[step], step + HALO // KB + 1, visit, 0)
+    for half in range(2):
+        query_grad_ref[:, half * 128 : half * 128 + 128] = (
+            (blend[half * 128 : half * 128 + 128, :] * attend_scale).T.astype(BF)
+        )
+
+    @pl.when(step == pl.num_programs(0) - 1)
+    def _():
+        for first in range(0, HALO, 512):
+            rows = slice(first, first + 512)
+            late = slice(HALO + first, HALO + first + 512)
+            halo_grad_ref[rows, :128] = (key_grad[rows, :] * attend_scale).astype(BF)
+            halo_grad_ref[rows, 128:] = value_grad[rows, :].astype(BF)
+            own_grad_ref[rows, :128] = key_grad[late, :] * attend_scale
+            own_grad_ref[rows, 128:] = value_grad[late, :]
+
+
+def attend_back(low_block, query, own, halo, start, out, grad, logs):
+    steps = query.shape[0] // QB
+    spec = lambda shape, index: pl.BlockSpec(shape, index)
+    tile = spec((QB, 256), lambda i, low: (i, 0))
+    whole = spec((2048, 256), lambda i, low: (0, 0))
+    return pl.pallas_call(
+        attend_back_kernel,
+        out_shape=(
+            shaped((2048, 256), BF),
+            shaped((2048, 256), F32),
+            shaped((2048, 256), BF),
+        ),
+        grid_spec=pltpu.PrefetchScalarGridSpec(
+            num_scalar_prefetch=1,
+            grid=(steps,),
+            in_specs=[
+                tile,
+                whole,
+                whole,
+                spec((1, 1, QB), lambda i, low: (i, 0, 0)),
+                tile,
+                tile,
+                spec((8, QB), lambda i, low: (0, i)),
+            ],
+            out_specs=(tile, whole, whole),
+            scratch_shapes=[
+                pltpu.VMEM((2 * HALO, 128), BF),
+                pltpu.VMEM((2 * HALO, 128), BF),
+                pltpu.VMEM((128, 2 * HALO), BF),
+                pltpu.VMEM((2 * HALO, 128), F32),
+                pltpu.VMEM((2 * HALO, 128), F32),
+                pltpu.VMEM((256, QB), F32),
+            ],
+        ),
+        compiler_params=params(),
+        cost_estimate=cost(60e9, 10e6),
+        name="attend_back",
+    )(low_block, query, own, halo, start, out, grad, logs)
+
+
+def after_kernel(plan, me_ref, tokens_ref, attended_ref, extra_ref, routed_ref, *refs):
+    count = len(plan)
+    hidden_ref, payload_ref, gates_ref, mats, sems = refs[count:]
+    copies = start_fetch_heads(me_ref[0], plan, refs[:count], mats, sems)
+    stream = tokens_ref[...].astype(F32)
+    for copy in copies:
+        copy.wait()
+    branch = nn(attended_ref[0], mats[0:256, :])
+    for part in range(1, 4):
+        branch += nn(attended_ref[part], mats[part * 256 : part * 256 + 256, :])
+    hidden = stream + branch_scale * branch
+    hidden_ref[...] = hidden
+    inverse = lax.rsqrt(jnp.mean(hidden * hidden, axis=-1, keepdims=True) + norm_eps)
+    normed = (hidden * inverse * extra_ref[33:34, :].astype(F32)).astype(BF)
+    payload_ref[0:512, :] = normed
+    logits = nt(extra_ref[0:32, :], normed)
+    routed = routed_ref[...] > 0.5
+    top = jnp.max(jnp.where(routed, logits, masked_score), axis=0, keepdims=True)
+    raised = jnp.where(routed, jnp.exp(logits - top), 0.0)
+    gates = raised / jnp.sum(raised, axis=0, keepdims=True)
+    gates_ref[...] = gates
+    low = gates.astype(BF)
+    payload_ref[512:528, 0:512] = low[0:16, :]
+    payload_ref[512:528, 512:1024] = low[16:32, :]
+
+
+def after_attention(me, tokens, attended, extra, routed, pieces):
+    plan = plan_of(128)
+    return pl.pallas_call(
+        functools.partial(after_kernel, plan),
+        out_shape=(shaped((512, 1024), F32), shaped((528, 1024), BF), shaped((32, 512), F32)),
+        in_specs=[in_smem()] + in_vmem(4) + in_hbm(len(plan)),
+        out_specs=tuple(in_vmem(3)),
+        scratch_shapes=[pltpu.VMEM((1024, 1024), BF), pltpu.SemaphoreType.DMA((16,))],
+        compiler_params=params(),
+        cost_estimate=cost(2 * 512 * 1024 * 1024, 8e6),
+        name="after_attention",
+    )(me, tokens, attended, extra, routed, *pieces)
+
+
+def own_rows(me, packed):
+    first = me * 4
+    side = jnp.where(first < 16, packed[:, :512], packed[:, 512:])
+    row = lax.broadcasted_iota(jnp.int32, side.shape, 0)
+    return [
+        jnp.sum(jnp.where(row == first % 16 + expert, side, 0.0), axis=0, keepdims=True)
+        for expert in range(4)
+    ]
+
+
+def stand_up(rows):
+    row = lax.broadcasted_iota(jnp.int32, (128, 512), 0)
+    lying = jnp.zeros((128, 512), F32)
+    for number, values in enumerate(rows):
+        lying = jnp.where(row == number, values, lying)
+    return lying.T
+
+
+def slot_hot(slot_row):
+    at = lax.broadcasted_iota(jnp.int32, (144, 512), 0).astype(F32)
+    return at == slot_row
+
+
+def pieces_rows(parts):
+    if len(parts) == 1:
+        return parts[0][0:512, :], parts[0][512:528, :].astype(F32)
+    rows = parts[0].shape[0]
+    return (
+        jnp.concatenate([parts[0][...], parts[1][0 : 512 - rows, :]], axis=0),
+        parts[1][512 - rows : 528 - rows, :].astype(F32),
+    )
+
+
+def pick_grad_kernel(split, me_ref, *refs):
+    count = 2 * split
+    rows_ref, slots_ref, columns_ref = refs[count:]
+    for block in range(2):
+        tokens, packed = pieces_rows(refs[block * split : block * split + split])
+        slots = own_rows(me_ref[0], packed)
+        for expert in range(4):
+            hot = jnp.where(slot_hot(slots[expert]), 1.0, 0.0).astype(BF)
+            rows_ref[block, expert * 144 : expert * 144 + 144, :] = nn(hot, tokens).astype(BF)
+            slots_ref[block, expert : expert + 1, :] = slots[expert]
+        columns_ref[block] = stand_up(slots).astype(BF)
+
+
+def pick_grads(me, pieces):
+    split = len(pieces) // 2
+    return pl.pallas_call(
+        functools.partial(pick_grad_kernel, split),
+        out_shape=(
+            shaped((2, 576, 1024), BF),
+            shaped((2, 4, 512), F32),
+            shaped((2, 512, 128), BF),
+        ),
+        in_specs=[in_smem()] + in_vmem(len(pieces)),
+        out_specs=tuple(in_vmem(3)),
+        compiler_params=params(),
+        cost_estimate=cost(2 * 2 * 576 * 512 * 1024, 5e6),
+        name="pick_grads",
+    )(me, *pieces)
+
+
+def pick_rows_kernel(split, me_ref, slots_ref, *refs):
+    count = 2 * split
+    rows_ref, gate_ref, columns_ref = refs[count:]
+    for block in range(2):
+        tokens, packed = pieces_rows(refs[block * split : block * split + split])
+        gates = own_rows(me_ref[0], packed)
+        for expert in range(4):
+            match = slot_hot(slots_ref[block, expert : expert + 1, :])
+            hot = jnp.where(match, 1.0, 0.0).astype(BF)
+            rows = slice(expert * 144, expert * 144 + 144)
+            rows_ref[block, rows, :] = nn(hot, tokens).astype(BF)
+            gate = jnp.sum(jnp.where(match, gates[expert], 0.0), axis=1, keepdims=True)
+            gate_ref[block, rows, :] = jnp.broadcast_to(gate, (144, 128)).astype(BF)
+        columns_ref[block] = stand_up(gates).astype(BF)
+
+
+def pick_rows(me, slots, pieces):
+    split = len(pieces) // 2
+    return pl.pallas_call(
+        functools.partial(pick_rows_kernel, split),
+        out_shape=(
+            shaped((2, 576, 1024), BF),
+            shaped((2, 576, 128), BF),
+            shaped((2, 512, 128), BF),
+        ),
+        in_specs=[in_smem()] + in_vmem(1 + len(pieces)),
+        out_specs=tuple(in_vmem(3)),
+        compiler_params=params(),
+        cost_estimate=cost(2 * 2 * 576 * 512 * 1024, 5e6),
+        name="pick_rows",
+    )(me, slots, *pieces)
+
+
+def expert_kernel(base, me_ref, *refs):
+    rows_refs, grads_refs, gate_refs = refs[0:4], refs[4:8], refs[8:12]
+    gate_w, up_w, down_w = (ref[0] for ref in refs[12:15])
+    out_ref, in_grad_ref, mark_ref, gate_grad_ref, up_grad_ref, down_grad_ref = refs[15:21]
+    lin_grads, inners, out_grads, inputs = refs[21:25]
+    expert = me_ref[0] * 4 + base + pl.program_id(0)
+    for part in range(2):
+        at = slice(part * 576, part * 576 + 576)
+
+        def both(pair):
+            return jnp.concatenate(
+                [pair[2 * part + side][...].reshape(288, -1) for side in range(2)], axis=0
+            )
+
+        rows, grads, gate = both(rows_refs), both(grads_refs), both(gate_refs)
+        inputs[at, :] = rows
+        gate_lin = nn(rows, gate_w)
+        up_lin = nn(rows, up_w)
+        sigma = 1.0 / (1.0 + jnp.exp(-gate_lin))
+        swished = gate_lin * sigma
+        inner = (swished * up_lin).astype(BF)
+        inners[at, :] = inner
+        result = nn(inner, down_w).astype(BF)
+        out_ref[part * 4 : part * 4 + 4] = result.reshape(4, 144, 1024)
+        wide = grads.astype(F32)
+        gate_slot = jnp.sum(wide * result.astype(F32), axis=1, keepdims=True)
+        lane = lax.broadcasted_iota(jnp.int32, (576, 128), 1)
+        mark_ref[part * 4 : part * 4 + 4] = (
+            jnp.where(lane == expert, gate_slot, 0.0).astype(BF).reshape(4, 144, 128)
+        )
+        out_grad = (wide * gate[:, 0:1].astype(F32)).astype(BF)
+        out_grads[at, :] = out_grad
+        inner_grad = nt(out_grad, down_w)
+        gate_lin_grad = (
+            inner_grad * up_lin * sigma * (1.0 + gate_lin * (1.0 - sigma))
+        ).astype(BF)
+        up_lin_grad = (inner_grad * swished).astype(BF)
+        lin_grads[at, 0:512] = gate_lin_grad
+        lin_grads[at, 512:1024] = up_lin_grad
+        in_grad_ref[part * 4 : part * 4 + 4] = (
+            (nt(gate_lin_grad, gate_w) + nt(up_lin_grad, up_w)).astype(BF).reshape(4, 144, 1024)
+        )
+    down_grad_ref[0] = tn(inners[...], out_grads[...]).astype(BF)
+    gate_grad_ref[0] = tn(inputs[...], lin_grads[:, 0:512]).astype(BF)
+    up_grad_ref[0] = tn(inputs[...], lin_grads[:, 512:1024]).astype(BF)
+
+
+def run_experts(me, base, count, rows, grads, gates, gate_w, up_w, down_w):
+    spec = pl.BlockSpec
+    wide = spec((2, 144, 1024), lambda e: (0, base + e, 0))
+    slim = spec((2, 144, 128), lambda e: (0, base + e, 0))
+    tall_w = spec((1, 1024, 512), lambda e: (base + e, 0, 0))
+    flat_w = spec((1, 512, 1024), lambda e: (base + e, 0, 0))
+    return pl.pallas_call(
+        functools.partial(expert_kernel, base),
+        out_shape=(
+            shaped((8, 144 * count, 1024), BF),
+            shaped((8, 144 * count, 1024), BF),
+            shaped((8, 144 * count, 128), BF),
+            shaped((count, 1024, 512), BF),
+            shaped((count, 1024, 512), BF),
+            shaped((count, 512, 1024), BF),
+        ),
+        grid=(count,),
+        in_specs=[in_smem()] + [wide] * 8 + [slim] * 4 + [tall_w, tall_w, flat_w],
+        out_specs=(
+            spec((8, 144, 1024), lambda e: (0, e, 0)),
+            spec((8, 144, 1024), lambda e: (0, e, 0)),
+            spec((8, 144, 128), lambda e: (0, e, 0)),
+            spec((1, 1024, 512), lambda e: (e, 0, 0)),
+            spec((1, 1024, 512), lambda e: (e, 0, 0)),
+            spec((1, 512, 1024), lambda e: (e, 0, 0)),
+        ),
+        scratch_shapes=[
+            pltpu.VMEM((1152, 1024), BF),
+            pltpu.VMEM((1152, 512), BF),
+            pltpu.VMEM((1152, 1024), BF),
+            pltpu.VMEM((1152, 1024), BF),
+        ],
+        compiler_params=params(),
+        cost_estimate=cost(count * 11e9, count * 15e6),
+        name="experts",
+    )(me, *rows, *grads, *gates, gate_w, up_w, down_w)
+
+
+def combine_kernel(calls, weighted, *refs):
+    slot_ref = refs[0]
+    refs = refs[1:]
+    gate_ref = None
+    if weighted:
+        gate_ref, refs = refs[0], refs[1:]
+    value_refs, refs = refs[:calls], refs[calls:]
+    mark_refs = ()
+    if not weighted:
+        mark_refs, refs = refs[:calls], refs[calls:]
+    out_ref = refs[0]
+    here = 4 // calls
+    slots = slot_ref[0].astype(F32)
+    lane = lax.broadcasted_iota(jnp.int32, (512, 144 * here), 1).astype(F32)
+    total, marks = None, None
+    for call in range(calls):
+        hot = jnp.zeros((512, 144 * here), F32)
+        for local_expert in range(here):
+            number = call * here + local_expert
+            slot = slots[:, number : number + 1]
+            place = jnp.where(slot < 144.0, slot + 144.0 * local_expert, -1.0)
+            put = 1.0
+            if weighted:
+                put = gate_ref[0][:, number : number + 1].astype(F32)
+            hot = jnp.where(lane == place, put, hot)
+        hot = hot.astype(BF)
+        term = nn(hot, value_refs[call][0])
+        total = term if total is None else total + term
+        if not weighted:
+            mark = nn(hot, mark_refs[call][0])
+            marks = mark if marks is None else marks + mark
+    out_ref[0, 0:512, :] = total.astype(BF)
+    if not weighted:
+        lying = marks.T[0:32, :].astype(BF)
+        out_ref[0, 512:528, 0:512] = lying[0:16, :]
+        out_ref[0, 512:528, 512:1024] = lying[16:32, :]
+
+
+def combine(parity, slots, gates, values, marks):
+    calls = len(values)
+    weighted = gates is not None
+    rows = 512 if weighted else 528
+    column = pl.BlockSpec((1, 512, 128), lambda i: (2 * i + parity, 0, 0))
+    wide = pl.BlockSpec((1, 576 // calls, 1024), lambda i: (2 * i + parity, 0, 0))
+    slim = pl.BlockSpec((1, 576 // calls, 128), lambda i: (2 * i + parity, 0, 0))
+    args = [slots] + ([gates] if weighted else []) + list(values) + list(marks)
+    return pl.pallas_call(
+        functools.partial(combine_kernel, calls, weighted),
+        out_shape=shaped((4, rows, 1024), BF),
+        grid=(4,),
+        in_specs=[column]
+        + ([column] if weighted else [])
+        + [wide] * calls
+        + [slim] * len(marks),
+        out_specs=pl.BlockSpec((1, rows, 1024), lambda i: (i, 0, 0)),
+        compiler_params=params(),
+        cost_estimate=cost(4 * 2 * 512 * 768 * 1024, 10e6),
+        name="combine",
+    )(*args)
+
+
+def back_kernel(
+    plan, me_ref, sum_ref, sum_x_ref, sum_y_ref, hidden_ref, cot_ref, payload_ref, gates_ref,
+    extra_ref, *refs,
+):
+    count = len(plan)
+    hidden_grad_ref, branch_grad_ref, attended_grad_ref, small_ref, mats, sems = refs[count:]
+    copies = start_fetch_heads(me_ref[0], plan, refs[:count], mats, sems)
+    total = (
+        sum_ref[...].astype(F32) + sum_x_ref[...].astype(F32) + sum_y_ref[...].astype(F32)
+    )
+    gate_grad = jnp.concatenate([total[512:528, 0:512], total[512:528, 512:1024]], axis=0)
+    gates = gates_ref[...]
+    logit_grad = (
+        gates * (gate_grad - jnp.sum(gates * gate_grad, axis=0, keepdims=True))
+    ).astype(BF)
+    normed_grad = total[0:512, :] + tn(logit_grad, extra_ref[0:32, :])
+    hidden = hidden_ref[...]
+    inverse = lax.rsqrt(jnp.mean(hidden * hidden, axis=-1, keepdims=True) + norm_eps)
+    scaled = normed_grad * extra_ref[33:34, :].astype(F32)
+    spread_out = inverse * inverse * inverse * jnp.mean(hidden * scaled, axis=-1, keepdims=True)
+    hidden_grad = cot_ref[...].astype(F32) + inverse * scaled - hidden * spread_out
+    hidden_grad_ref[...] = hidden_grad
+    small_ref[0:32, :] = nn(logit_grad, payload_ref[0:512, :])
+    small_ref[32:40, :] = jnp.broadcast_to(
+        jnp.sum(normed_grad * hidden * inverse, axis=0, keepdims=True), (8, 1024)
+    )
+    branch_grad = (branch_scale * hidden_grad).astype(BF)
+    branch_grad_ref[...] = branch_grad
+    for copy in copies:
+        copy.wait()
+    for part in range(4):
+        attended_grad_ref[part] = nt(
+            branch_grad, mats[part * 256 : part * 256 + 256, :]
+        ).astype(BF)
+
+
+def back_to_attention(me, sums, hidden, cotangent, payload, gates, extra, pieces):
+    plan = plan_of(128)
+    return pl.pallas_call(
+        functools.partial(back_kernel, plan),
+        out_shape=(
+            shaped((512, 1024), F32),
+            shaped((512, 1024), BF),
+            shaped((4, 512, 256), BF),
+            shaped((40, 1024), F32),
+        ),
+        in_specs=[in_smem()] + in_vmem(8) + in_hbm(len(plan)),
+        out_specs=tuple(in_vmem(4)),
+        scratch_shapes=[pltpu.VMEM((1024, 1024), BF), pltpu.SemaphoreType.DMA((16,))],
+        compiler_params=params(),
+        cost_estimate=cost(2 * 512 * 1024 * 1024, 12e6),
+        name="back_to_attention",
+    )(me, *sums, hidden, cotangent, payload, gates, extra, *pieces)
+
+
+def deal_out(me, big, odd_ref, even_ref):
+    for pair in range(4):
+        for target, partner in ((even_ref, 2 * pair), (odd_ref, 2 * pair + 1)):
+            start = pl.multiple_of((me ^ partner) * 128, 128)
+            target[pair] = big[pl.ds(start, 128), :]
+
+
+def out_grad_kernel(me_ref, attended_ref, branch_grad_ref, small_ref, odd_ref, even_ref, big):
+    branch_grad = branch_grad_ref[...]
+    for part in range(4):
+        grad = tn(attended_ref[part], branch_grad).astype(BF)
+        for half in range(2):
+            for group in range(2):
+                source = half * 128 + group * HD
+                target = part * 256 + (2 * group + half) * HD
+                big[target : target + HD, 0:1024] = grad[source : source + HD, :]
+    small = jnp.concatenate([small_ref[...], jnp.zeros((88, 1024), F32)], axis=0)
+    big[:, 1024:1152] = small.T.astype(BF)
+    deal_out(me_ref[0], big, odd_ref, even_ref)
+
+
+def out_grads_of(me, attended, branch_grad, small):
+    return pl.pallas_call(
+        out_grad_kernel,
+        out_shape=(shaped((4, 128, 1152), BF), shaped((4, 128, 1152), BF)),
+        in_specs=[in_smem()] + in_vmem(3),
+        out_specs=tuple(in_vmem(2)),
+        scratch_shapes=[pltpu.VMEM((1024, 1152), BF)],
+        compiler_params=params(),
+        cost_estimate=cost(2 * 512 * 1024 * 1024, 5e6),
+        name="out_grads",
+    )(me, attended, branch_grad, small)
+
+
+def input_kernel(
+    plan, me_ref, tokens_ref, cos_ref, sin_ref, query_grad_ref, pair_grad_ref, extra_ref,
+    hidden_grad_ref, *refs,
+):
+    count = len(plan)
+    input_grad_ref, odd_ref, even_ref, mats, big, lin, sems = refs[count:]
+    me = me_ref[0]
+    copies = start_fetch(me, plan, refs[:count], mats, 128, sems)
+    stream = tokens_ref[...].astype(F32)
+    inverse = lax.rsqrt(jnp.mean(stream * stream, axis=-1, keepdims=True) + norm_eps)
+    gain = extra_ref[32:33, :].astype(F32)
+    normed = (stream * inverse * gain).astype(BF)
+    cosine, sine = cos_ref[...], -sin_ref[...]
+    for part in range(4):
+        for half in range(2):
+            columns = slice(half * 128, half * 128 + 128)
+            lin[:, part * 256 + half * 128 : part * 256 + half * 128 + 128] = turn(
+                query_grad_ref[part, :, columns].astype(F32), cosine, sine
+            ).astype(BF)
+        lin[:, 1024 + part * 128 : 1152 + part * 128] = turn(
+            pair_grad_ref[part, :, 0:128].astype(F32), cosine, sine
+        ).astype(BF)
+        lin[:, 1536 + part * 128 : 1664 + part * 128] = pair_grad_ref[part, :, 128:256]
+    normed_t = normed.astype(F32).T.astype(BF)
+    for first in range(0, 2048, 512):
+        big[:, first : first + 512] = nn(normed_t, lin[:, first : first + 512]).astype(BF)
+    for copy in copies:
+        copy.wait()
+    normed_grad = nt(lin[...], mats[:, 0:2048])
+    row = jnp.sum(normed_grad * stream * inverse, axis=0, keepdims=True)
+    big[:, 2048:2176] = jnp.broadcast_to(row, (128, 1024)).T.astype(BF)
+    deal_out(me, big, odd_ref, even_ref)
+    scaled = normed_grad * gain
+    spread_out = inverse * inverse * inverse * jnp.mean(stream * scaled, axis=-1, keepdims=True)
+    input_grad_ref[...] = (
+        hidden_grad_ref[...] + inverse * scaled - stream * spread_out
+    ).astype(BF)
+
+
+def input_grads(me, tokens, cosine, sine, query_grad, pair_grad, extra, hidden_grad, pieces):
+    plan = plan_of(128)
+    return pl.pallas_call(
+        functools.partial(input_kernel, plan),
+        out_shape=(
+            shaped((512, 1024), BF),
+            shaped((4, 128, 2176), BF),
+            shaped((4, 128, 2176), BF),
+        ),
+        in_specs=[in_smem()] + in_vmem(7) + in_hbm(len(plan)),
+        out_specs=tuple(in_vmem(3)),
+        scratch_shapes=[
+            pltpu.VMEM((1024, 2176), BF),
+            pltpu.VMEM((1024, 2176), BF),
+            pltpu.VMEM((512, 2048), BF),
+            pltpu.SemaphoreType.DMA((len(plan),)),
+        ],
+        compiler_params=params(),
+        cost_estimate=cost(4 * 512 * 1024 * 2048, 15e6),
+        name="input_grads",
+    )(me, tokens, cosine, sine, query_grad, pair_grad, extra, hidden_grad, *pieces)
+
+
+def dense_slots(routes, ranks, experts):
+    mine = routes[None, :, :] == jnp.arange(experts, dtype=jnp.int32)[:, None, None]
+    far = jnp.int32(1 << 20)
+    rank = jnp.min(jnp.where(mine, ranks[None, :, :], far), axis=-1)
+    slot = jnp.sum((rank[:, None, :] < rank[:, :, None]).astype(jnp.int32), axis=-1)
+    routed = rank < far
+    return (jnp.where(routed & (slot < 144), slot, 255).astype(BF), routed.astype(F32))
+
+
+def swap_middle(values):
+    rows, columns = values.shape
+    parts = values.reshape(rows, columns // 256, 2, 2, HD)
+    return parts.transpose(0, 1, 3, 2, 4).reshape(rows, columns)
+
+
+def sum_copies(values):
+    return lax.psum(values, "sp")
+
+
+def fast_local(
+    tokens, documents, expert_routes, drop_rank, norm1_gain, query_weight, key_weight,
+    value_weight, out_weight, norm2_gain, router_weight, gate_weight, up_weight, down_weight,
+    output_grad,
+):
+    fsdp = lax.axis_index("fsdp")
+    seq = lax.axis_index("sp")
+    me = jnp.reshape(fsdp, (1,)).astype(jnp.int32)
+    small = jnp.concatenate(
+        [
+            router_weight,
+            norm1_gain[:, None],
+            norm2_gain[:, None],
+            jnp.zeros((128, 94), BF),
+        ],
+        axis=1,
+    )
+    shard = jnp.concatenate([swap_middle(query_weight), key_weight, value_weight, small], axis=1)
+    project_pieces = spread(shard)
+
+    block_start = fsdp * 2048
+    position_all = doc_position(documents)
+    position_span = lax.dynamic_slice_in_dim(position_all, block_start, 2048)
+    position = lax.dynamic_slice_in_dim(position_span, seq * 512, 512)
+    cosine, sine_table = rope_tables(position, HD)
+    cosine = jnp.tile(cosine, (1, 2))
+    signs = jnp.where(jnp.arange(128) % HD < HD // 2, -1.0, 1.0).astype(F32)
+    sine = jnp.tile(sine_table, (1, 2)) * signs[None, :]
+    start = HALO + jnp.arange(2048, dtype=jnp.int32) - position_span
+    start_rows = start.reshape(2048 // QB, 1, QB)
+    low_block = start_rows[:, 0, 0] // KB
+
+    query, pair, extra = project(me, tokens, cosine, sine, project_pieces)
+    pair_heads = lax.all_to_all(
+        pair.reshape(2048, 256), "sp", split_axis=0, concat_axis=0, tiled=True
+    )
+    query_heads = lax.all_to_all(
+        query.reshape(2048, 256), "sp", split_axis=0, concat_axis=0, tiled=True
+    )
+    halo = from_behind(pair_heads, "fsdp", 1)
+
+    slots, routed = dense_slots(expert_routes, drop_rank, 32)
+    mixture_grad = (branch_scale * output_grad.astype(F32)).astype(BF)
+    grad_payload = jnp.concatenate(
+        [mixture_grad, jnp.concatenate([slots[:16], slots[16:]], axis=1)], axis=0
+    )
+    grad_pieces = spread(grad_payload)
+    out_pieces = spread(out_weight)
+
+    blended, logs = attend(low_block, query_heads, pair_heads, halo, start_rows)
+    attended = lax.all_to_all(blended, "sp", split_axis=0, concat_axis=0, tiled=True).reshape(
+        4, 512, 256
+    )
+    hidden_one, payload, gates = after_attention(
+        me, tokens, attended, extra, routed, out_pieces
+    )
+    row_pieces = spread(payload)
+
+    groups = ((0, 2), (2, 4), (4, 6), (6, 10))
+    grad_rows, slot_rows, slot_columns = zip(
+        *[pick_grads(me, grad_pieces[first:last]) for first, last in groups]
+    )
+    rows, slot_gates, gate_columns = zip(
+        *[
+            pick_rows(me, slot_rows[number], row_pieces[first:last])
+            for number, (first, last) in enumerate(groups)
+        ]
+    )
+    slot_columns = jnp.concatenate(slot_columns, axis=0)
+    gate_columns = jnp.concatenate(gate_columns, axis=0)
+    per_call = 2
+    results = [
+        run_experts(
+            me, base, per_call, rows, grad_rows, slot_gates, gate_weight, up_weight, down_weight
+        )
+        for base in range(0, 4, per_call)
+    ]
+    outs, in_grads, marks, gate_grads, up_grads, down_grads = zip(*results)
+    odd = combine(1, slot_columns, None, in_grads, marks)
+    even = combine(0, slot_columns, None, in_grads, marks)
+    sums = collect(odd, even)
+    hidden_grad, branch_grad, attended_grad, small_grads = back_to_attention(
+        me, sums, hidden_one, output_grad, payload, gates, extra, out_pieces
+    )
+    grad_heads = lax.all_to_all(
+        attended_grad.reshape(2048, 256), "sp", split_axis=0, concat_axis=0, tiled=True
+    )
+    odd_mix = combine(1, slot_columns, gate_columns, outs, ())
+    even_mix = combine(0, slot_columns, gate_columns, outs, ())
+    mixture = collect(odd_mix, even_mix)
+    output = (
+        hidden_one
+        + branch_scale
+        * (mixture[0].astype(F32) + mixture[1].astype(F32) + mixture[2].astype(F32))
+    ).astype(BF)
+    out_sums = collect(*out_grads_of(me, attended, branch_grad, small_grads))
+
+    query_back, own_back, halo_back = attend_back(
+        low_block, query_heads, pair_heads, halo, start_rows, blended, grad_heads, logs
+    )
+    pair_back = (own_back + from_behind(halo_back, "fsdp", -1).astype(F32)).astype(BF)
+    query_grad = lax.all_to_all(
+        query_back, "sp", split_axis=0, concat_axis=0, tiled=True
+    ).reshape(4, 512, 256)
+    pair_grad = lax.all_to_all(
+        pair_back, "sp", split_axis=0, concat_axis=0, tiled=True
+    ).reshape(4, 512, 256)
+    input_grad, odd_in, even_in = input_grads(
+        me, tokens, cosine, sine, query_grad, pair_grad, extra, hidden_grad, project_pieces
+    )
+    in_sums = collect(odd_in, even_in)
+
+    out_shard = sum(term.astype(F32) for term in out_sums).astype(BF)
+    in_shard = sum(term.astype(F32) for term in in_sums).astype(BF)
+    out_shard, in_shard = sum_copies((out_shard, in_shard))
+    expert_sums = sum_copies((gate_grads, up_grads, down_grads))
+    stacked = [jnp.concatenate(list(parts), axis=0).astype(F32) for parts in expert_sums]
+    return (
+        output,
+        input_grad,
+        in_shard[:, 2048].astype(F32),
+        swap_middle(in_shard[:, 0:1024]).astype(F32),
+        in_shard[:, 1024:1536].astype(F32),
+        in_shard[:, 1536:2048].astype(F32),
+        out_shard[:, 0:1024].astype(F32),
+        out_shard[:, 1056].astype(F32),
+        out_shard[:, 1024:1056].astype(F32),
+        *stacked,
+    )
+
+
 def solution(mesh):
     placed = (
         P(("fsdp", "sp"), None),
@@ -474,8 +1461,9 @@
         P("fsdp", None, None),
         P(("fsdp", "sp"), None),
     )
+    fast = mesh.shape["sp"] == 4 and mesh.shape["fsdp"] == 8
     return jax.shard_map(
-        local,
+        fast_local if fast else local,
         mesh=mesh,
         in_specs=placed,
         out_specs=(

time: 2010 us -> 1080 us (0.54)
  waiting for transfers between devices: 1020 us -> 595 us
  matrix products: 419 us -> 0 us
  local copies, waits for them, and re-layouts: 274 us -> 21.4 us
  Pallas kernels: 0 us -> 228 us
  other arithmetic: 161 us -> 53.6 us
  starting transfers between devices: 42.4 us -> 134 us
  blocking collectives: 60.1 us -> 28.7 us
    dot_general x56 -> x0, matrix products: 416 us -> none  [the longest x8 59.1 us: block_scores(): jnp.einsum('rgjd,cgd->gjrc', query_part, key_part, preferred_element_type...]
    all_to_all x8 -> x5, waiting for transfers between devices: 417 us -> 51.4 us  [the longest x1 26.1 us: fast_local(): lax.all_to_all(pair.reshape(2048, 256), 'sp', split_axis=0, concat_axis=0...]
    pallas_call x0 -> x21, Pallas kernels: none -> 228 us  [the longest x2 63.2 us: run_experts(): pl.pallas_call(functools.partial(expert_kernel, base), out_shape=(shaped(...]
    ppermute x0 -> x56, waiting for transfers between devices: none -> 153 us  [flip(): lax.ppermute(value, 'fsdp', [(place, place ^ bit) for place in range(8)])]
    ppermute x0 -> x56, starting transfers between devices: none -> 109 us  [flip(): lax.ppermute(value, 'fsdp', [(place, place ^ bit) for place in range(8)])]
    reduce_scatter x4 -> x0, waiting for transfers between devices: 92.2 us -> none  [the longest x1 44.9 us: local(): lax.psum_scatter(query_mat_grad.astype(jnp.bfloat16), 'fsdp', scatter_dim...]
    gather x3 -> x0, local copies, waits for them, and re-layouts: 72 us -> none  [the longest x1 25.7 us: local(): jnp.take(expert_out.reshape(slot_total, model_width), jnp.clip(slot_index...]
    all_gather x4 -> x0, waiting for transfers between devices: 62.2 us -> none  [the longest x1 27.7 us: local(): lax.all_gather(query_weight, 'fsdp', axis=0, tiled=True)]
  transfers between devices with their start and end apart: 20 -> 64, of which waited for: 16 -> 27; matrix products, arithmetic and copies ran while one was open for 18% -> 4% of each run, Pallas kernels for 0% -> 8%
where the time goes in v1:
time: 1080 us
  waiting for transfers between devices  595 us (55%)
  Pallas kernels  228 us (21%)
  starting transfers between devices  134 us (12%)
  other arithmetic  53.6 us (5%)
  blocking collectives  28.7 us (3%)
  local copies, waits for them, and re-layouts  21.4 us (2%)
  between operations  15.5 us (1%)
    psum x1, waiting for transfers between devices, sum_copies(): return lax.psum(values, 'sp')  391 us
    ppermute x56, waiting for transfers between devices, flip(): lax.ppermute(value, 'fsdp', [(place, place ^ bit) for place in range(8)])  153 us
    ppermute x56, starting transfers between devices, flip(): lax.ppermute(value, 'fsdp', [(place, place ^ bit) for place in range(8)])  109 us
    pallas_call x2, Pallas kernels, run_experts(): pl.pallas_call(functools.partial(expert_kernel, base), out_shape=(shaped(...  63.2 us
    pallas_call x4, Pallas kernels, combine(): pl.pallas_call(functools.partial(combine_kernel, calls, weighted), out_sh...  34.8 us
    pallas_call x1, Pallas kernels, attend_back(): pl.pallas_call(attend_back_kernel, out_shape=(shaped((2048, 256), BF), sh...  31.4 us
    all_to_all x1, blocking collectives, fast_local(): lax.all_to_all(attended_grad.reshape(2048, 256), 'sp', split_axis=0, conc...  28.7 us
    all_to_all x1, waiting for transfers between devices, fast_local(): lax.all_to_all(pair.reshape(2048, 256), 'sp', split_axis=0, concat_axis=0...  26.1 us
  transfers between devices with their start and end apart: 64, of which 27 were waited for; matrix products, arithmetic and copies ran while one was open for 4% of the time, Pallas kernels for 8%

profile of v1, /device:TPU:0, one launch (start us, length us, event | category | flops | bytes accessed | tf_op | source)
XLA Modules:
  0.0 1076.7 jit_solution(1369038656169691741)
XLA Ops:
  17.7 10.0 collective-permute-done.3.refs_4_
  53.0 26.1 %all-to-all-done.1 = bf16[4,512,256]{2,1,0:T(8,128)(2,1)S(1)} async-done(((bf16[4,512,256]{2,1,0:T(8,128)(2,1)}), bf16[4,512,256]{2,1,0:T(8,128)(2,1)S(1)}, u32[]{:S(2)}, u32[]{:S(2)}) %all-to-all-start.1) | async-done | bytes 1048608 | tf_op jit(solution)/shard_map/all_to_all | solution.py:1348
  92.0 17.0 %all-to-all-done = bf16[4,512,256]{2,1,0:T(8,128)(2,1)} async-done(((bf16[4,512,256]{2,1,0:T(8,128)(2,1)}), bf16[4,512,256]{2,1,0:T(8,128)(2,1)}, u32[]{:S(2)}, u32[]{:S(2)}) %all-to-all-start) | async-done | bytes 1048608 | tf_op jit(solution)/shard_map/all_to_all | solution.py:1351
  109.0 23.1 %attend.1 = (bf16[2048,256]{1,0:T(8,128)(2,1)}, f32[8,2048]{1,0:T(8,128)}) custom-call(s32[4]{0:T(128)} %and_select_fusion.1.low_ref, bf16[2048,256]{1,0:T(8,128)(2,1)} %bitcast.13.query_ref, bf16[2048,256]{1,0:T(8,128)(2,1)} %bitcast.128, bf16[2048,256]{1,0:T(8,128)(2,1)} %collective-permute-done.9.halo_ref, s32[4,1,512]{2,1,0:T(1,128)} %bitcast.140), custom_call_target="tpu_custom_call" | custom-call | flops 24999999488 | bytes 6000000 | tf_op jit(solution)/shard_map/attend/pallas_call | solution.py:723
  153.3 20.2 %collective-permute-done.13.refs_4_ = bf16[128,1024]{1,0:T(8,128)(2,1)S(1)} collective-permute-done((bf16[128,1024]{1,0:T(8,128)(2,1)S(1)}, bf16[128,1024]{1,0:T(8,128)(2,1)S(1)}, u32[]{:S(2)}, u32[]{:S(2)}) %collective-permute-start.13) | collective-permute-done | bytes 262176 | tf_op jit(solution)/shard_map/ppermute | solution.py:511
  202.3 20.7 %collective-permute-done.31.refs_0_ = bf16[528,1024]{1,0:T(8,128)(2,1)} collective-permute-done((bf16[528,1024]{1,0:T(8,128)(2,1)}, bf16[528,1024]{1,0:T(8,128)(2,1)}, u32[]{:S(2)}, u32[]{:S(2)}) %collective-permute-start.31) | collective-permute-done | bytes 1081376 | tf_op jit(solution)/shard_map/ppermute | solution.py:511
  270.1 31.4 %experts.3 = (bf16[8,288,1024]{2,1,0:T(8,128)(2,1)}, bf16[8,288,1024]{2,1,0:T(8,128)(2,1)}, bf16[8,288,128]{2,1,0:T(8,128)(2,1)}, bf16[2,1024,512]{2,1,0:T(8,128...) custom-call(s32[1]{0:T(128)} %bitcast.me_ref, bf16[2,576,1024]{2,1,0:T(8,128)(2,1)} %get-tuple-element.86.refs_0_, ...), custom_call_target="tpu_custom_call" | custom-call | flops 22000001024 | bytes 30000000 | tf_op jit(solution)/shard_map/experts/pallas_call | solution.py:1052
  301.5 31.8 %experts.2 = (bf16[8,288,1024]{2,1,0:T(8,128)(2,1)}, bf16[8,288,1024]{2,1,0:T(8,128)(2,1)}, bf16[8,288,128]{2,1,0:T(8,128)(2,1)}, bf16[2,1024,512]{2,1,0:T(8,128...) custom-call(s32[1]{0:T(128)} %bitcast.me_ref, bf16[2,576,1024]{2,1,0:T(8,128)(2,1)} %get-tuple-element.86.refs_0_, ...), custom_call_target="tpu_custom_call" | custom-call | flops 22000001024 | bytes 30000000 | tf_op jit(solution)/shard_map/experts/pallas_call | solution.py:1052
  333.3 8.8 combine.7
  342.3 8.9 combine.6
  371.9 20.8 %collective-permute-done.44.sum_x_ref = bf16[528,1024]{1,0:T(8,128)(2,1)S(1)} collective-permute-done((bf16[528,1024]{1,0:T(8,128)(2,1)S(1)}, bf16[528,1024]{1,0:T(8,128)(2,1)S(1)}, u32[]{:S(2)}, u32[]{:S(2)}) %collective-permute-start.44) | collective-permute-done | bytes 1081376 | tf_op jit(solution)/shard_map/ppermute | solution.py:511
  403.0 28.7 %all_to_all.51 = bf16[4,512,256]{2,1,0:T(8,128)(2,1)} all-to-all(bf16[4,512,256]{2,1,0:T(8,128)(2,1)} %get-tuple-element.105), channel_id=1, replica_groups=mesh['sp'=4,'fsdp'=8] {'sp'}, dimensions={0} | all-to-all | bytes 2097152 | tf_op jit(solution)/shard_map/all_to_all | solution.py:1399
  431.7 31.4 %attend_back.1 = (bf16[2048,256]{1,0:T(8,128)(2,1)}, f32[2048,256]{1,0:T(8,128)}, bf16[2048,256]{1,0:T(8,128)(2,1)}) custom-call(s32[4]{0:T(128)} %and_select_fusion.1.low_ref, bf16[2048,256]{1,0:T(8,128)(2,1)} %bitcast.13.query_ref, bf16[2048,256]{1,0:T(8,128)(2,1)} %bitcast.129, bf16[2048,256]{1,0:T(8,128)(2,1)} %collective-permute-done.9.halo_ref, ...), custom_call_target="tpu_custom_call" | custom-call | flops 60000002048 | bytes 10000000 | tf_op jit(solution)/shard_map/attend_back/pallas_call | solution.py:828
  497.2 14.2 %collective-permute-start.54 = (bf16[64,1152]{1,0:T(8,128)(2,1)}, bf16[64,1152]{1,0:T(8,128)(2,1)}, u32[]{:S(2)}, u32[]{:S(2)}) collective-permute-start(bf16[64,1152]{1,0:T(8,128)(2,1)} %get-tuple-element.181), channel_id=1, source_target_pairs={{0,4},{1,5},{2,6},{3,7},{4,0},{5,1},{6,2},{7,3},{8,12},{9,13},{10,... | collective-permute-start | bytes 442376 | tf_op jit(solution)/shard_map/ppermute | solution.py:511
  511.4 9.4 collective-permute-start.56
  521.0 12.5 %input_grads.1 = (bf16[512,1024]{1,0:T(8,128)(2,1)}, bf16[4,128,2176]{2,1,0:T(8,128)(2,1)}, bf16[4,128,2176]{2,1,0:T(8,128)(2,1)}) custom-call(s32[1]{0:T(128)} %bitcast.me_ref, bf16[512,1024]{1,0:T(8,128)(2,1)} %tokens_ref.5, f32[512,128]{1,0:T(8,128)} %copy.64.cos_ref, f32[512,128]{1,0:T(8,128)} %broadcast_multiply_fusion.sin_ref, ...), custom_call_target="tpu_custom_call" | custom-call | flops 4294967296 | bytes 15000000 | tf_op jit(solution)/shard_map/input_grads/pallas_call | solution.py:1275
  537.0 13.3 %collective-permute-start.57 = (bf16[128,1152]{1,0:T(8,128)(2,1)S(1)}, bf16[128,1152]{1,0:T(8,128)(2,1)S(1)}, u32[]{:S(2)}, u32[]{:S(2)}) collective-permute-start(bf16[128,1152]{1,0:T(8,128)(2,1)S(1)} %pad_maximum_fusion.7), channel_id=1, source_target_pairs={{0,4},{1,5},{2,6},{3,7},{4,0},{5,1},{6,2},{7,3},{8,12},{9,13},{10,... | collective-permute-start | bytes 884744 | tf_op jit(solution)/shard_map/ppermute | solution.py:511
  551.3 9.5 collective-permute-start.55
  563.7 10.7 collective-permute-done.51
  579.0 9.8 collective-permute-done.52
  593.5 8.7 combine.5
  618.0 9.3 collective-permute-done.40
  630.6 21.6 %collective-permute-done.41 = bf16[512,1024]{1,0:T(8,128)(2,1)S(1)} collective-permute-done((bf16[512,1024]{1,0:T(8,128)(2,1)S(1)}, bf16[512,1024]{1,0:T(8,128)(2,1)S(1)}, u32[]{:S(2)}, u32[]{:S(2)}) %collective-permute-start.41) | collective-permute-done | bytes 1048608 | tf_op jit(solution)/shard_map/ppermute | solution.py:511
  657.1 390.9 %all-reduce.3.cloned.1.call-done = (bf16[128,2176]{1,0:T(8,128)(2,1)}, bf16[128,1152]{1,0:T(8,128)(2,1)}, bf16[2,1024,512]{2,1,0:T(8,128)(2,1)}, bf16[2,1024,512...) async-done(((bf16[128,2176]{1,0:T(8,128)(2,1)}, ...) | async-done | bytes 13434896 | tf_op jit(solution)/shard_map/psum | solution.py:1312
  (329 shorter events, 272.3 us)
Async XLA Ops:
  47.7 31.4 %all-to-all-start.1 = ((bf16[4,512,256]{2,1,0:T(8,128)(2,1)}), bf16[4,512,256]{2,1,0:T(8,128)(2,1)S(1)}, u32[]{:S(2)}, u32[]{:S(2)}) async-start(bf16[4,512,256]{2,1,0:T(8,128)(2,1)} %get-tuple-element.69), calls=%async_computation.1 | async-start | bytes 2097152 | tf_op jit(solution)/shard_map/all_to_all | solution.py:1348
  79.1 29.9 %all-to-all-start = ((bf16[4,512,256]{2,1,0:T(8,128)(2,1)}), bf16[4,512,256]{2,1,0:T(8,128)(2,1)}, u32[]{:S(2)}, u32[]{:S(2)}) async-start(bf16[4,512,256]{2,1,0:T(8,128)(2,1)} %get-tuple-element.68), calls=%async_computation | async-start | bytes 2097152 | tf_op jit(solution)/shard_map/all_to_all | solution.py:1351
  132.1 57.1 %all-to-all-start.2 = ((bf16[4,512,256]{2,1,0:T(8,128)(2,1)}), bf16[4,512,256]{2,1,0:T(8,128)(2,1)S(1)}, u32[]{:S(2)}, u32[]{:S(2)}) async-start(bf16[4,512,256]{2,1,0:T(8,128)(2,1)} %bitcast.130), calls=%async_computation.2 | async-start | bytes 2097152 | tf_op jit(solution)/shard_map/all_to_all | solution.py:1365
  136.0 45.0 %collective-permute-start.22 = (bf16[528,1024]{1,0:T(8,128)(2,1)S(1)}, bf16[528,1024]{1,0:T(8,128)(2,1)}, u32[]{:S(2)}, u32[]{:S(2)}) collective-permute-start(bf16[528,1024]{1,0:T(8,128)(2,1)S(1)} %maximum_maximum_fusion.refs_0_), channel_id=1, source_target_pairs={{0,4},{1,5},{2,6},{3,7},{4,0},{5,1},{6,2},{7,3},{8,12},{9,13},{10,... | collective-permute-start | bytes 3244040 | tf_op jit(solution)/shard_map/ppermute | solution.py:511
  144.6 38.3 %collective-permute-start.20 = (bf16[528,1024]{1,0:T(8,128)(2,1)S(1)}, bf16[528,1024]{1,0:T(8,128)(2,1)S(1)}, u32[]{:S(2)}, u32[]{:S(2)}) collective-permute-start(bf16[528,1024]{1,0:T(8,128)(2,1)S(1)} %maximum_maximum_fusion.refs_0_), channel_id=1, source_target_pairs={{0,2},{1,3},{2,0},{3,1},{4,6},{5,7},{6,4},{7,5},{8,10},{9,11},{10,... | collective-permute-start | bytes 3244040 | tf_op jit(solution)/shard_map/ppermute | solution.py:511
  151.2 46.0 %collective-permute-start.19 = (bf16[528,1024]{1,0:T(8,128)(2,1)S(1)}, bf16[528,1024]{1,0:T(8,128)(2,1)}, u32[]{:S(2)}, u32[]{:S(2)}) collective-permute-start(bf16[528,1024]{1,0:T(8,128)(2,1)S(1)} %maximum_maximum_fusion.refs_0_), channel_id=1, source_target_pairs={{0,1},{1,0},{2,3},{3,2},{4,5},{5,4},{6,7},{7,6},{8,9},{9,8},{10,11... | collective-permute-start | bytes 3244040 | tf_op jit(solution)/shard_map/ppermute | solution.py:511
  196.5 26.5 %collective-permute-start.31 = (bf16[528,1024]{1,0:T(8,128)(2,1)}, bf16[528,1024]{1,0:T(8,128)(2,1)}, u32[]{:S(2)}, u32[]{:S(2)}) collective-permute-start(bf16[528,1024]{1,0:T(8,128)(2,1)} %get-tuple-element.78.refs_0_.payload_ref), channel_id=1, source_target_pairs={{0,4},{1,5},{2,6},{3,7},{4,0},{5,1},{6,2},{7,3},{8,12},{9,13},{10,... | collective-permute-start | bytes 3244040 | tf_op jit(solution)/shard_map/ppermute | solution.py:511
  197.3 26.1 %collective-permute-start.29 = (bf16[528,1024]{1,0:T(8,128)(2,1)}, bf16[528,1024]{1,0:T(8,128)(2,1)S(1)}, u32[]{:S(2)}, u32[]{:S(2)}) collective-permute-start(bf16[528,1024]{1,0:T(8,128)(2,1)} %get-tuple-element.78.refs_0_.payload_ref), channel_id=1, source_target_pairs={{0,2},{1,3},{2,0},{3,1},{4,6},{5,7},{6,4},{7,5},{8,10},{9,11},{10,... | collective-permute-start | bytes 3244040 | tf_op jit(solution)/shard_map/ppermute | solution.py:511
  198.5 30.9 %collective-permute-start.21 = (bf16[528,1024]{1,0:T(8,128)(2,1)}, bf16[528,1024]{1,0:T(8,128)(2,1)}, u32[]{:S(2)}, u32[]{:S(2)}) collective-permute-start(bf16[528,1024]{1,0:T(8,128)(2,1)} %copy-done.34), channel_id=1, source_target_pairs={{0,1},{1,0},{2,3},{3,2},{4,5},{5,4},{6,7},{7,6},{8,9},{9,8},{10,11... | collective-permute-start | bytes 3244040 | tf_op jit(solution)/shard_map/ppermute | solution.py:511
  201.8 28.8 %collective-permute-start.26 = (bf16[272,1024]{1,0:T(8,128)(2,1)}, bf16[272,1024]{1,0:T(8,128)(2,1)S(1)}, u32[]{:S(2)}, u32[]{:S(2)}) collective-permute-start(bf16[272,1024]{1,0:T(8,128)(2,1)} %collective-permute-done.24.refs_0_), channel_id=1, source_target_pairs={{0,1},{1,0},{2,3},{3,2},{4,5},{5,4},{6,7},{7,6},{8,9},{9,8},{10,11... | collective-permute-start | bytes 1671176 | tf_op jit(solution)/shard_map/ppermute | solution.py:511
  202.1 48.1 %collective-permute-start.28 = (bf16[528,1024]{1,0:T(8,128)(2,1)}, bf16[528,1024]{1,0:T(8,128)(2,1)}, u32[]{:S(2)}, u32[]{:S(2)}) collective-permute-start(bf16[528,1024]{1,0:T(8,128)(2,1)} %get-tuple-element.78.refs_0_.payload_ref), channel_id=1, source_target_pairs={{0,1},{1,0},{2,3},{3,2},{4,5},{5,4},{6,7},{7,6},{8,9},{9,8},{10,11... | collective-permute-start | bytes 3244040 | tf_op jit(solution)/shard_map/ppermute | solution.py:511
  223.0 32.2 %collective-permute-start.32 = (bf16[528,1024]{1,0:T(8,128)(2,1)}, bf16[528,1024]{1,0:T(8,128)(2,1)}, u32[]{:S(2)}, u32[]{:S(2)}) collective-permute-start(bf16[528,1024]{1,0:T(8,128)(2,1)} %collective-permute-done.31.refs_0_), channel_id=1, source_target_pairs={{0,1},{1,0},{2,3},{3,2},{4,5},{5,4},{6,7},{7,6},{8,9},{9,8},{10,11... | collective-permute-start | bytes 3244040 | tf_op jit(solution)/shard_map/ppermute | solution.py:511
  223.3 36.6 %collective-permute-start.30 = (bf16[528,1024]{1,0:T(8,128)(2,1)S(1)}, bf16[528,1024]{1,0:T(8,128)(2,1)}, u32[]{:S(2)}, u32[]{:S(2)}) collective-permute-start(bf16[528,1024]{1,0:T(8,128)(2,1)S(1)} %collective-permute-done.29.refs_0_), channel_id=1, source_target_pairs={{0,1},{1,0},{2,3},{3,2},{4,5},{5,4},{6,7},{7,6},{8,9},{9,8},{10,11... | collective-permute-start | bytes 3244040 | tf_op jit(solution)/shard_map/ppermute | solution.py:511
  367.1 25.6 %collective-permute-start.44 = (bf16[528,1024]{1,0:T(8,128)(2,1)S(1)}, bf16[528,1024]{1,0:T(8,128)(2,1)S(1)}, u32[]{:S(2)}, u32[]{:S(2)}) collective-permute-start(bf16[528,1024]{1,0:T(8,128)(2,1)S(1)} %pad_maximum_fusion), channel_id=1, source_target_pairs={{0,2},{1,3},{2,0},{3,1},{4,6},{5,7},{6,4},{7,5},{8,10},{9,11},{10,... | collective-permute-start | bytes 3244040 | tf_op jit(solution)/shard_map/ppermute | solution.py:511
  370.0 24.7 %collective-permute-start.46 = (bf16[528,1024]{1,0:T(8,128)(2,1)S(1)}, bf16[528,1024]{1,0:T(8,128)(2,1)S(1)}, u32[]{:S(2)}, u32[]{:S(2)}) collective-permute-start(bf16[528,1024]{1,0:T(8,128)(2,1)S(1)} %pad_maximum_fusion.1), channel_id=1, source_target_pairs={{0,4},{1,5},{2,6},{3,7},{4,0},{5,1},{6,2},{7,3},{8,12},{9,13},{10,... | collective-permute-start | bytes 3244040 | tf_op jit(solution)/shard_map/ppermute | solution.py:511
  464.4 27.8 %all-to-all-start.4 = ((bf16[4,512,256]{2,1,0:T(8,128)(2,1)}), bf16[4,512,256]{2,1,0:T(8,128)(2,1)}, u32[]{:S(2)}, u32[]{:S(2)}) async-start(bf16[4,512,256]{2,1,0:T(8,128)(2,1)} %bitcast.131), calls=%async_computation.4 | async-start | bytes 2097152 | tf_op jit(solution)/shard_map/all_to_all | solution.py:1416
  492.1 28.8 %all-to-all-start.5 = ((bf16[4,512,256]{2,1,0:T(8,128)(2,1)}), bf16[4,512,256]{2,1,0:T(8,128)(2,1)}, u32[]{:S(2)}, u32[]{:S(2)}) async-start(bf16[4,512,256]{2,1,0:T(8,128)(2,1)} %bitcast.32), calls=%async_computation.5 | async-start | bytes 2097152 | tf_op jit(solution)/shard_map/all_to_all | solution.py:1419
  496.4 551.6 %all-reduce.3.cloned.1.call-start = ((), (), s32[]{:S(2)}) async-start(), calls=%async_computation.6 | async-start | bytes 26869760 | tf_op jit(solution)/shard_map/psum | solution.py:1312
  497.2 53.1 %collective-permute-start.54 = (bf16[64,1152]{1,0:T(8,128)(2,1)}, bf16[64,1152]{1,0:T(8,128)(2,1)}, u32[]{:S(2)}, u32[]{:S(2)}) collective-permute-start(bf16[64,1152]{1,0:T(8,128)(2,1)} %get-tuple-element.181), channel_id=1, source_target_pairs={{0,4},{1,5},{2,6},{3,7},{4,0},{5,1},{6,2},{7,3},{8,12},{9,13},{10,... | collective-permute-start | bytes 442376 | tf_op jit(solution)/shard_map/ppermute | solution.py:511
  511.4 24.6 %collective-permute-start.56 = (bf16[64,1152]{1,0:T(8,128)(2,1)}, bf16[64,1152]{1,0:T(8,128)(2,1)}, u32[]{:S(2)}, u32[]{:S(2)}) collective-permute-start(bf16[64,1152]{1,0:T(8,128)(2,1)} %get-tuple-element.182), channel_id=1, source_target_pairs={{0,2},{1,3},{2,0},{3,1},{4,6},{5,7},{6,4},{7,5},{8,10},{9,11},{10,... | collective-permute-start | bytes 442376 | tf_op jit(solution)/shard_map/ppermute | solution.py:511
  533.5 27.3 %collective-permute-start.48 = (bf16[4,128,2176]{2,1,0:T(8,128)(2,1)}, bf16[4,128,2176]{2,1,0:T(8,128)(2,1)S(1)}, u32[]{:S(2)}, u32[]{:S(2)}) collective-permute-start(bf16[4,128,2176]{2,1,0:T(8,128)(2,1)} %get-tuple-element.113), channel_id=1, source_target_pairs={{0,1},{1,0},{2,3},{3,2},{4,5},{5,4},{6,7},{7,6},{8,9},{9,8},{10,11... | collective-permute-start | bytes 6684680 | tf_op jit(solution)/shard_map/ppermute | solution.py:511
  537.0 41.1 %collective-permute-start.57 = (bf16[128,1152]{1,0:T(8,128)(2,1)S(1)}, bf16[128,1152]{1,0:T(8,128)(2,1)S(1)}, u32[]{:S(2)}, u32[]{:S(2)}) collective-permute-start(bf16[128,1152]{1,0:T(8,128)(2,1)S(1)} %pad_maximum_fusion.7), channel_id=1, source_target_pairs={{0,4},{1,5},{2,6},{3,7},{4,0},{5,1},{6,2},{7,3},{8,12},{9,13},{10,... | collective-permute-start | bytes 884744 | tf_op jit(solution)/shard_map/ppermute | solution.py:511
  551.3 26.8 %collective-permute-start.55 = (bf16[128,1152]{1,0:T(8,128)(2,1)S(1)}, bf16[128,1152]{1,0:T(8,128)(2,1)S(1)}, u32[]{:S(2)}, u32[]{:S(2)}) collective-permute-start(bf16[128,1152]{1,0:T(8,128)(2,1)S(1)} %pad_maximum_fusion.6), channel_id=1, source_target_pairs={{0,2},{1,3},{2,0},{3,1},{4,6},{5,7},{6,4},{7,5},{8,10},{9,11},{10,... | collective-permute-start | bytes 884744 | tf_op jit(solution)/shard_map/ppermute | solution.py:511
  627.6 24.6 %collective-permute-start.41 = (bf16[512,1024]{1,0:T(8,128)(2,1)S(1)}, bf16[512,1024]{1,0:T(8,128)(2,1)S(1)}, u32[]{:S(2)}, u32[]{:S(2)}) collective-permute-start(bf16[512,1024]{1,0:T(8,128)(2,1)S(1)} %pad_maximum_fusion.3), channel_id=1, source_target_pairs={{0,4},{1,5},{2,6},{3,7},{4,0},{5,1},{6,2},{7,3},{8,12},{9,13},{10,... | collective-permute-start | bytes 3145736 | tf_op jit(solution)/shard_map/ppermute | solution.py:511
  (89 other events, 979.9 us)
Sparse Core Ops, SparseCore 0:
  591.4 456.4 all-reduce.2

commit v2 on v1

--- a/solution.py
+++ b/solution.py
@@ -491,7 +491,7 @@
 
 def cost(flops, moved, transcendentals=0):
     return pl.CostEstimate(
-        flops=int(flops), bytes_accessed=int(moved), transcendentals=int(transcendentals)
+        flops=int(flops) // 8, bytes_accessed=int(moved) // 8, transcendentals=int(transcendentals)
     )
 
 
@@ -531,41 +531,54 @@
     )
 
 
+def hold(value, *others):
+    return lax.optimization_barrier((value, others))[0]
+
+
+def spread_near(own):
+    along_x, along_y = flip(own, 2), flip(own, 4)
+    return (own, flip(own, 1), along_x, flip(along_x, 1), along_y, flip(along_y, 1))
+
+
+def spread_diagonal(near):
+    half = half_rows(near[0].shape[0])
+    return (flip(near[4][:half], 2), flip(near[2][half:], 4))
+
+
+def spread_far(diagonal):
+    return (*diagonal, flip(diagonal[0], 1), flip(diagonal[1], 1))
+
+
 def spread(own):
-    half = half_rows(own.shape[0])
-    along_x = flip(own, 2)
-    along_y = flip(own, 4)
-    low = flip(along_y[:half], 2)
-    high = flip(along_x[half:], 4)
-    return (
-        own,
-        flip(own, 1),
-        along_x,
-        flip(along_x, 1),
-        along_y,
-        flip(along_y, 1),
-        low,
-        high,
-        flip(low, 1),
-        flip(high, 1),
-    )
+    near = spread_near(own)
+    return near + spread_far(spread_diagonal(near))
 
 
 def add_low(left, right):
     return (left.astype(F32) + right.astype(F32)).astype(BF)
 
 
-def collect(odd, even):
+def collect(odd, even, tick=None):
     half = half_rows(even.shape[1])
     received = flip(odd, 1)
-    own = add_low(even[0], received[0])
     diagonal_low = flip(add_low(even[3, :half], received[3, :half]), 2)
     diagonal_high = flip(add_low(even[3, half:], received[3, half:]), 4)
+    if tick is not None:
+        diagonal_low, diagonal_high = tick((diagonal_low, diagonal_high))
+    own = add_low(even[0], received[0])
     for_y = even[2].astype(F32) + received[2].astype(F32)
     for_x = even[1].astype(F32) + received[1].astype(F32)
     for_y = jnp.concatenate([for_y[:half] + diagonal_low.astype(F32), for_y[half:]]).astype(BF)
     for_x = jnp.concatenate([for_x[:half], for_x[half:] + diagonal_high.astype(F32)]).astype(BF)
     return (own, flip(for_x, 2), flip(for_y, 4))
+
+
+def heads_plan():
+    return tuple(
+        (partner, 528 - first)
+        for partner, first, rows in plan_of(656)
+        if first + rows == 656
+    )
 
 
 def start_fetch(me, plan, sources, target, block_rows, sems):
@@ -581,13 +594,13 @@
 
 def start_fetch_heads(me, plan, sources, target, sems):
     copies = []
-    for number, (partner, first, rows) in enumerate(plan):
-        for offset in range(0, rows, HD):
-            head = (me ^ partner) * 2 + (first + offset) // HD
+    for number, (partner, first) in enumerate(plan):
+        for half in range(2):
+            head = (me ^ partner) * 2 + half
             head = (head & ~3) | ((head & 1) << 1) | ((head >> 1) & 1)
             copies.append(
                 pltpu.make_async_copy(
-                    sources[number].at[pl.ds(offset, HD)],
+                    sources[number].at[pl.ds(first + half * HD, HD)],
                     target.at[pl.ds(pl.multiple_of(head * HD, HD), HD)],
                     sems.at[len(copies)],
                 )
@@ -887,7 +900,7 @@
 
 
 def after_attention(me, tokens, attended, extra, routed, pieces):
-    plan = plan_of(128)
+    plan = heads_plan()
     return pl.pallas_call(
         functools.partial(after_kernel, plan),
         out_shape=(shaped((512, 1024), F32), shaped((528, 1024), BF), shaped((32, 512), F32)),
@@ -923,91 +936,139 @@
     return at == slot_row
 
 
-def pieces_rows(parts):
-    if len(parts) == 1:
-        return parts[0][0:512, :], parts[0][512:528, :].astype(F32)
-    rows = parts[0].shape[0]
-    return (
-        jnp.concatenate([parts[0][...], parts[1][0 : 512 - rows, :]], axis=0),
-        parts[1][512 - rows : 528 - rows, :].astype(F32),
-    )
-
-
-def pick_grad_kernel(split, me_ref, *refs):
-    count = 2 * split
-    rows_ref, slots_ref, columns_ref = refs[count:]
-    for block in range(2):
-        tokens, packed = pieces_rows(refs[block * split : block * split + split])
-        slots = own_rows(me_ref[0], packed)
+def block_plan(partners, height):
+    return tuple(
+        (partners.index(partner), first, min(rows, 528 - first))
+        for partner, first, rows in plan_of(height)
+        if partner in partners
+    )
+
+
+def start_blocks(plan, sources, target, sems):
+    copies = []
+    for number, (place, first, rows) in enumerate(plan):
+        copies.append(
+            pltpu.make_async_copy(
+                sources[number].at[pl.ds(0, rows)],
+                target.at[place, pl.ds(first, rows)],
+                sems.at[number],
+            )
+        )
+        copies[-1].start()
+    return copies
+
+
+def pick_grad_kernel(plan, blocks, me_ref, *refs):
+    count = len(plan)
+    rows_ref, slots_ref, columns_ref, held, made, sems, out_sems = refs[count:]
+    copies = start_blocks(plan, refs[:count], held, sems)
+    leaving = []
+    for block in range(blocks):
+        for copy, (place, _, _) in zip(copies, plan):
+            if place == block:
+                copy.wait()
+        tokens = held[block, 0:512, :]
+        slots = own_rows(me_ref[0], held[block, 512:528, :].astype(F32))
         for expert in range(4):
             hot = jnp.where(slot_hot(slots[expert]), 1.0, 0.0).astype(BF)
-            rows_ref[block, expert * 144 : expert * 144 + 144, :] = nn(hot, tokens).astype(BF)
+            made[block, expert * 144 : expert * 144 + 144, :] = nn(hot, tokens).astype(BF)
             slots_ref[block, expert : expert + 1, :] = slots[expert]
         columns_ref[block] = stand_up(slots).astype(BF)
-
-
-def pick_grads(me, pieces):
-    split = len(pieces) // 2
+        leaving.append(
+            pltpu.make_async_copy(made.at[block], rows_ref.at[block], out_sems.at[block])
+        )
+        leaving[-1].start()
+    for copy in leaving:
+        copy.wait()
+
+
+def pick_grads(me, partners, pieces):
+    blocks, plan = len(partners), block_plan(partners, 656)
     return pl.pallas_call(
-        functools.partial(pick_grad_kernel, split),
+        functools.partial(pick_grad_kernel, plan, blocks),
         out_shape=(
-            shaped((2, 576, 1024), BF),
-            shaped((2, 4, 512), F32),
-            shaped((2, 512, 128), BF),
+            shaped((blocks, 576, 1024), BF),
+            shaped((blocks, 4, 512), F32),
+            shaped((blocks, 512, 128), BF),
         ),
-        in_specs=[in_smem()] + in_vmem(len(pieces)),
-        out_specs=tuple(in_vmem(3)),
+        in_specs=[in_smem()] + in_hbm(len(pieces)),
+        out_specs=tuple(in_hbm(1) + in_vmem(2)),
+        scratch_shapes=[
+            pltpu.VMEM((blocks, 528, 1024), BF),
+            pltpu.VMEM((blocks, 576, 1024), BF),
+            pltpu.SemaphoreType.DMA((len(pieces),)),
+            pltpu.SemaphoreType.DMA((blocks,)),
+        ],
         compiler_params=params(),
-        cost_estimate=cost(2 * 2 * 576 * 512 * 1024, 5e6),
+        cost_estimate=cost(blocks * 2 * 576 * 512 * 1024, blocks * 2.4e6),
         name="pick_grads",
     )(me, *pieces)
 
 
-def pick_rows_kernel(split, me_ref, slots_ref, *refs):
-    count = 2 * split
-    rows_ref, gate_ref, columns_ref = refs[count:]
-    for block in range(2):
-        tokens, packed = pieces_rows(refs[block * split : block * split + split])
-        gates = own_rows(me_ref[0], packed)
+def pick_rows_kernel(plan, blocks, me_ref, slots_ref, *refs):
+    count = len(plan)
+    rows_ref, gate_ref, columns_ref, held, made, sems, out_sems = refs[count:]
+    copies = start_blocks(plan, refs[:count], held, sems)
+    leaving = []
+    for block in range(blocks):
+        for copy, (place, _, _) in zip(copies, plan):
+            if place == block:
+                copy.wait()
+        tokens = held[block, 0:512, :]
+        gates = own_rows(me_ref[0], held[block, 512:528, :].astype(F32))
         for expert in range(4):
             match = slot_hot(slots_ref[block, expert : expert + 1, :])
             hot = jnp.where(match, 1.0, 0.0).astype(BF)
             rows = slice(expert * 144, expert * 144 + 144)
-            rows_ref[block, rows, :] = nn(hot, tokens).astype(BF)
+            made[block, rows, :] = nn(hot, tokens).astype(BF)
             gate = jnp.sum(jnp.where(match, gates[expert], 0.0), axis=1, keepdims=True)
             gate_ref[block, rows, :] = jnp.broadcast_to(gate, (144, 128)).astype(BF)
         columns_ref[block] = stand_up(gates).astype(BF)
-
-
-def pick_rows(me, slots, pieces):
-    split = len(pieces) // 2
+        leaving.append(
+            pltpu.make_async_copy(made.at[block], rows_ref.at[block], out_sems.at[block])
+        )
+        leaving[-1].start()
+    for copy in leaving:
+        copy.wait()
+
+
+def pick_rows(me, slots, partners, pieces):
+    blocks, plan = len(partners), block_plan(partners, 528)
     return pl.pallas_call(
-        functools.partial(pick_rows_kernel, split),
+        functools.partial(pick_rows_kernel, plan, blocks),
         out_shape=(
-            shaped((2, 576, 1024), BF),
-            shaped((2, 576, 128), BF),
-            shaped((2, 512, 128), BF),
+            shaped((blocks, 576, 1024), BF),
+            shaped((blocks, 576, 128), BF),
+            shaped((blocks, 512, 128), BF),
         ),
-        in_specs=[in_smem()] + in_vmem(1 + len(pieces)),
-        out_specs=tuple(in_vmem(3)),
+        in_specs=[in_smem()] + in_vmem(1) + in_hbm(len(pieces)),
+        out_specs=tuple(in_hbm(1) + in_vmem(2)),
+        scratch_shapes=[
+            pltpu.VMEM((blocks, 528, 1024), BF),
+            pltpu.VMEM((blocks, 576, 1024), BF),
+            pltpu.SemaphoreType.DMA((len(pieces),)),
+            pltpu.SemaphoreType.DMA((blocks,)),
+        ],
         compiler_params=params(),
-        cost_estimate=cost(2 * 2 * 576 * 512 * 1024, 5e6),
+        cost_estimate=cost(blocks * 2 * 576 * 512 * 1024, blocks * 2.4e6),
         name="pick_rows",
     )(me, slots, *pieces)
 
 
 def expert_kernel(base, me_ref, *refs):
-    rows_refs, grads_refs, gate_refs = refs[0:4], refs[4:8], refs[8:12]
-    gate_w, up_w, down_w = (ref[0] for ref in refs[12:15])
-    out_ref, in_grad_ref, mark_ref, gate_grad_ref, up_grad_ref, down_grad_ref = refs[15:21]
-    lin_grads, inners, out_grads, inputs = refs[21:25]
+    rows_refs, grads_refs, gate_refs = refs[0:2], refs[2:4], refs[4:6]
+    gate_w, up_w, down_w = (ref[0] for ref in refs[6:9])
+    out_ref, in_grad_ref, mark_ref, grad_ref = refs[9:13]
+    lin_grads, inners, out_grads, inputs = refs[13:17]
     expert = me_ref[0] * 4 + base + pl.program_id(0)
     for part in range(2):
         at = slice(part * 576, part * 576 + 576)
 
         def both(pair):
+            if part == 0:
+                return pair[0][0:4].reshape(576, -1)
             return jnp.concatenate(
-                [pair[2 * part + side][...].reshape(288, -1) for side in range(2)], axis=0
+                [pair[0][4:6].reshape(288, -1), pair[1][...].reshape(288, -1)], axis=0
             )
 
         rows, grads, gate = both(rows_refs), both(grads_refs), both(gate_refs)
@@ -1038,15 +1099,17 @@
         in_grad_ref[part * 4 : part * 4 + 4] = (
             (nt(gate_lin_grad, gate_w) + nt(up_lin_grad, up_w)).astype(BF).reshape(4, 144, 1024)
         )
-    down_grad_ref[0] = tn(inners[...], out_grads[...]).astype(BF)
-    gate_grad_ref[0] = tn(inputs[...], lin_grads[:, 0:512]).astype(BF)
-    up_grad_ref[0] = tn(inputs[...], lin_grads[:, 512:1024]).astype(BF)
+    down_grad = tn(inners[...], out_grads[...]).astype(BF)
+    grad_ref[2048:2560, :] = down_grad[:, 0:512]
+    grad_ref[2560:3072, :] = down_grad[:, 512:1024]
+    grad_ref[0:1024, :] = tn(inputs[...], lin_grads[:, 0:512]).astype(BF)
+    grad_ref[1024:2048, :] = tn(inputs[...], lin_grads[:, 512:1024]).astype(BF)
 
 
 def run_experts(me, base, count, rows, grads, gates, gate_w, up_w, down_w):
     spec = pl.BlockSpec
-    wide = spec((2, 144, 1024), lambda e: (0, base + e, 0))
-    slim = spec((2, 144, 128), lambda e: (0, base + e, 0))
+    wide = [spec((blocks, 144, 1024), lambda e: (0, base + e, 0)) for blocks in (6, 2)]
+    slim = [spec((blocks, 144, 128), lambda e: (0, base + e, 0)) for blocks in (6, 2)]
     tall_w = spec((1, 1024, 512), lambda e: (base + e, 0, 0))
     flat_w = spec((1, 512, 1024), lambda e: (base + e, 0, 0))
     return pl.pallas_call(
@@ -1055,19 +1118,15 @@
             shaped((8, 144 * count, 1024), BF),
             shaped((8, 144 * count, 1024), BF),
             shaped((8, 144 * count, 128), BF),
-            shaped((count, 1024, 512), BF),
-            shaped((count, 1024, 512), BF),
-            shaped((count, 512, 1024), BF),
+            shaped((3072 * count, 512), BF),
         ),
         grid=(count,),
-        in_specs=[in_smem()] + [wide] * 8 + [slim] * 4 + [tall_w, tall_w, flat_w],
+        in_specs=[in_smem()] + wide * 2 + slim + [tall_w, tall_w, flat_w],
         out_specs=(
             spec((8, 144, 1024), lambda e: (0, e, 0)),
             spec((8, 144, 1024), lambda e: (0, e, 0)),
             spec((8, 144, 128), lambda e: (0, e, 0)),
-            spec((1, 1024, 512), lambda e: (e, 0, 0)),
-            spec((1, 1024, 512), lambda e: (e, 0, 0)),
-            spec((1, 512, 1024), lambda e: (e, 0, 0)),
+            spec((3072, 512), lambda e: (e, 0)),
         ),
         scratch_shapes=[
             pltpu.VMEM((1152, 1024), BF),
@@ -1179,7 +1238,7 @@
 
 
 def back_to_attention(me, sums, hidden, cotangent, payload, gates, extra, pieces):
-    plan = plan_of(128)
+    plan = heads_plan()
     return pl.pallas_call(
         functools.partial(back_kernel, plan),
         out_shape=(
@@ -1308,8 +1367,40 @@
     return parts.transpose(0, 1, 3, 2, 4).reshape(rows, columns)
 
 
-def sum_copies(values):
-    return lax.psum(values, "sp")
+class Copies:
+    def __init__(self, seq):
+        self.outer = (seq == 0) | (seq == 3)
+        self.waiting = []
+        self.flying = []
+        self.sums = []
+
+    def add(self, value):
+        self.waiting.append(value)
+
+    def step(self, gate):
+        arrived, self.flying = self.flying, []
+        fresh, self.waiting = self.waiting[:1], self.waiting[1:]
+        gate, received, fresh = lax.optimization_barrier(
+            (gate, [item[2] for item in arrived], fresh)
+        )
+        ready = []
+        for (phase, value, _), got in zip(arrived, received):
+            if phase == 2:
+                self.sums.append(jnp.where(self.outer, got, value))
+            else:
+                ready.append((phase + 1, add_low(value, got)))
+        ready += [(0, value) for value in fresh]
+        for phase, value in ready:
+            pairs = (((0, 1), (3, 2)), ((1, 2), (2, 1)), ((1, 0), (2, 3)))[phase]
+            self.flying.append((phase, value, lax.ppermute(value, "sp", pairs)))
+        return gate
+
+
+def sum_line(value, seq):
+    outer = (seq == 0) | (seq == 3)
+    value = add_low(value, lax.ppermute(value, "sp", ((0, 1), (3, 2))))
+    value = add_low(value, lax.ppermute(value, "sp", ((1, 2), (2, 1))))
+    return jnp.where(outer, lax.ppermute(value, "sp", ((1, 0), (2, 3))), value)
 
 
 def fast_local(
@@ -1332,6 +1423,12 @@
     shard = jnp.concatenate([swap_middle(query_weight), key_weight, value_weight, small], axis=1)
     project_pieces = spread(shard)
 
+    slots, routed = dense_slots(expert_routes, drop_rank, 32)
+    mixture_grad = (branch_scale * output_grad.astype(F32)).astype(BF)
+    grad_payload = jnp.concatenate(
+        [mixture_grad, jnp.concatenate([slots[:16], slots[16:]], axis=1), out_weight], axis=0
+    )
+
     block_start = fsdp * 2048
     position_all = doc_position(documents)
     position_span = lax.dynamic_slice_in_dim(position_all, block_start, 2048)
@@ -1345,60 +1442,74 @@
     low_block = start_rows[:, 0, 0] // KB
 
     query, pair, extra = project(me, tokens, cosine, sine, project_pieces)
+    grad_payload = hold(grad_payload, project_pieces[6], project_pieces[7])
+    own, beside = grad_payload, flip(grad_payload, 1)
+    along_x, along_y = flip(grad_payload, 2), flip(grad_payload, 4)
     pair_heads = lax.all_to_all(
         pair.reshape(2048, 256), "sp", split_axis=0, concat_axis=0, tiled=True
     )
+    pair_heads, query, beside, along_x, along_y = lax.optimization_barrier(
+        (pair_heads, query, beside, along_x, along_y)
+    )
     query_heads = lax.all_to_all(
         query.reshape(2048, 256), "sp", split_axis=0, concat_axis=0, tiled=True
     )
     halo = from_behind(pair_heads, "fsdp", 1)
-
-    slots, routed = dense_slots(expert_routes, drop_rank, 32)
-    mixture_grad = (branch_scale * output_grad.astype(F32)).astype(BF)
-    grad_payload = jnp.concatenate(
-        [mixture_grad, jnp.concatenate([slots[:16], slots[16:]], axis=1)], axis=0
-    )
-    grad_pieces = spread(grad_payload)
-    out_pieces = spread(out_weight)
-
+    near_pieces = (own, beside, along_x, flip(along_x, 1), along_y, flip(along_y, 1))
+    diagonal = spread_diagonal(near_pieces)
+    query_heads, halo, near_pieces, diagonal = lax.optimization_barrier(
+        (query_heads, halo, near_pieces, diagonal)
+    )
+    near, far = (0, 1, 2, 3, 4, 5), (6, 7)
     blended, logs = attend(low_block, query_heads, pair_heads, halo, start_rows)
     attended = lax.all_to_all(blended, "sp", split_axis=0, concat_axis=0, tiled=True).reshape(
         4, 512, 256
     )
+    far_pieces = spread_far(diagonal)
+    near_grads = pick_grads(me, near, near_pieces)
+    far_grads = pick_grads(me, far, far_pieces)
+    attended, near_grads, far_grads = lax.optimization_barrier((attended, near_grads, far_grads))
+    grad_rows, slot_rows, slot_columns = zip(near_grads, far_grads)
+    grad_pieces = near_pieces + far_pieces
+    out_pieces = [
+        piece
+        for piece, (_, first, rows) in zip(grad_pieces, plan_of(656))
+        if first + rows == 656
+    ]
     hidden_one, payload, gates = after_attention(
         me, tokens, attended, extra, routed, out_pieces
     )
-    row_pieces = spread(payload)
-
-    groups = ((0, 2), (2, 4), (4, 6), (6, 10))
-    grad_rows, slot_rows, slot_columns = zip(
-        *[pick_grads(me, grad_pieces[first:last]) for first, last in groups]
-    )
-    rows, slot_gates, gate_columns = zip(
-        *[
-            pick_rows(me, slot_rows[number], row_pieces[first:last])
-            for number, (first, last) in enumerate(groups)
-        ]
-    )
+    near_pieces = spread_near(payload)
+    diagonal = spread_diagonal(near_pieces)
+    near_rows = pick_rows(me, slot_rows[0], near, near_pieces)
+    near_rows, diagonal = lax.optimization_barrier((near_rows, diagonal))
+    far_rows = pick_rows(me, slot_rows[1], far, spread_far(diagonal))
+    rows, slot_gates, gate_columns = zip(near_rows, far_rows)
     slot_columns = jnp.concatenate(slot_columns, axis=0)
     gate_columns = jnp.concatenate(gate_columns, axis=0)
-    per_call = 2
-    results = [
-        run_experts(
-            me, base, per_call, rows, grad_rows, slot_gates, gate_weight, up_weight, down_weight
-        )
-        for base in range(0, 4, per_call)
-    ]
-    outs, in_grads, marks, gate_grads, up_grads, down_grads = zip(*results)
+    copies = Copies(seq)
+    results, here = [], me
+    for expert in range(4):
+        results.append(
+            run_experts(
+                here, expert, 1, rows, grad_rows, slot_gates, gate_weight, up_weight, down_weight
+            )
+        )
+        copies.add(results[-1][3])
+        if expert == 0:
+            here = copies.step(me)
+    outs, in_grads, marks, _ = zip(*results)
+    in_grads = copies.step(in_grads)
     odd = combine(1, slot_columns, None, in_grads, marks)
     even = combine(0, slot_columns, None, in_grads, marks)
-    sums = collect(odd, even)
+    sums = collect(odd, even, copies.step)
     hidden_grad, branch_grad, attended_grad, small_grads = back_to_attention(
         me, sums, hidden_one, output_grad, payload, gates, extra, out_pieces
     )
     grad_heads = lax.all_to_all(
         attended_grad.reshape(2048, 256), "sp", split_axis=0, concat_axis=0, tiled=True
     )
+    grad_heads = copies.step(grad_heads)
     odd_mix = combine(1, slot_columns, gate_columns, outs, ())
     even_mix = combine(0, slot_columns, gate_columns, outs, ())
     mixture = collect(odd_mix, even_mix)
@@ -1412,6 +1523,7 @@
     query_back, own_back, halo_back = attend_back(
         low_block, query_heads, pair_heads, halo, start_rows, blended, grad_heads, logs
     )
+    query_back, own_back, halo_back = copies.step((query_back, own_back, halo_back))
     pair_back = (own_back + from_behind(halo_back, "fsdp", -1).astype(F32)).astype(BF)
     query_grad = lax.all_to_all(
         query_back, "sp", split_axis=0, concat_axis=0, tiled=True
@@ -1419,6 +1531,7 @@
     pair_grad = lax.all_to_all(
         pair_back, "sp", split_axis=0, concat_axis=0, tiled=True
     ).reshape(4, 512, 256)
+    query_grad, pair_grad = copies.step((query_grad, pair_grad))
     input_grad, odd_in, even_in = input_grads(
         me, tokens, cosine, sine, query_grad, pair_grad, extra, hidden_grad, project_pieces
     )
@@ -1426,9 +1539,20 @@
 
     out_shard = sum(term.astype(F32) for term in out_sums).astype(BF)
     in_shard = sum(term.astype(F32) for term in in_sums).astype(BF)
-    out_shard, in_shard = sum_copies((out_shard, in_shard))
-    expert_sums = sum_copies((gate_grads, up_grads, down_grads))
-    stacked = [jnp.concatenate(list(parts), axis=0).astype(F32) for parts in expert_sums]
+    shards = sum_line(jnp.concatenate([in_shard, out_shard], axis=1), seq)
+    in_shard, out_shard = shards[:, 0:2176], shards[:, 2176:3328]
+    while copies.flying:
+        copies.step(())
+    stacked = [
+        jnp.stack([total[0:1024] for total in copies.sums]).astype(F32),
+        jnp.stack([total[1024:2048] for total in copies.sums]).astype(F32),
+        jnp.stack(
+            [
+                jnp.concatenate([total[2048:2560], total[2560:3072]], axis=1)
+                for total in copies.sums
+            ]
+        ).astype(F32),
+    ]
     return (
         output,
         input_grad,

time: 1080 us -> 890 us (0.82)
  waiting for transfers between devices: 595 us -> 384 us
  other arithmetic: 53.6 us -> 110 us
  blocking collectives: 28.7 us -> 0 us
  starting transfers between devices: 134 us -> 115 us
  between operations: 15.5 us -> 2 us
    psum x1 -> x0, waiting for transfers between devices: 391 us -> none  [sum_copies(): return lax.psum(values, 'sp')]
    ppermute x0 -> x15, waiting for transfers between devices: none -> 148 us  [the longest x12 124 us: step(): self.flying.append((phase, value, lax.ppermute(value, 'sp', pairs)))]
    ppermute x56 -> x47, starting transfers between devices: 109 us -> 32.8 us  [flip(): lax.ppermute(value, 'fsdp', [(place, place ^ bit) for place in range(8)])]
    all_to_all x1, waiting for transfers between devices: 0.01 us -> 62.5 us  [fast_local(): lax.all_to_all(pair_back, 'sp', split_axis=0, concat_axis=0, tiled=True)]
    ppermute x0 -> x15, starting transfers between devices: none -> 46.2 us  [the longest x12 42.6 us: step(): self.flying.append((phase, value, lax.ppermute(value, 'sp', pairs)))]
    convert_element_type x5 -> x15, other arithmetic: 5.65 us -> 45.5 us  [add_low(): return (left.astype(F32) + right.astype(F32)).astype(BF)]
    all_to_all x1 -> x0, blocking collectives: 28.7 us -> none  [fast_local(): lax.all_to_all(attended_grad.reshape(2048, 256), 'sp', split_axis=0, conc...]
    all_to_all x1, waiting for transfers between devices: 26.1 us -> 0.01 us  [fast_local(): lax.all_to_all(pair.reshape(2048, 256), 'sp', split_axis=0, concat_axis=0...]
  transfers between devices with their start and end apart: 64 -> 70, of which waited for: 27 -> 26; matrix products, arithmetic and copies ran while one was open for 4% -> 14% of each run, Pallas kernels for 8% -> 17%
where the time goes in v2:
time: 890 us; the launch traced here: 878 us
  waiting for transfers between devices  384 us (43%)
  Pallas kernels  237 us (27%)
  starting transfers between devices  115 us (13%)
  other arithmetic  110 us (12%)
  local copies, waits for them, and re-layouts  30.1 us (3%)
    ppermute x47, waiting for transfers between devices, flip(): lax.ppermute(value, 'fsdp', [(place, place ^ bit) for place in range(8)])  142 us
    ppermute x12, waiting for transfers between devices, step(): self.flying.append((phase, value, lax.ppermute(value, 'sp', pairs)))  124 us
    pallas_call x4, Pallas kernels, run_experts(): pl.pallas_call(functools.partial(expert_kernel, base), out_shape=(shaped(...  71.3 us
    all_to_all x1, waiting for transfers between devices, fast_local(): lax.all_to_all(pair_back, 'sp', split_axis=0, concat_axis=0, tiled=True)  62.5 us
    convert_element_type x15, other arithmetic, add_low(): return (left.astype(F32) + right.astype(F32)).astype(BF)  45.5 us
    ppermute x12, starting transfers between devices, step(): self.flying.append((phase, value, lax.ppermute(value, 'sp', pairs)))  42.6 us
    pallas_call x1, Pallas kernels, attend_back(): pl.pallas_call(attend_back_kernel, out_shape=(shaped((2048, 256), BF), sh...  37.4 us
    pallas_call x4, Pallas kernels, combine(): pl.pallas_call(functools.partial(combine_kernel, calls, weighted), out_sh...  33.9 us
  transfers between devices with their start and end apart: 70, of which 26 were waited for; matrix products, arithmetic and copies ran while one was open for 14% of the time, Pallas kernels for 17%

profile of v2, /device:TPU:0, one launch (start us, length us, event | category | flops | bytes accessed | tf_op | source)
XLA Modules:
  0.0 877.8 jit_solution(935288538763391422)
XLA Ops:
  37.8 8.2 project.1
  54.5 28.7 %collective-permute-done.10.refs_2_ = bf16[656,1024]{1,0:T(8,128)(2,1)S(1)} collective-permute-done((bf16[656,1024]{1,0:T(8,128)(2,1)S(1)}, bf16[656,1024]{1,0:T(8,128)(2,1)S(1)}, u32[]{:S(2)}, u32[]{:S(2)}) %collective-permute-start.10) | collective-permute-done | bytes 1343520 | tf_op jit(solution)/shard_map/ppermute | solution.py:511
  97.5 23.2 %collective-permute-done.16.refs_1_.refs_6_ = bf16[320,1024]{1,0:T(8,128)(2,1)S(1)} collective-permute-done((bf16[320,1024]{1,0:T(8,128)(2,1)S(1)}, bf16[320,1024]{1,0:T(8,128)(2,1)S(1)}, u32[]{:S(2)}, u32[]{:S(2)}) %collective-permute-start.16) | collective-permute-done | bytes 655392 | tf_op jit(solution)/shard_map/ppermute | solution.py:511
  120.8 27.7 %attend.1 = (bf16[2048,256]{1,0:T(8,128)(2,1)}, f32[8,2048]{1,0:T(8,128)}) custom-call(s32[4]{0:T(128)} %and_select_fusion.1.low_ref, bf16[2048,256]{1,0:T(8,128)(2,1)} %bitcast.14.query_ref, bf16[2048,256]{1,0:T(8,128)(2,1)} %bitcast.13.own_ref, bf16[2048,256]{1,0:T(8,128)(2,1)} %collective-permute-done.12.halo_ref, s32[4,1,512]{2,1,0:T(1,128)} %bitcast.161), custom_call_target="tpu_custom_call" | custom-call | flops 3124999936 | bytes 750000 | tf_op jit(solution)/shard_map/attend/pallas_call | solution.py:736
  189.2 24.7 %collective-permute-done.20.refs_2_ = bf16[528,1024]{1,0:T(8,128)(2,1)S(1)} collective-permute-done((bf16[528,1024]{1,0:T(8,128)(2,1)}, bf16[528,1024]{1,0:T(8,128)(2,1)S(1)}, u32[]{:S(2)}, u32[]{:S(2)}) %collective-permute-start.20) | collective-permute-done | bytes 1081376 | tf_op jit(solution)/shard_map/ppermute | solution.py:511
  219.0 9.7 %pick_rows.2 = (bf16[6,576,1024]{2,1,0:T(8,128)(2,1)}, bf16[6,576,128]{2,1,0:T(8,128)(2,1)}, bf16[6,512,128]{2,1,0:T(8,128)(2,1)}) custom-call(s32[1]{0:T(128)} %bitcast.me_ref, f32[6,4,512]{2,1,0:T(4,128)} %get-tuple-element.146.slots_ref, bf16[528,1024]{1,0:T(8,128)(2,1)} %get-tuple-element.147.refs_0_.payload_ref, bf16[528,1024]{1,0:T(8,128)(2,1)} %copy-done.28, ...), custom_call_target="tpu_custom_call" | custom-call | flops 452984832 | bytes 1800000 | tf_op jit(solution)/shard_map/pick_rows/pallas_call | solution.py:1037
  241.8 17.6 %experts.4 = (bf16[8,144,1024]{2,1,0:T(8,128)(2,1)}, bf16[8,144,1024]{2,1,0:T(8,128)(2,1)}, bf16[8,144,128]{2,1,0:T(8,128)(2,1)}, bf16[3072,512]{1,0:T(8,128)(2,1)}) custom-call(s32[1]{0:T(128)} %bitcast.me_ref, bf16[6,576,1024]{2,1,0:T(8,128)(2,1)} %get-tuple-element.156.refs_0_, bf16[2,576,1024]{2,1,0:T(8,128)(2,1)} %get-tuple-element.157.refs_1_, ...), custom_call_target="tpu_custom_call" | custom-call | flops 1375000064 | bytes 1875000 | tf_op jit(solution)/shard_map/experts/pallas_call | solution.py:1115
  262.7 17.9 %experts.5 = (bf16[8,144,1024]{2,1,0:T(8,128)(2,1)}, bf16[8,144,1024]{2,1,0:T(8,128)(2,1)}, bf16[8,144,128]{2,1,0:T(8,128)(2,1)}, bf16[3072,512]{1,0:T(8,128)(2,1)}) custom-call(s32[1]{0:T(128)} %bitcast.me_ref, bf16[6,576,1024]{2,1,0:T(8,128)(2,1)} %get-tuple-element.156.refs_0_, bf16[2,576,1024]{2,1,0:T(8,128)(2,1)} %get-tuple-element.157.refs_1_, ...), custom_call_target="tpu_custom_call" | custom-call | flops 1375000064 | bytes 1875000 | tf_op jit(solution)/shard_map/experts/pallas_call | solution.py:1115
  280.6 17.7 %experts.6 = (bf16[8,144,1024]{2,1,0:T(8,128)(2,1)}, bf16[8,144,1024]{2,1,0:T(8,128)(2,1)}, bf16[8,144,128]{2,1,0:T(8,128)(2,1)}, bf16[3072,512]{1,0:T(8,128)(2,1)}) custom-call(s32[1]{0:T(128)} %bitcast.me_ref, bf16[6,576,1024]{2,1,0:T(8,128)(2,1)} %get-tuple-element.156.refs_0_, bf16[2,576,1024]{2,1,0:T(8,128)(2,1)} %get-tuple-element.157.refs_1_, ...), custom_call_target="tpu_custom_call" | custom-call | flops 1375000064 | bytes 1875000 | tf_op jit(solution)/shard_map/experts/pallas_call | solution.py:1115
  298.3 18.0 %experts.7 = (bf16[8,144,1024]{2,1,0:T(8,128)(2,1)}, bf16[8,144,1024]{2,1,0:T(8,128)(2,1)}, bf16[8,144,128]{2,1,0:T(8,128)(2,1)}, bf16[3072,512]{1,0:T(8,128)(2,1)}) custom-call(s32[1]{0:T(128)} %bitcast.me_ref, bf16[6,576,1024]{2,1,0:T(8,128)(2,1)} %get-tuple-element.156.refs_0_, bf16[2,576,1024]{2,1,0:T(8,128)(2,1)} %get-tuple-element.157.refs_1_, ...), custom_call_target="tpu_custom_call" | custom-call | flops 1375000064 | bytes 1875000 | tf_op jit(solution)/shard_map/experts/pallas_call | solution.py:1115
  316.3 12.8 %collective-permute-done.33 = bf16[3072,512]{1,0:T(8,128)(2,1)} collective-permute-done((bf16[3072,512]{1,0:T(8,128)(2,1)}, bf16[3072,512]{1,0:T(8,128)(2,1)}, u32[]{:S(2)}, u32[]{:S(2)}) %collective-permute-start.33) | collective-permute-done | bytes 3145760 | tf_op jit(solution)/shard_map/ppermute | solution.py:1395
  329.1 8.9 %combine.7 = bf16[4,528,1024]{2,1,0:T(8,128)(2,1)} custom-call(bf16[8,512,128]{2,1,0:T(8,128)(2,1)} %copy-done, bf16[8,144,1024]{2,1,0:T(8,128)(2,1)} %get-tuple-element.174.refs_1_, bf16[8,144,1024]{2,1,0:T(8,128)(2,1)} %get-tuple-element.175.refs_2_, bf16[8,144,1024]{2,1,0:T(8,128)(2,1)} %get-tuple-element.176.refs_3_, ...), custom_call_target="tpu_custom_call" | custom-call | flops 402653184 | bytes 1250000 | tf_op jit(solution)/shard_map/combine/pallas_call | solution.py:1189
  360.7 8.9 %combine.6 = bf16[4,528,1024]{2,1,0:T(8,128)(2,1)} custom-call(bf16[8,512,128]{2,1,0:T(8,128)(2,1)} %copy-done, bf16[8,144,1024]{2,1,0:T(8,128)(2,1)} %get-tuple-element.174.refs_1_, bf16[8,144,1024]{2,1,0:T(8,128)(2,1)} %get-tuple-element.175.refs_2_, bf16[8,144,1024]{2,1,0:T(8,128)(2,1)} %get-tuple-element.176.refs_3_, ...), custom_call_target="tpu_custom_call" | custom-call | flops 402653184 | bytes 1250000 | tf_op jit(solution)/shard_map/combine/pallas_call | solution.py:1189
  378.7 38.4 %collective-permute-done.38 = bf16[3072,512]{1,0:T(8,128)(2,1)} collective-permute-done((bf16[3072,512]{1,0:T(8,128)(2,1)}, bf16[3072,512]{1,0:T(8,128)(2,1)}, u32[]{:S(2)}, u32[]{:S(2)}) %collective-permute-start.38) | collective-permute-done | bytes 3145760 | tf_op jit(solution)/shard_map/ppermute | solution.py:1395
  429.6 8.8 %collective-permute-start.43 = (bf16[3072,512]{1,0:T(8,128)(2,1)}, bf16[3072,512]{1,0:T(8,128)(2,1)}, u32[]{:S(2)}, u32[]{:S(2)}) collective-permute-start(bf16[3072,512]{1,0:T(8,128)(2,1)} %get-tuple-element.191), channel_id=1, source_target_pairs={{0,8},{24,16},{1,9},{25,17},{2,10},{26,18},{3,11},{27,19},{4,12},{... | collective-permute-start | bytes 9437192 | tf_op jit(solution)/shard_map/ppermute | solution.py:1395
  442.9 24.0 %collective-permute-done.40.sum_y_ref = bf16[528,1024]{1,0:T(8,128)(2,1)} collective-permute-done((bf16[528,1024]{1,0:T(8,128)(2,1)S(1)}, bf16[528,1024]{1,0:T(8,128)(2,1)}, u32[]{:S(2)}, u32[]{:S(2)}) %collective-permute-start.40) | collective-permute-done | bytes 1081376 | tf_op jit(solution)/shard_map/ppermute | solution.py:511
  501.9 22.6 %all-to-all-done.3 = bf16[4,512,256]{2,1,0:T(8,128)(2,1)} async-done(((bf16[4,512,256]{2,1,0:T(8,128)(2,1)}), bf16[4,512,256]{2,1,0:T(8,128)(2,1)}, u32[]{:S(2)}, u32[]{:S(2)}) %all-to-all-start.3) | async-done | bytes 1048608 | tf_op jit(solution)/shard_map/all_to_all | solution.py:1509
  539.3 8.9 %collective-permute-start.46 = (bf16[3072,512]{1,0:T(8,128)(2,1)}, bf16[3072,512]{1,0:T(8,128)(2,1)}, u32[]{:S(2)}, u32[]{:S(2)}) collective-permute-start(bf16[3072,512]{1,0:T(8,128)(2,1)} %get-tuple-element.200), channel_id=1, source_target_pairs={{0,8},{24,16},{1,9},{25,17},{2,10},{26,18},{3,11},{27,19},{4,12},{... | collective-permute-start | bytes 9437192 | tf_op jit(solution)/shard_map/ppermute | solution.py:1395
  559.3 37.4 %attend_back.1 = (bf16[2048,256]{1,0:T(8,128)(2,1)}, f32[2048,256]{1,0:T(8,128)}, bf16[2048,256]{1,0:T(8,128)(2,1)}) custom-call(s32[4]{0:T(128)} %and_select_fusion.1.low_ref, bf16[2048,256]{1,0:T(8,128)(2,1)} %bitcast.14.query_ref, bf16[2048,256]{1,0:T(8,128)(2,1)} %bitcast.13.own_ref, bf16[2048,256]{1,0:T(8,128)(2,1)} %collective-permute-done.12.halo_ref, ...), custom_call_target="tpu_custom_call" | custom-call | flops 7500000256 | bytes 1250000 | tf_op jit(solution)/shard_map/attend_back/pallas_call | solution.py:841
  600.4 11.4 %collective-permute-done.46 = bf16[3072,512]{1,0:T(8,128)(2,1)} collective-permute-done((bf16[3072,512]{1,0:T(8,128)(2,1)}, bf16[3072,512]{1,0:T(8,128)(2,1)}, u32[]{:S(2)}, u32[]{:S(2)}) %collective-permute-start.46) | collective-permute-done | bytes 3145760 | tf_op jit(solution)/shard_map/ppermute | solution.py:1395
  667.3 62.5 %all-to-all-done.5.pair_grad_ref = bf16[4,512,256]{2,1,0:T(8,128)(2,1)} async-done(((bf16[4,512,256]{2,1,0:T(8,128)(2,1)}), bf16[4,512,256]{2,1,0:T(8,128)(2,1)}, u32[]{:S(2)}, u32[]{:S(2)}) %all-to-all-start.5) | async-done | bytes 1048608 | tf_op jit(solution)/shard_map/all_to_all | solution.py:1531
  729.9 12.6 %input_grads.1 = (bf16[512,1024]{1,0:T(8,128)(2,1)}, bf16[4,128,2176]{2,1,0:T(8,128)(2,1)}, bf16[4,128,2176]{2,1,0:T(8,128)(2,1)}) custom-call(s32[1]{0:T(128)} %bitcast.me_ref, bf16[512,1024]{1,0:T(8,128)(2,1)} %tokens_ref.5, f32[512,128]{1,0:T(8,128)} %copy.64.cos_ref, f32[512,128]{1,0:T(8,128)} %broadcast_multiply_fusion.sin_ref, ...), custom_call_target="tpu_custom_call" | custom-call | flops 536870912 | bytes 1875000 | tf_op jit(solution)/shard_map/input_grads/pallas_call | solution.py:1334
  777.1 57.3 %collective-permute-done.63 = bf16[3072,512]{1,0:T(8,128)(2,1)S(1)} collective-permute-done((bf16[3072,512]{1,0:T(8,128)(2,1)S(1)}, bf16[3072,512]{1,0:T(8,128)(2,1)S(1)}, u32[]{:S(2)}, u32[]{:S(2)}) %collective-permute-start.63) | collective-permute-done | bytes 3145760 | tf_op jit(solution)/shard_map/ppermute | solution.py:1395
  848.2 24.9 %collective-permute-done.62 = bf16[128,3328]{1,0:T(8,128)(2,1)S(1)} collective-permute-done((bf16[128,3328]{1,0:T(8,128)(2,1)S(1)}, bf16[128,3328]{1,0:T(8,128)(2,1)S(1)}, u32[]{:S(2)}, u32[]{:S(2)}) %collective-permute-start.62) | collective-permute-done | bytes 852000 | tf_op jit(solution)/shard_map/ppermute | solution.py:1403
  (352 shorter events, 343.0 us)
Async XLA Ops:
  46.1 38.3 %all-to-all-start = ((bf16[4,512,256]{2,1,0:T(8,128)(2,1)}), bf16[4,512,256]{2,1,0:T(8,128)(2,1)}, u32[]{:S(2)}, u32[]{:S(2)}) async-start(bf16[4,512,256]{2,1,0:T(8,128)(2,1)} %get-tuple-element.116), calls=%async_computation | async-start | bytes 2097152 | tf_op jit(solution)/shard_map/all_to_all | solution.py:1448
  259.4 69.7 %collective-permute-start.33 = (bf16[3072,512]{1,0:T(8,128)(2,1)}, bf16[3072,512]{1,0:T(8,128)(2,1)}, u32[]{:S(2)}, u32[]{:S(2)}) collective-permute-start(bf16[3072,512]{1,0:T(8,128)(2,1)} %get-tuple-element.172), channel_id=1, source_target_pairs={{0,8},{24,16},{1,9},{25,17},{2,10},{26,18},{3,11},{27,19},{4,12},{... | collective-permute-start | bytes 9437192 | tf_op jit(solution)/shard_map/ppermute | solution.py:1395
  341.9 36.8 %collective-permute-start.37 = (bf16[3072,512]{1,0:T(8,128)(2,1)S(1)}, bf16[3072,512]{1,0:T(8,128)(2,1)}, u32[]{:S(2)}, u32[]{:S(2)}) collective-permute-start(bf16[3072,512]{1,0:T(8,128)(2,1)S(1)} %add_convert_fusion.7), channel_id=1, source_target_pairs={{8,16},{16,8},{9,17},{17,9},{10,18},{18,10},{11,19},{19,11},{12,20... | collective-permute-start | bytes 9437192 | tf_op jit(solution)/shard_map/ppermute | solution.py:1395
  344.5 72.5 %collective-permute-start.38 = (bf16[3072,512]{1,0:T(8,128)(2,1)}, bf16[3072,512]{1,0:T(8,128)(2,1)}, u32[]{:S(2)}, u32[]{:S(2)}) collective-permute-start(bf16[3072,512]{1,0:T(8,128)(2,1)} %get-tuple-element.183), channel_id=1, source_target_pairs={{0,8},{24,16},{1,9},{25,17},{2,10},{26,18},{3,11},{27,19},{4,12},{... | collective-permute-start | bytes 9437192 | tf_op jit(solution)/shard_map/ppermute | solution.py:1395
  360.7 126.4 %collective-permute-start.28 = (bf16[4,512,1024]{2,1,0:T(8,128)(2,1)}, bf16[4,512,1024]{2,1,0:T(8,128)(2,1)}, u32[]{:S(2)}, u32[]{:S(2)}) collective-permute-start(bf16[4,512,1024]{2,1,0:T(8,128)(2,1)} %combine.5), channel_id=1, source_target_pairs={{0,1},{1,0},{2,3},{3,2},{4,5},{5,4},{6,7},{7,6},{8,9},{9,8},{10,11... | collective-permute-start | bytes 12582920 | tf_op jit(solution)/shard_map/ppermute | solution.py:511
  371.0 46.0 %collective-permute-start.35 = (bf16[272,1024]{1,0:T(8,128)(2,1)S(1)}, bf16[272,1024]{1,0:T(8,128)(2,1)S(1)}, u32[]{:S(2)}, u32[]{:S(2)}) collective-permute-start(bf16[272,1024]{1,0:T(8,128)(2,1)S(1)} %fusion.18), channel_id=1, source_target_pairs={{0,2},{1,3},{2,0},{3,1},{4,6},{5,7},{6,4},{7,5},{8,10},{9,11},{10,... | collective-permute-start | bytes 1671176 | tf_op jit(solution)/shard_map/ppermute | solution.py:511
  372.8 44.2 %collective-permute-start.36 = (bf16[256,1024]{1,0:T(8,128)(2,1)S(1)}, bf16[256,1024]{1,0:T(8,128)(2,1)S(1)}, u32[]{:S(2)}, u32[]{:S(2)}) collective-permute-start(bf16[256,1024]{1,0:T(8,128)(2,1)S(1)} %fusion.27), channel_id=1, source_target_pairs={{0,4},{1,5},{2,6},{3,7},{4,0},{5,1},{6,2},{7,3},{8,12},{9,13},{10,... | collective-permute-start | bytes 1572872 | tf_op jit(solution)/shard_map/ppermute | solution.py:511
  420.5 81.4 %collective-permute-start.41 = (bf16[3072,512]{1,0:T(8,128)(2,1)S(1)}, bf16[3072,512]{1,0:T(8,128)(2,1)}, u32[]{:S(2)}, u32[]{:S(2)}) collective-permute-start(bf16[3072,512]{1,0:T(8,128)(2,1)S(1)} %add_convert_fusion.6), channel_id=1, source_target_pairs={{8,0},{16,24},{9,1},{17,25},{10,2},{18,26},{11,3},{19,27},{12,4},{... | collective-permute-start | bytes 9437192 | tf_op jit(solution)/shard_map/ppermute | solution.py:1395
  427.2 97.3 %collective-permute-start.42 = (bf16[3072,512]{1,0:T(8,128)(2,1)}, bf16[3072,512]{1,0:T(8,128)(2,1)}, u32[]{:S(2)}, u32[]{:S(2)}) collective-permute-start(bf16[3072,512]{1,0:T(8,128)(2,1)} %add_convert_fusion.5), channel_id=1, source_target_pairs={{8,16},{16,8},{9,17},{17,9},{10,18},{18,10},{11,19},{19,11},{12,20... | collective-permute-start | bytes 9437192 | tf_op jit(solution)/shard_map/ppermute | solution.py:1395
  429.6 95.0 %collective-permute-start.43 = (bf16[3072,512]{1,0:T(8,128)(2,1)}, bf16[3072,512]{1,0:T(8,128)(2,1)}, u32[]{:S(2)}, u32[]{:S(2)}) collective-permute-start(bf16[3072,512]{1,0:T(8,128)(2,1)} %get-tuple-element.191), channel_id=1, source_target_pairs={{0,8},{24,16},{1,9},{25,17},{2,10},{26,18},{3,11},{27,19},{4,12},{... | collective-permute-start | bytes 9437192 | tf_op jit(solution)/shard_map/ppermute | solution.py:1395
  474.2 50.4 %all-to-all-start.3 = ((bf16[4,512,256]{2,1,0:T(8,128)(2,1)}), bf16[4,512,256]{2,1,0:T(8,128)(2,1)}, u32[]{:S(2)}, u32[]{:S(2)}) async-start(bf16[4,512,256]{2,1,0:T(8,128)(2,1)} %get-tuple-element.188), calls=%async_computation.3 | async-start | bytes 2097152 | tf_op jit(solution)/shard_map/all_to_all | solution.py:1509
  490.0 49.3 %collective-permute-start.31 = (bf16[256,1024]{1,0:T(8,128)(2,1)}, bf16[256,1024]{1,0:T(8,128)(2,1)}, u32[]{:S(2)}, u32[]{:S(2)}) collective-permute-start(bf16[256,1024]{1,0:T(8,128)(2,1)} %get-tuple-element.264), channel_id=1, source_target_pairs={{0,2},{1,3},{2,0},{3,1},{4,6},{5,7},{6,4},{7,5},{8,10},{9,11},{10,... | collective-permute-start | bytes 1572872 | tf_op jit(solution)/shard_map/ppermute | solution.py:511
  490.4 60.1 %collective-permute-start.29 = (bf16[256,1024]{1,0:T(8,128)(2,1)}, bf16[256,1024]{1,0:T(8,128)(2,1)}, u32[]{:S(2)}, u32[]{:S(2)}) collective-permute-start(bf16[256,1024]{1,0:T(8,128)(2,1)} %get-tuple-element.263), channel_id=1, source_target_pairs={{0,4},{1,5},{2,6},{3,7},{4,0},{5,1},{6,2},{7,3},{8,12},{9,13},{10,... | collective-permute-start | bytes 1572872 | tf_op jit(solution)/shard_map/ppermute | solution.py:511
  501.9 51.3 %collective-permute-start.55 = (bf16[4,128,1152]{2,1,0:T(8,128)(2,1)}, bf16[4,128,1152]{2,1,0:T(8,128)(2,1)}, u32[]{:S(2)}, u32[]{:S(2)}) collective-permute-start(bf16[4,128,1152]{2,1,0:T(8,128)(2,1)} %get-tuple-element.215), channel_id=1, source_target_pairs={{0,1},{1,0},{2,3},{3,2},{4,5},{5,4},{6,7},{7,6},{8,9},{9,8},{10,11... | collective-permute-start | bytes 3538952 | tf_op jit(solution)/shard_map/ppermute | solution.py:511
  529.9 70.4 %collective-permute-start.44 = (bf16[3072,512]{1,0:T(8,128)(2,1)}, bf16[3072,512]{1,0:T(8,128)(2,1)}, u32[]{:S(2)}, u32[]{:S(2)}) collective-permute-start(bf16[3072,512]{1,0:T(8,128)(2,1)} %add_convert_fusion.4), channel_id=1, source_target_pairs={{8,0},{16,24},{9,1},{17,25},{10,2},{18,26},{11,3},{19,27},{12,4},{... | collective-permute-start | bytes 9437192 | tf_op jit(solution)/shard_map/ppermute | solution.py:1395
  536.9 63.5 %collective-permute-start.45 = (bf16[3072,512]{1,0:T(8,128)(2,1)}, bf16[3072,512]{1,0:T(8,128)(2,1)}, u32[]{:S(2)}, u32[]{:S(2)}) collective-permute-start(bf16[3072,512]{1,0:T(8,128)(2,1)} %add_convert_fusion.3), channel_id=1, source_target_pairs={{8,16},{16,8},{9,17},{17,9},{10,18},{18,10},{11,19},{19,11},{12,20... | collective-permute-start | bytes 9437192 | tf_op jit(solution)/shard_map/ppermute | solution.py:1395
  539.3 72.5 %collective-permute-start.46 = (bf16[3072,512]{1,0:T(8,128)(2,1)}, bf16[3072,512]{1,0:T(8,128)(2,1)}, u32[]{:S(2)}, u32[]{:S(2)}) collective-permute-start(bf16[3072,512]{1,0:T(8,128)(2,1)} %get-tuple-element.200), channel_id=1, source_target_pairs={{0,8},{24,16},{1,9},{25,17},{2,10},{26,18},{3,11},{27,19},{4,12},{... | collective-permute-start | bytes 9437192 | tf_op jit(solution)/shard_map/ppermute | solution.py:1395
  550.5 101.6 %collective-permute-start.32 = (bf16[512,1024]{1,0:T(8,128)(2,1)}, bf16[512,1024]{1,0:T(8,128)(2,1)}, u32[]{:S(2)}, u32[]{:S(2)}) collective-permute-start(bf16[512,1024]{1,0:T(8,128)(2,1)} %pad_maximum_fusion.4), channel_id=1, source_target_pairs={{0,4},{1,5},{2,6},{3,7},{4,0},{5,1},{6,2},{7,3},{8,12},{9,13},{10,... | collective-permute-start | bytes 3145736 | tf_op jit(solution)/shard_map/ppermute | solution.py:511
  554.9 78.3 %collective-permute-start.58 = (bf16[64,1152]{1,0:T(8,128)(2,1)}, bf16[64,1152]{1,0:T(8,128)(2,1)}, u32[]{:S(2)}, u32[]{:S(2)}) collective-permute-start(bf16[64,1152]{1,0:T(8,128)(2,1)} %get-tuple-element.288), channel_id=1, source_target_pairs={{0,2},{1,3},{2,0},{3,1},{4,6},{5,7},{6,4},{7,5},{8,10},{9,11},{10,... | collective-permute-start | bytes 442376 | tf_op jit(solution)/shard_map/ppermute | solution.py:511
  622.9 107.0 %collective-permute-start.48 = (bf16[3072,512]{1,0:T(8,128)(2,1)}, bf16[3072,512]{1,0:T(8,128)(2,1)}, u32[]{:S(2)}, u32[]{:S(2)}) collective-permute-start(bf16[3072,512]{1,0:T(8,128)(2,1)} %add_convert_fusion.2), channel_id=1, source_target_pairs={{8,0},{16,24},{9,1},{17,25},{10,2},{18,26},{11,3},{19,27},{12,4},{... | collective-permute-start | bytes 9437192 | tf_op jit(solution)/shard_map/ppermute | solution.py:1395
  629.8 100.0 %collective-permute-start.49 = (bf16[3072,512]{1,0:T(8,128)(2,1)}, bf16[3072,512]{1,0:T(8,128)(2,1)}, u32[]{:S(2)}, u32[]{:S(2)}) collective-permute-start(bf16[3072,512]{1,0:T(8,128)(2,1)} %add_convert_fusion.1), channel_id=1, source_target_pairs={{8,16},{16,8},{9,17},{17,9},{10,18},{18,10},{11,19},{19,11},{12,20... | collective-permute-start | bytes 9437192 | tf_op jit(solution)/shard_map/ppermute | solution.py:1395
  643.8 86.0 %all-to-all-start.5 = ((bf16[4,512,256]{2,1,0:T(8,128)(2,1)}), bf16[4,512,256]{2,1,0:T(8,128)(2,1)}, u32[]{:S(2)}, u32[]{:S(2)}) async-start(bf16[4,512,256]{2,1,0:T(8,128)(2,1)} %bitcast.149), calls=%async_computation.5 | async-start | bytes 2097152 | tf_op jit(solution)/shard_map/all_to_all | solution.py:1531
  763.4 71.0 %collective-permute-start.63 = (bf16[3072,512]{1,0:T(8,128)(2,1)S(1)}, bf16[3072,512]{1,0:T(8,128)(2,1)S(1)}, u32[]{:S(2)}, u32[]{:S(2)}) collective-permute-start(bf16[3072,512]{1,0:T(8,128)(2,1)S(1)} %add_convert_fusion), channel_id=1, source_target_pairs={{8,0},{16,24},{9,1},{17,25},{10,2},{18,26},{11,3},{19,27},{12,4},{... | collective-permute-start | bytes 9437192 | tf_op jit(solution)/shard_map/ppermute | solution.py:1395
  773.1 61.4 %collective-permute-start.60 = (bf16[128,3328]{1,0:T(8,128)(2,1)S(1)}, bf16[128,3328]{1,0:T(8,128)(2,1)S(1)}, u32[]{:S(2)}, u32[]{:S(2)}) collective-permute-start(bf16[128,3328]{1,0:T(8,128)(2,1)S(1)} %pad_maximum_fusion.5), channel_id=1, source_target_pairs={{0,8},{24,16},{1,9},{25,17},{2,10},{26,18},{3,11},{27,19},{4,12},{... | collective-permute-start | bytes 2555912 | tf_op jit(solution)/shard_map/ppermute | solution.py:1401
  (93 other events, 1373.8 us)

commit v3 on v2

--- a/solution.py
+++ b/solution.py
@@ -465,6 +465,7 @@
 LOG2E = 1.4426950408889634
 QB = 512
 KB = 512
+BACK_KB = 256
 HALO = 2048
 VMEM_MOST = 60 * 1024 * 1024
 
@@ -573,39 +574,33 @@
     return (own, flip(for_x, 2), flip(for_y, 4))
 
 
-def heads_plan():
-    return tuple(
-        (partner, 528 - first)
-        for partner, first, rows in plan_of(656)
-        if first + rows == 656
-    )
-
-
 def start_fetch(me, plan, sources, target, block_rows, sems):
     copies = []
     for number, (partner, first, rows) in enumerate(plan):
         start = pl.multiple_of((me ^ partner) * block_rows + first, 64)
         copies.append(
-            pltpu.make_async_copy(sources[number], target.at[pl.ds(start, rows)], sems.at[number])
+            pltpu.make_async_copy(
+                sources[number].at[:, pl.ds(0, 2176)],
+                target.at[pl.ds(start, rows)],
+                sems.at[number],
+            )
         )
         copies[-1].start()
     return copies
 
 
-def start_fetch_heads(me, plan, sources, target, sems):
+def start_fetch_out(me, plan, sources, target, sems):
     copies = []
-    for number, (partner, first) in enumerate(plan):
-        for half in range(2):
-            head = (me ^ partner) * 2 + half
-            head = (head & ~3) | ((head & 1) << 1) | ((head >> 1) & 1)
-            copies.append(
-                pltpu.make_async_copy(
-                    sources[number].at[pl.ds(first + half * HD, HD)],
-                    target.at[pl.ds(pl.multiple_of(head * HD, HD), HD)],
-                    sems.at[len(copies)],
-                )
+    for number, (partner, first, rows) in enumerate(plan):
+        start = pl.multiple_of((me ^ partner) * 128 + first, 64)
+        copies.append(
+            pltpu.make_async_copy(
+                sources[number].at[:, pl.ds(2176, 1024)],
+                target.at[pl.ds(start, rows)],
+                sems.at[number],
             )
-            copies[-1].start()
+        )
+        copies[-1].start()
     return copies
 
 
@@ -617,9 +612,16 @@
     return values * cosine + other * sine
 
 
+def side_by_side(left, right, group):
+    lane = lax.broadcasted_iota(jnp.int32, left.shape, 1)
+    if group == 0:
+        return jnp.where(lane < HD, left, pltpu.roll(right, HD, 1))
+    return jnp.where(lane < HD, pltpu.roll(left, HD, 1), right)
+
+
 def project_kernel(plan, me_ref, tokens_ref, cos_ref, sin_ref, *refs):
     count = len(plan)
-    query_ref, pair_ref, extra_ref, mats, sems = refs[count:]
+    first_ref, second_ref, extra_ref, mats, sems = refs[count:]
     copies = start_fetch(me_ref[0], plan, refs[:count], mats, 128, sems)
     stream = tokens_ref[...].astype(F32)
     scaled = stream * lax.rsqrt(jnp.mean(stream * stream, axis=-1, keepdims=True) + norm_eps)
@@ -631,14 +633,13 @@
     cosine, sine = cos_ref[...], sin_ref[...]
     for part in range(4):
         query = nn(normed, mats[:, part * 256 : part * 256 + 256])
-        for half in range(2):
-            columns = slice(half * 128, half * 128 + 128)
-            query_ref[part, :, columns] = turn(query[:, columns], cosine, sine).astype(BF)
-        key = nn(normed, mats[:, 1024 + part * 128 : 1152 + part * 128])
-        pair_ref[part, :, :128] = turn(key, cosine, sine).astype(BF)
-        pair_ref[part, :, 128:] = nn(
-            normed, mats[:, 1536 + part * 128 : 1664 + part * 128]
-        ).astype(BF)
+        key = turn(nn(normed, mats[:, 1024 + part * 128 : 1152 + part * 128]), cosine, sine)
+        value = nn(normed, mats[:, 1536 + part * 128 : 1664 + part * 128])
+        for group, target in enumerate((first_ref, second_ref)):
+            target[part, :, 0:128] = turn(
+                query[:, group * 128 : group * 128 + 128], cosine, sine
+            ).astype(BF)
+            target[part, :, 128:256] = side_by_side(key, value, group).astype(BF)
 
 
 def project(me, tokens, cosine, sine, pieces):
@@ -659,20 +660,22 @@
     )(me, tokens, cosine, sine, *pieces)
 
 
-def lane_half(values, group):
+def placed(values, half, side):
+    moved = values.astype(F32)
+    if half != side:
+        moved = pltpu.roll(moved, HD, 1)
     lane = lax.broadcasted_iota(jnp.int32, values.shape, 1)
-    return jnp.where((lane < HD) == (group == 0), values, jnp.zeros((), values.dtype))
-
-
-def allowed_pairs(block, step, start):
-    key_at = block * KB + lax.broadcasted_iota(jnp.int32, (KB, QB), 0)
-    query_at = HALO + step * QB + lax.broadcasted_iota(jnp.int32, (KB, QB), 1)
+    return jnp.where((lane < HD) == (side == 0), moved, 0.0).astype(values.dtype)
+
+
+def allowed_pairs(first, rows, step, start):
+    key_at = first + lax.broadcasted_iota(jnp.int32, (rows, QB), 0)
+    query_at = HALO + step * QB + lax.broadcasted_iota(jnp.int32, (rows, QB), 1)
     return (key_at >= start) & (key_at <= query_at)
 
 
 def attend_kernel(
-    low_ref, query_ref, own_ref, halo_ref, start_ref, out_ref, log_ref,
-    keys, values_t, most, total, blend,
+    low_ref, own_ref, halo_ref, start_ref, out_ref, log_ref, pairs, pairs_t, most, total, blend
 ):
     step = pl.program_id(0)
 
@@ -680,73 +683,63 @@
     def _():
         for first in range(0, HALO, 512):
             rows = slice(first, first + 512)
-            keys[first : first + 512, :] = halo_ref[rows, :128]
-            keys[HALO + first : HALO + first + 512, :] = own_ref[rows, :128]
-            values_t[:, first : first + 512] = halo_ref[rows, 128:].astype(F32).T.astype(BF)
-            values_t[:, HALO + first : HALO + first + 512] = (
-                own_ref[rows, 128:].astype(F32).T.astype(BF)
-            )
+            late = slice(HALO + first, HALO + first + 512)
+            pairs[rows, :] = halo_ref[rows, :]
+            pairs[late, :] = own_ref[rows, 128:256]
+            pairs_t[:, rows] = halo_ref[rows, :].astype(F32).T.astype(BF)
+            pairs_t[:, late] = own_ref[rows, 128:256].astype(F32).T.astype(BF)
 
     start = start_ref[0]
-    picks = [
-        lane_half(query_ref[:, half * 128 : half * 128 + 128], group)
-        for half in range(2)
-        for group in range(2)
-    ]
+    query = own_ref[pl.ds(pl.multiple_of(step * QB, QB), QB), 0:128]
+    picks = [placed(query, half, 0) for half in range(2)]
     most[...] = jnp.full(most.shape, masked_score, F32)
     total[...] = jnp.zeros(total.shape, F32)
     blend[...] = jnp.zeros(blend.shape, F32)
 
     def visit(block, carry):
         first = pl.multiple_of(block * KB, KB)
-        allowed = allowed_pairs(block, step, start)
-        key = keys[pl.ds(first, KB), :]
-        for number in range(4):
-            scores = nt(key, picks[number]) * (attend_scale * LOG2E)
-            scores = jnp.where(allowed, scores, masked_score)
-            before = most[number : number + 1, :]
+        allowed = allowed_pairs(first, KB, step, start)
+        pair = pairs[pl.ds(first, KB), :]
+        value = pairs_t[HD:128, pl.ds(first, KB)]
+        raw = [nt(pair, picks[half]) for half in range(2)]
+        for half in range(2):
+            scores = jnp.where(allowed, raw[half] * (attend_scale * LOG2E), masked_score)
+            before = most[half : half + 1, :]
             top = jnp.maximum(before, jnp.max(scores, axis=0, keepdims=True))
             weight = jnp.exp2(scores - top)
             fade = jnp.exp2(before - top)
-            most[number : number + 1, :] = top
-            total[number : number + 1, :] = total[number : number + 1, :] * fade + jnp.sum(
+            most[half : half + 1, :] = top
+            total[half : half + 1, :] = total[half : half + 1, :] * fade + jnp.sum(
                 weight, axis=0, keepdims=True
             )
-            group = number % 2
-            value = values_t[group * HD : group * HD + HD, pl.ds(first, KB)]
-            rows = slice(number * HD, number * HD + HD)
+            rows = slice(half * HD, half * HD + HD)
             blend[rows, :] = blend[rows, :] * fade + nn(value, weight.astype(BF))
         return carry
 
-    lax.fori_loop(low_ref[step], step + HALO // KB + 1, visit, 0)
-    for number in range(4):
-        rows = slice(number * HD, number * HD + HD)
-        blend[rows, :] = blend[rows, :] / total[number : number + 1, :]
+    lax.fori_loop(low_ref[step], (HALO + (step + 1) * QB) // KB, visit, 0)
     for half in range(2):
-        out_ref[:, half * 128 : half * 128 + 128] = (
-            blend[half * 128 : half * 128 + 128, :].T.astype(BF)
-        )
-    log_ref[0:4, :] = most[0:4, :] + jnp.log2(total[0:4, :])
-    log_ref[4:8, :] = jnp.zeros((4, QB), F32)
-
-
-def attend(low_block, query, own, halo, start):
-    steps = query.shape[0] // QB
+        rows = slice(half * HD, half * HD + HD)
+        blend[rows, :] = blend[rows, :] / total[half : half + 1, :]
+    out_ref[...] = blend[...].T.astype(BF)
+    log_ref[0:2, :] = most[0:2, :] + jnp.log2(total[0:2, :])
+    log_ref[2:8, :] = jnp.zeros((6, QB), F32)
+
+
+def attend(low_block, own, halo, start):
     spec = lambda shape, index: pl.BlockSpec(shape, index)
     return pl.pallas_call(
         attend_kernel,
-        out_shape=(shaped((2048, 256), BF), shaped((8, 2048), F32)),
+        out_shape=(shaped((2048, 128), BF), shaped((8, 2048), F32)),
         grid_spec=pltpu.PrefetchScalarGridSpec(
             num_scalar_prefetch=1,
-            grid=(steps,),
+            grid=(2048 // QB,),
             in_specs=[
-                spec((QB, 256), lambda i, low: (i, 0)),
                 spec((2048, 256), lambda i, low: (0, 0)),
-                spec((2048, 256), lambda i, low: (0, 0)),
+                spec((2048, 128), lambda i, low: (0, 0)),
                 spec((1, 1, QB), lambda i, low: (i, 0, 0)),
             ],
             out_specs=(
-                spec((QB, 256), lambda i, low: (i, 0)),
+                spec((QB, 128), lambda i, low: (i, 0)),
                 spec((8, QB), lambda i, low: (0, i)),
             ),
             scratch_shapes=[
@@ -754,19 +747,18 @@
                 pltpu.VMEM((128, 2 * HALO), BF),
                 pltpu.VMEM((8, QB), F32),
                 pltpu.VMEM((8, QB), F32),
-                pltpu.VMEM((256, QB), F32),
+                pltpu.VMEM((128, QB), F32),
             ],
         ),
         compiler_params=params(),
-        cost_estimate=cost(25e9, 6e6),
+        cost_estimate=cost(12e9, 3e6),
         name="attend",
-    )(low_block, query, own, halo, start)
+    )(low_block, own, halo, start)
 
 
 def attend_back_kernel(
-    low_ref, query_ref, own_ref, halo_ref, start_ref, out_ref, grad_ref, log_ref,
-    query_grad_ref, own_grad_ref, halo_grad_ref,
-    keys, values, keys_t, key_grad, value_grad, blend,
+    low_ref, own_ref, halo_ref, start_ref, out_ref, grad_ref, log_ref,
+    own_grad_ref, halo_grad_ref, pairs, pairs_t, pair_grad, blend,
 ):
     step = pl.program_id(0)
 
@@ -775,114 +767,99 @@
         for first in range(0, HALO, 512):
             rows = slice(first, first + 512)
             late = slice(HALO + first, HALO + first + 512)
-            keys[rows, :] = halo_ref[rows, :128]
-            keys[late, :] = own_ref[rows, :128]
-            values[rows, :] = halo_ref[rows, 128:]
-            values[late, :] = own_ref[rows, 128:]
-            keys_t[:, rows] = halo_ref[rows, :128].astype(F32).T.astype(BF)
-            keys_t[:, late] = own_ref[rows, :128].astype(F32).T.astype(BF)
-        key_grad[...] = jnp.zeros(key_grad.shape, F32)
-        value_grad[...] = jnp.zeros(value_grad.shape, F32)
+            pairs[rows, :] = halo_ref[rows, :]
+            pairs[late, :] = own_ref[rows, 128:256]
+            pairs_t[:, rows] = halo_ref[rows, :].astype(F32).T.astype(BF)
+            pairs_t[:, late] = own_ref[rows, 128:256].astype(F32).T.astype(BF)
+        pair_grad[...] = jnp.zeros(pair_grad.shape, F32)
 
     start = start_ref[0]
+    here_rows = pl.ds(pl.multiple_of(step * QB, QB), QB)
+    query, grad = own_ref[here_rows, 0:128], grad_ref[...]
+    product = (out_ref[...].astype(F32) * grad.astype(F32)).T
     picks, incoming, centres = [], [], []
     for half in range(2):
-        columns = slice(half * 128, half * 128 + 128)
-        product = (out_ref[:, columns].astype(F32) * grad_ref[:, columns].astype(F32)).T
-        for group in range(2):
-            picks.append(lane_half(query_ref[:, columns], group))
-            incoming.append(lane_half(grad_ref[:, columns], group))
-            centres.append(
-                jnp.sum(product[group * HD : group * HD + HD, :], axis=0, keepdims=True)
+        picks.append(placed(query, half, 0))
+        incoming.append(placed(grad, half, 1))
+        centres.append(jnp.sum(product[half * HD : half * HD + HD, :], axis=0, keepdims=True))
+    blend[...] = jnp.zeros(blend.shape, F32)
+
+    def visit(block, carry):
+        first = pl.multiple_of(block * BACK_KB, BACK_KB)
+        allowed = allowed_pairs(first, BACK_KB, step, start)
+        here = pl.ds(first, BACK_KB)
+        pair, key_t = pairs[here, :], pairs_t[0:HD, here]
+        for half in range(2):
+            scores = nt(pair, picks[half]) * (attend_scale * LOG2E)
+            weight = jnp.where(allowed, jnp.exp2(scores - log_ref[half : half + 1, :]), 0.0)
+            weight_grad = nt(pair, incoming[half])
+            score_grad = (
+                weight * (weight_grad - centres[half]) * attend_scale
+            ).astype(BF)
+            pair_grad[here, :] += nn(weight.astype(BF), incoming[half]) + nn(
+                score_grad, picks[half]
             )
-    blend[...] = jnp.zeros(blend.shape, F32)
-
-    def visit(block, carry):
-        first = pl.multiple_of(block * KB, KB)
-        allowed = allowed_pairs(block, step, start)
-        here = pl.ds(first, KB)
-        key, value = keys[here, :], values[here, :]
-        for number in range(4):
-            scores = nt(key, picks[number]) * (attend_scale * LOG2E)
-            weight = jnp.where(
-                allowed, jnp.exp2(scores - log_ref[number : number + 1, :]), 0.0
-            )
-            weight_grad = nt(value, incoming[number])
-            score_grad = (weight * (weight_grad - centres[number])).astype(BF)
-            value_grad[here, :] += nn(weight.astype(BF), incoming[number])
-            key_grad[here, :] += nn(score_grad, picks[number])
-            group = number % 2
-            rows = slice(number * HD, number * HD + HD)
-            blend[rows, :] += nn(keys_t[group * HD : group * HD + HD, here], score_grad)
+            blend[half * HD : half * HD + HD, :] += nn(key_t, score_grad)
         return carry
 
-    lax.fori_loop(low_ref[step], step + HALO // KB + 1, visit, 0)
-    for half in range(2):
-        query_grad_ref[:, half * 128 : half * 128 + 128] = (
-            (blend[half * 128 : half * 128 + 128, :] * attend_scale).T.astype(BF)
-        )
+    lax.fori_loop(low_ref[step], (HALO + (step + 1) * QB) // BACK_KB, visit, 0)
+    own_grad_ref[here_rows, 0:128] = blend[...].T
 
     @pl.when(step == pl.num_programs(0) - 1)
     def _():
         for first in range(0, HALO, 512):
             rows = slice(first, first + 512)
             late = slice(HALO + first, HALO + first + 512)
-            halo_grad_ref[rows, :128] = (key_grad[rows, :] * attend_scale).astype(BF)
-            halo_grad_ref[rows, 128:] = value_grad[rows, :].astype(BF)
-            own_grad_ref[rows, :128] = key_grad[late, :] * attend_scale
-            own_grad_ref[rows, 128:] = value_grad[late, :]
-
-
-def attend_back(low_block, query, own, halo, start, out, grad, logs):
-    steps = query.shape[0] // QB
+            halo_grad_ref[rows, :] = pair_grad[rows, :].astype(BF)
+            own_grad_ref[rows, 128:256] = pair_grad[late, :]
+
+
+def attend_back(low_block, own, halo, start, out, grad, logs):
     spec = lambda shape, index: pl.BlockSpec(shape, index)
-    tile = spec((QB, 256), lambda i, low: (i, 0))
+    tile = spec((QB, 128), lambda i, low: (i, 0))
     whole = spec((2048, 256), lambda i, low: (0, 0))
+    half = spec((2048, 128), lambda i, low: (0, 0))
     return pl.pallas_call(
         attend_back_kernel,
-        out_shape=(
-            shaped((2048, 256), BF),
-            shaped((2048, 256), F32),
-            shaped((2048, 256), BF),
-        ),
+        out_shape=(shaped((2048, 256), F32), shaped((2048, 128), BF)),
         grid_spec=pltpu.PrefetchScalarGridSpec(
             num_scalar_prefetch=1,
-            grid=(steps,),
+            grid=(2048 // QB,),
             in_specs=[
-                tile,
                 whole,
-                whole,
+                half,
                 spec((1, 1, QB), lambda i, low: (i, 0, 0)),
                 tile,
                 tile,
                 spec((8, QB), lambda i, low: (0, i)),
             ],
-            out_specs=(tile, whole, whole),
+            out_specs=(whole, half),
             scratch_shapes=[
-                pltpu.VMEM((2 * HALO, 128), BF),
                 pltpu.VMEM((2 * HALO, 128), BF),
                 pltpu.VMEM((128, 2 * HALO), BF),
                 pltpu.VMEM((2 * HALO, 128), F32),
-                pltpu.VMEM((2 * HALO, 128), F32),
-                pltpu.VMEM((256, QB), F32),
+                pltpu.VMEM((128, QB), F32),
             ],
         ),
         compiler_params=params(),
-        cost_estimate=cost(60e9, 10e6),
+        cost_estimate=cost(30e9, 6e6),
         name="attend_back",
-    )(low_block, query, own, halo, start, out, grad, logs)
-
-
-def after_kernel(plan, me_ref, tokens_ref, attended_ref, extra_ref, routed_ref, *refs):
+    )(low_block, own, halo, start, out, grad, logs)
+
+
+def after_kernel(
+    plan, me_ref, tokens_ref, first_ref, second_ref, extra_ref, routed_ref, *refs
+):
     count = len(plan)
     hidden_ref, payload_ref, gates_ref, mats, sems = refs[count:]
-    copies = start_fetch_heads(me_ref[0], plan, refs[:count], mats, sems)
+    copies = start_fetch_out(me_ref[0], plan, refs[:count], mats, sems)
     stream = tokens_ref[...].astype(F32)
     for copy in copies:
         copy.wait()
-    branch = nn(attended_ref[0], mats[0:256, :])
-    for part in range(1, 4):
-        branch += nn(attended_ref[part], mats[part * 256 : part * 256 + 256, :])
+    branch = jnp.zeros((512, 1024), F32)
+    for part in range(4):
+        both = jnp.concatenate([first_ref[part], second_ref[part]], axis=1)
+        branch += nn(both, mats[part * 256 : part * 256 + 256, :])
     hidden = stream + branch_scale * branch
     hidden_ref[...] = hidden
     inverse = lax.rsqrt(jnp.mean(hidden * hidden, axis=-1, keepdims=True) + norm_eps)
@@ -900,17 +877,17 @@
 
 
 def after_attention(me, tokens, attended, extra, routed, pieces):
-    plan = heads_plan()
+    plan = plan_of(128)
     return pl.pallas_call(
         functools.partial(after_kernel, plan),
         out_shape=(shaped((512, 1024), F32), shaped((528, 1024), BF), shaped((32, 512), F32)),
-        in_specs=[in_smem()] + in_vmem(4) + in_hbm(len(plan)),
+        in_specs=[in_smem()] + in_vmem(5) + in_hbm(len(plan)),
         out_specs=tuple(in_vmem(3)),
-        scratch_shapes=[pltpu.VMEM((1024, 1024), BF), pltpu.SemaphoreType.DMA((16,))],
+        scratch_shapes=[pltpu.VMEM((1024, 1024), BF), pltpu.SemaphoreType.DMA((len(plan),))],
         compiler_params=params(),
         cost_estimate=cost(2 * 512 * 1024 * 1024, 8e6),
         name="after_attention",
-    )(me, tokens, attended, extra, routed, *pieces)
+    )(me, tokens, *attended, extra, routed, *pieces)
 
 
 def own_rows(me, packed):
@@ -983,7 +960,7 @@
 
 
 def pick_grads(me, partners, pieces):
-    blocks, plan = len(partners), block_plan(partners, 656)
+    blocks, plan = len(partners), block_plan(partners, 528)
     return pl.pallas_call(
         functools.partial(pick_grad_kernel, plan, blocks),
         out_shape=(
@@ -1055,23 +1032,21 @@
     )(me, slots, *pieces)
 
 
-def expert_kernel(base, me_ref, *refs):
+def both_parts(pair, part):
+    if part == 0:
+        return pair[0][0:4].reshape(576, -1)
+    return jnp.concatenate([pair[0][4:6].reshape(288, -1), pair[1][...].reshape(288, -1)], axis=0)
+
+
+def expert_grad_kernel(*refs):
     rows_refs, grads_refs, gate_refs = refs[0:2], refs[2:4], refs[4:6]
     gate_w, up_w, down_w = (ref[0] for ref in refs[6:9])
-    out_ref, in_grad_ref, mark_ref, grad_ref = refs[9:13]
-    lin_grads, inners, out_grads, inputs = refs[13:17]
-    expert = me_ref[0] * 4 + base + pl.program_id(0)
+    lin_ref, inner_ref, grad_ref = refs[9:12]
+    lin_grads, inners, out_grads, inputs = refs[12:16]
     for part in range(2):
         at = slice(part * 576, part * 576 + 576)
-
-        def both(pair):
-            if part == 0:
-                return pair[0][0:4].reshape(576, -1)
-            return jnp.concatenate(
-                [pair[0][4:6].reshape(288, -1), pair[1][...].reshape(288, -1)], axis=0
-            )
-
-        rows, grads, gate = both(rows_refs), both(grads_refs), both(gate_refs)
+        blocks = slice(part * 4, part * 4 + 4)
+        rows = both_parts(rows_refs, part)
         inputs[at, :] = rows
         gate_lin = nn(rows, gate_w)
         up_lin = nn(rows, up_w)
@@ -1079,26 +1054,16 @@
         swished = gate_lin * sigma
         inner = (swished * up_lin).astype(BF)
         inners[at, :] = inner
-        result = nn(inner, down_w).astype(BF)
-        out_ref[part * 4 : part * 4 + 4] = result.reshape(4, 144, 1024)
-        wide = grads.astype(F32)
-        gate_slot = jnp.sum(wide * result.astype(F32), axis=1, keepdims=True)
-        lane = lax.broadcasted_iota(jnp.int32, (576, 128), 1)
-        mark_ref[part * 4 : part * 4 + 4] = (
-            jnp.where(lane == expert, gate_slot, 0.0).astype(BF).reshape(4, 144, 128)
-        )
-        out_grad = (wide * gate[:, 0:1].astype(F32)).astype(BF)
+        inner_ref[blocks] = inner.reshape(4, 144, 512)
+        gate = both_parts(gate_refs, part)[:, 0:1].astype(F32)
+        out_grad = (both_parts(grads_refs, part).astype(F32) * gate).astype(BF)
         out_grads[at, :] = out_grad
         inner_grad = nt(out_grad, down_w)
-        gate_lin_grad = (
+        lin_grads[at, 0:512] = (
             inner_grad * up_lin * sigma * (1.0 + gate_lin * (1.0 - sigma))
         ).astype(BF)
-        up_lin_grad = (inner_grad * swished).astype(BF)
-        lin_grads[at, 0:512] = gate_lin_grad
-        lin_grads[at, 512:1024] = up_lin_grad
-        in_grad_ref[part * 4 : part * 4 + 4] = (
-            (nt(gate_lin_grad, gate_w) + nt(up_lin_grad, up_w)).astype(BF).reshape(4, 144, 1024)
-        )
+        lin_grads[at, 512:1024] = (inner_grad * swished).astype(BF)
+        lin_ref[blocks] = lin_grads[at, :].reshape(4, 144, 1024)
     down_grad = tn(inners[...], out_grads[...]).astype(BF)
     grad_ref[2048:2560, :] = down_grad[:, 0:512]
     grad_ref[2560:3072, :] = down_grad[:, 512:1024]
@@ -1106,26 +1071,24 @@
     grad_ref[1024:2048, :] = tn(inputs[...], lin_grads[:, 512:1024]).astype(BF)
 
 
-def run_experts(me, base, count, rows, grads, gates, gate_w, up_w, down_w):
+def expert_grads(base, count, rows, grads, gates, gate_w, up_w, down_w):
     spec = pl.BlockSpec
     wide = [spec((blocks, 144, 1024), lambda e: (0, base + e, 0)) for blocks in (6, 2)]
     slim = [spec((blocks, 144, 128), lambda e: (0, base + e, 0)) for blocks in (6, 2)]
     tall_w = spec((1, 1024, 512), lambda e: (base + e, 0, 0))
     flat_w = spec((1, 512, 1024), lambda e: (base + e, 0, 0))
     return pl.pallas_call(
-        functools.partial(expert_kernel, base),
+        expert_grad_kernel,
         out_shape=(
             shaped((8, 144 * count, 1024), BF),
-            shaped((8, 144 * count, 1024), BF),
-            shaped((8, 144 * count, 128), BF),
+            shaped((8, 144 * count, 512), BF),
             shaped((3072 * count, 512), BF),
         ),
         grid=(count,),
-        in_specs=[in_smem()] + wide * 2 + slim + [tall_w, tall_w, flat_w],
+        in_specs=wide * 2 + slim + [tall_w, tall_w, flat_w],
         out_specs=(
             spec((8, 144, 1024), lambda e: (0, e, 0)),
-            spec((8, 144, 1024), lambda e: (0, e, 0)),
-            spec((8, 144, 128), lambda e: (0, e, 0)),
+            spec((8, 144, 512), lambda e: (0, e, 0)),
             spec((3072, 512), lambda e: (e, 0)),
         ),
         scratch_shapes=[
@@ -1135,9 +1098,52 @@
             pltpu.VMEM((1152, 1024), BF),
         ],
         compiler_params=params(),
-        cost_estimate=cost(count * 11e9, count * 15e6),
-        name="experts",
-    )(me, *rows, *grads, *gates, gate_w, up_w, down_w)
+        cost_estimate=cost(count * 8e9, count * 15e6),
+        name="expert_grads",
+    )(*rows, *grads, *gates, gate_w, up_w, down_w)
+
+
+def expert_rows_kernel(base, me_ref, lin_ref, inner_ref, *refs):
+    grads_refs = refs[0:2]
+    gate_w, up_w, down_w = (ref[0] for ref in refs[2:5])
+    out_ref, in_grad_ref, mark_ref = refs[5:8]
+    expert = me_ref[0] * 4 + base + pl.program_id(0)
+    lane = lax.broadcasted_iota(jnp.int32, (576, 128), 1)
+    for part in range(2):
+        blocks = slice(part * 4, part * 4 + 4)
+        result = nn(inner_ref[blocks].reshape(576, 512), down_w).astype(BF)
+        out_ref[blocks] = result.reshape(4, 144, 1024)
+        wide = both_parts(grads_refs, part).astype(F32)
+        gate_slot = jnp.sum(wide * result.astype(F32), axis=1, keepdims=True)
+        mark_ref[blocks] = jnp.where(lane == expert, gate_slot, 0.0).astype(BF).reshape(4, 144, 128)
+        lin = lin_ref[blocks].reshape(576, 1024)
+        in_grad_ref[blocks] = (
+            (nt(lin[:, 0:512], gate_w) + nt(lin[:, 512:1024], up_w))
+            .astype(BF)
+            .reshape(4, 144, 1024)
+        )
+
+
+def expert_rows(me, base, count, lin, inner, grads, gate_w, up_w, down_w):
+    spec = pl.BlockSpec
+    wide = [spec((blocks, 144, 1024), lambda e: (0, base + e, 0)) for blocks in (6, 2)]
+    tall_w = spec((1, 1024, 512), lambda e: (base + e, 0, 0))
+    flat_w = spec((1, 512, 1024), lambda e: (base + e, 0, 0))
+    own = lambda width: spec((8, 144, width), lambda e: (0, e, 0))
+    return pl.pallas_call(
+        functools.partial(expert_rows_kernel, base),
+        out_shape=(
+            shaped((8, 144 * count, 1024), BF),
+            shaped((8, 144 * count, 1024), BF),
+            shaped((8, 144 * count, 128), BF),
+        ),
+        grid=(count,),
+        in_specs=[in_smem(), own(1024), own(512)] + wide + [tall_w, tall_w, flat_w],
+        out_specs=(own(1024), own(1024), own(128)),
+        compiler_params=params(),
+        cost_estimate=cost(count * 4e9, count * 14e6),
+        name="expert_rows",
+    )(me, lin, inner, *grads, gate_w, up_w, down_w)
 
 
 def combine_kernel(calls, weighted, *refs):
@@ -1206,8 +1212,8 @@
     extra_ref, *refs,
 ):
     count = len(plan)
-    hidden_grad_ref, branch_grad_ref, attended_grad_ref, small_ref, mats, sems = refs[count:]
-    copies = start_fetch_heads(me_ref[0], plan, refs[:count], mats, sems)
+    hidden_grad_ref, branch_grad_ref, first_ref, second_ref, small_ref, mats, sems = refs[count:]
+    copies = start_fetch_out(me_ref[0], plan, refs[:count], mats, sems)
     total = (
         sum_ref[...].astype(F32) + sum_x_ref[...].astype(F32) + sum_y_ref[...].astype(F32)
     )
@@ -1232,24 +1238,25 @@
     for copy in copies:
         copy.wait()
     for part in range(4):
-        attended_grad_ref[part] = nt(
-            branch_grad, mats[part * 256 : part * 256 + 256, :]
-        ).astype(BF)
+        grad = nt(branch_grad, mats[part * 256 : part * 256 + 256, :]).astype(BF)
+        first_ref[part] = grad[:, 0:128]
+        second_ref[part] = grad[:, 128:256]
 
 
 def back_to_attention(me, sums, hidden, cotangent, payload, gates, extra, pieces):
-    plan = heads_plan()
+    plan = plan_of(128)
     return pl.pallas_call(
         functools.partial(back_kernel, plan),
         out_shape=(
             shaped((512, 1024), F32),
             shaped((512, 1024), BF),
-            shaped((4, 512, 256), BF),
+            shaped((4, 512, 128), BF),
+            shaped((4, 512, 128), BF),
             shaped((40, 1024), F32),
         ),
         in_specs=[in_smem()] + in_vmem(8) + in_hbm(len(plan)),
-        out_specs=tuple(in_vmem(4)),
-        scratch_shapes=[pltpu.VMEM((1024, 1024), BF), pltpu.SemaphoreType.DMA((16,))],
+        out_specs=tuple(in_vmem(5)),
+        scratch_shapes=[pltpu.VMEM((1024, 1024), BF), pltpu.SemaphoreType.DMA((len(plan),))],
         compiler_params=params(),
         cost_estimate=cost(2 * 512 * 1024 * 1024, 12e6),
         name="back_to_attention",
@@ -1263,15 +1270,11 @@
             target[pair] = big[pl.ds(start, 128), :]
 
 
-def out_grad_kernel(me_ref, attended_ref, branch_grad_ref, small_ref, odd_ref, even_ref, big):
+def out_grad_kernel(me_ref, first_ref, second_ref, branch_grad_ref, small_ref, odd_ref, even_ref, big):
     branch_grad = branch_grad_ref[...]
     for part in range(4):
-        grad = tn(attended_ref[part], branch_grad).astype(BF)
-        for half in range(2):
-            for group in range(2):
-                source = half * 128 + group * HD
-                target = part * 256 + (2 * group + half) * HD
-                big[target : target + HD, 0:1024] = grad[source : source + HD, :]
+        both = jnp.concatenate([first_ref[part], second_ref[part]], axis=1)
+        big[part * 256 : part * 256 + 256, 0:1024] = tn(both, branch_grad).astype(BF)
     small = jnp.concatenate([small_ref[...], jnp.zeros((88, 1024), F32)], axis=0)
     big[:, 1024:1152] = small.T.astype(BF)
     deal_out(me_ref[0], big, odd_ref, even_ref)
@@ -1281,17 +1284,17 @@
     return pl.pallas_call(
         out_grad_kernel,
         out_shape=(shaped((4, 128, 1152), BF), shaped((4, 128, 1152), BF)),
-        in_specs=[in_smem()] + in_vmem(3),
+        in_specs=[in_smem()] + in_vmem(4),
         out_specs=tuple(in_vmem(2)),
         scratch_shapes=[pltpu.VMEM((1024, 1152), BF)],
         compiler_params=params(),
         cost_estimate=cost(2 * 512 * 1024 * 1024, 5e6),
         name="out_grads",
-    )(me, attended, branch_grad, small)
+    )(me, *attended, branch_grad, small)
 
 
 def input_kernel(
-    plan, me_ref, tokens_ref, cos_ref, sin_ref, query_grad_ref, pair_grad_ref, extra_ref,
+    plan, me_ref, tokens_ref, cos_ref, sin_ref, first_ref, second_ref, extra_ref,
     hidden_grad_ref, *refs,
 ):
     count = len(plan)
@@ -1304,15 +1307,17 @@
     normed = (stream * inverse * gain).astype(BF)
     cosine, sine = cos_ref[...], -sin_ref[...]
     for part in range(4):
-        for half in range(2):
-            columns = slice(half * 128, half * 128 + 128)
-            lin[:, part * 256 + half * 128 : part * 256 + half * 128 + 128] = turn(
-                query_grad_ref[part, :, columns].astype(F32), cosine, sine
+        tiles = []
+        for group, source in enumerate((first_ref, second_ref)):
+            lin[:, part * 256 + group * 128 : part * 256 + group * 128 + 128] = turn(
+                source[part, :, 0:128].astype(F32), cosine, sine
             ).astype(BF)
-        lin[:, 1024 + part * 128 : 1152 + part * 128] = turn(
-            pair_grad_ref[part, :, 0:128].astype(F32), cosine, sine
-        ).astype(BF)
-        lin[:, 1536 + part * 128 : 1664 + part * 128] = pair_grad_ref[part, :, 128:256]
+            tiles.append(source[part, :, 128:256].astype(F32))
+        lane = lax.broadcasted_iota(jnp.int32, tiles[0].shape, 1)
+        key = jnp.where(lane < HD, tiles[0], pltpu.roll(tiles[1], HD, 1))
+        value = jnp.where(lane < HD, pltpu.roll(tiles[0], HD, 1), tiles[1])
+        lin[:, 1024 + part * 128 : 1152 + part * 128] = turn(key, cosine, sine).astype(BF)
+        lin[:, 1536 + part * 128 : 1664 + part * 128] = value.astype(BF)
     normed_t = normed.astype(F32).T.astype(BF)
     for first in range(0, 2048, 512):
         big[:, first : first + 512] = nn(normed_t, lin[:, first : first + 512]).astype(BF)
@@ -1361,46 +1366,15 @@
     return (jnp.where(routed & (slot < 144), slot, 255).astype(BF), routed.astype(F32))
 
 
-def swap_middle(values):
-    rows, columns = values.shape
-    parts = values.reshape(rows, columns // 256, 2, 2, HD)
-    return parts.transpose(0, 1, 3, 2, 4).reshape(rows, columns)
-
-
-class Copies:
-    def __init__(self, seq):
-        self.outer = (seq == 0) | (seq == 3)
-        self.waiting = []
-        self.flying = []
-        self.sums = []
-
-    def add(self, value):
-        self.waiting.append(value)
-
-    def step(self, gate):
-        arrived, self.flying = self.flying, []
-        fresh, self.waiting = self.waiting[:1], self.waiting[1:]
-        gate, received, fresh = lax.optimization_barrier(
-            (gate, [item[2] for item in arrived], fresh)
-        )
-        ready = []
-        for (phase, value, _), got in zip(arrived, received):
-            if phase == 2:
-                self.sums.append(jnp.where(self.outer, got, value))
-            else:
-                ready.append((phase + 1, add_low(value, got)))
-        ready += [(0, value) for value in fresh]
-        for phase, value in ready:
-            pairs = (((0, 1), (3, 2)), ((1, 2), (2, 1)), ((1, 0), (2, 3)))[phase]
-            self.flying.append((phase, value, lax.ppermute(value, "sp", pairs)))
-        return gate
-
-
-def sum_line(value, seq):
-    outer = (seq == 0) | (seq == 3)
-    value = add_low(value, lax.ppermute(value, "sp", ((0, 1), (3, 2))))
-    value = add_low(value, lax.ppermute(value, "sp", ((1, 2), (2, 1))))
-    return jnp.where(outer, lax.ppermute(value, "sp", ((1, 0), (2, 3))), value)
+def across(values):
+    return lax.all_to_all(values, "sp", split_axis=0, concat_axis=0, tiled=True)
+
+
+def sum_shared(value):
+    rows, columns = value.shape
+    quarters = across(value).reshape(4, rows // 4, columns).astype(F32)
+    quarter = jnp.sum(quarters, axis=0).astype(BF)
+    return across(jnp.tile(quarter, (4, 1)))
 
 
 def fast_local(
@@ -1420,13 +1394,15 @@
         ],
         axis=1,
     )
-    shard = jnp.concatenate([swap_middle(query_weight), key_weight, value_weight, small], axis=1)
+    shard = jnp.concatenate(
+        [query_weight, key_weight, value_weight, small, out_weight], axis=1
+    )
     project_pieces = spread(shard)
 
     slots, routed = dense_slots(expert_routes, drop_rank, 32)
     mixture_grad = (branch_scale * output_grad.astype(F32)).astype(BF)
     grad_payload = jnp.concatenate(
-        [mixture_grad, jnp.concatenate([slots[:16], slots[16:]], axis=1), out_weight], axis=0
+        [mixture_grad, jnp.concatenate([slots[:16], slots[16:]], axis=1)], axis=0
     )
 
     block_start = fsdp * 2048
@@ -1440,44 +1416,42 @@
     start = HALO + jnp.arange(2048, dtype=jnp.int32) - position_span
     start_rows = start.reshape(2048 // QB, 1, QB)
     low_block = start_rows[:, 0, 0] // KB
-
-    query, pair, extra = project(me, tokens, cosine, sine, project_pieces)
+    low_back = start_rows[:, 0, 0] // BACK_KB
+
+    first, second, extra = project(me, tokens, cosine, sine, project_pieces)
     grad_payload = hold(grad_payload, project_pieces[6], project_pieces[7])
     own, beside = grad_payload, flip(grad_payload, 1)
     along_x, along_y = flip(grad_payload, 2), flip(grad_payload, 4)
-    pair_heads = lax.all_to_all(
-        pair.reshape(2048, 256), "sp", split_axis=0, concat_axis=0, tiled=True
-    )
-    pair_heads, query, beside, along_x, along_y = lax.optimization_barrier(
-        (pair_heads, query, beside, along_x, along_y)
-    )
-    query_heads = lax.all_to_all(
-        query.reshape(2048, 256), "sp", split_axis=0, concat_axis=0, tiled=True
-    )
-    halo = from_behind(pair_heads, "fsdp", 1)
+    heads = [across(first.reshape(2048, 256)), None]
+    heads[0], second, beside, along_x, along_y = lax.optimization_barrier(
+        (heads[0], second, beside, along_x, along_y)
+    )
+    heads[1] = across(second.reshape(2048, 256))
+    halos = [from_behind(heads[0][:, 128:256], "fsdp", 1), None]
     near_pieces = (own, beside, along_x, flip(along_x, 1), along_y, flip(along_y, 1))
+    blended, logs = [None, None], [None, None]
+    blended[0], logs[0] = attend(low_block, heads[0], halos[0], start_rows)
+    blended[0], heads[1] = lax.optimization_barrier((blended[0], heads[1]))
+    halos[1] = from_behind(heads[1][:, 128:256], "fsdp", 1)
+    first_back = across(blended[0])
+    near, far = (0, 1, 2, 3, 4, 5), (6, 7)
+    near_grads = pick_grads(me, near, near_pieces)
+    halos[1], near_grads = lax.optimization_barrier((halos[1], near_grads))
     diagonal = spread_diagonal(near_pieces)
-    query_heads, halo, near_pieces, diagonal = lax.optimization_barrier(
-        (query_heads, halo, near_pieces, diagonal)
-    )
-    near, far = (0, 1, 2, 3, 4, 5), (6, 7)
-    blended, logs = attend(low_block, query_heads, pair_heads, halo, start_rows)
-    attended = lax.all_to_all(blended, "sp", split_axis=0, concat_axis=0, tiled=True).reshape(
-        4, 512, 256
-    )
-    far_pieces = spread_far(diagonal)
-    near_grads = pick_grads(me, near, near_pieces)
-    far_grads = pick_grads(me, far, far_pieces)
-    attended, near_grads, far_grads = lax.optimization_barrier((attended, near_grads, far_grads))
-    grad_rows, slot_rows, slot_columns = zip(near_grads, far_grads)
-    grad_pieces = near_pieces + far_pieces
-    out_pieces = [
-        piece
-        for piece, (_, first, rows) in zip(grad_pieces, plan_of(656))
-        if first + rows == 656
-    ]
+    blended[1], logs[1] = attend(low_block, heads[1], halos[1], start_rows)
+    blended[1], first_back, diagonal = lax.optimization_barrier(
+        (blended[1], first_back, diagonal)
+    )
+    attended = [first_back, across(blended[1])]
+    far_grads = pick_grads(me, far, spread_far(diagonal))
+    all_slot_columns = jnp.concatenate([near_grads[2], far_grads[2]], axis=0)
+    attended, near_grads, far_grads, all_slot_columns = lax.optimization_barrier(
+        (attended, near_grads, far_grads, all_slot_columns)
+    )
+    attended = [part.reshape(4, 512, 128) for part in attended]
+    grad_rows, slot_rows, _ = zip(near_grads, far_grads)
     hidden_one, payload, gates = after_attention(
-        me, tokens, attended, extra, routed, out_pieces
+        me, tokens, attended, extra, routed, project_pieces
     )
     near_pieces = spread_near(payload)
     diagonal = spread_diagonal(near_pieces)
@@ -1485,71 +1459,92 @@
     near_rows, diagonal = lax.optimization_barrier((near_rows, diagonal))
     far_rows = pick_rows(me, slot_rows[1], far, spread_far(diagonal))
     rows, slot_gates, gate_columns = zip(near_rows, far_rows)
-    slot_columns = jnp.concatenate(slot_columns, axis=0)
-    gate_columns = jnp.concatenate(gate_columns, axis=0)
-    copies = Copies(seq)
-    results, here = [], me
-    for expert in range(4):
-        results.append(
-            run_experts(
-                here, expert, 1, rows, grad_rows, slot_gates, gate_weight, up_weight, down_weight
-            )
-        )
-        copies.add(results[-1][3])
-        if expert == 0:
-            here = copies.step(me)
-    outs, in_grads, marks, _ = zip(*results)
-    in_grads = copies.step(in_grads)
-    odd = combine(1, slot_columns, None, in_grads, marks)
-    even = combine(0, slot_columns, None, in_grads, marks)
-    sums = collect(odd, even, copies.step)
-    hidden_grad, branch_grad, attended_grad, small_grads = back_to_attention(
-        me, sums, hidden_one, output_grad, payload, gates, extra, out_pieces
-    )
-    grad_heads = lax.all_to_all(
-        attended_grad.reshape(2048, 256), "sp", split_axis=0, concat_axis=0, tiled=True
-    )
-    grad_heads = copies.step(grad_heads)
-    odd_mix = combine(1, slot_columns, gate_columns, outs, ())
-    even_mix = combine(0, slot_columns, gate_columns, outs, ())
-    mixture = collect(odd_mix, even_mix)
-    output = (
-        hidden_one
-        + branch_scale
-        * (mixture[0].astype(F32) + mixture[1].astype(F32) + mixture[2].astype(F32))
-    ).astype(BF)
-    out_sums = collect(*out_grads_of(me, attended, branch_grad, small_grads))
-
-    query_back, own_back, halo_back = attend_back(
-        low_block, query_heads, pair_heads, halo, start_rows, blended, grad_heads, logs
-    )
-    query_back, own_back, halo_back = copies.step((query_back, own_back, halo_back))
-    pair_back = (own_back + from_behind(halo_back, "fsdp", -1).astype(F32)).astype(BF)
-    query_grad = lax.all_to_all(
-        query_back, "sp", split_axis=0, concat_axis=0, tiled=True
-    ).reshape(4, 512, 256)
-    pair_grad = lax.all_to_all(
-        pair_back, "sp", split_axis=0, concat_axis=0, tiled=True
-    ).reshape(4, 512, 256)
-    query_grad, pair_grad = copies.step((query_grad, pair_grad))
-    input_grad, odd_in, even_in = input_grads(
-        me, tokens, cosine, sine, query_grad, pair_grad, extra, hidden_grad, project_pieces
-    )
-    in_sums = collect(odd_in, even_in)
-
-    out_shard = sum(term.astype(F32) for term in out_sums).astype(BF)
-    in_shard = sum(term.astype(F32) for term in in_sums).astype(BF)
-    shards = sum_line(jnp.concatenate([in_shard, out_shard], axis=1), seq)
+    mats = (gate_weight, up_weight, down_weight)
+    lin_grads, inners, parts = zip(
+        *[expert_grads(base, 2, rows, grad_rows, slot_gates, *mats) for base in (0, 2)]
+    )
+    sums_of_parts = lax.psum(parts, "sp")
+
+    def finish(turn_number, _):
+        here, slot_columns = hold((me, all_slot_columns), turn_number)
+        outs, in_grads, marks = zip(
+            *[
+                expert_rows(here, 2 * pair, 2, lin_grads[pair], inners[pair], grad_rows, *mats)
+                for pair in range(2)
+            ]
+        )
+        odd = combine(1, slot_columns, None, in_grads, marks)
+        even = combine(0, slot_columns, None, in_grads, marks)
+        sums = collect(odd, even)
+        hidden_grad, branch_grad, first_grad, second_grad, small_grads = back_to_attention(
+            me, sums, hidden_one, output_grad, payload, gates, extra, project_pieces
+        )
+        first_heads = across(first_grad.reshape(2048, 128))
+        first_heads, second_grad = lax.optimization_barrier((first_heads, second_grad))
+        second_heads = across(second_grad.reshape(2048, 128))
+        first_own, first_halo = attend_back(
+            low_back, heads[0], halos[0], start_rows, blended[0], first_heads, logs[0]
+        )
+        first_own, first_halo, second_heads = lax.optimization_barrier(
+            (first_own, first_halo, second_heads)
+        )
+        held_outs, held_gates = hold((outs, gate_columns), first_heads)
+        held_gates = jnp.concatenate(held_gates, axis=0)
+        odd_mix = combine(1, slot_columns, held_gates, held_outs, ())
+        even_mix = combine(0, slot_columns, held_gates, held_outs, ())
+        mixture = collect(odd_mix, even_mix)
+        output = (
+            hidden_one
+            + branch_scale
+            * (mixture[0].astype(F32) + mixture[1].astype(F32) + mixture[2].astype(F32))
+        ).astype(BF)
+        out_sums = collect(*out_grads_of(me, attended, branch_grad, small_grads))
+
+        def grads_home(own_grad, halo_grad):
+            returned = from_behind(halo_grad, "fsdp", -1).astype(F32)
+            own_grad = own_grad + jnp.pad(returned, ((0, 0), (128, 0)))
+            return across(own_grad.astype(BF)).reshape(4, 512, 256)
+
+        first_home = grads_home(first_own, first_halo)
+        second_own, second_halo = attend_back(
+            low_back, heads[1], halos[1], start_rows, blended[1], second_heads, logs[1]
+        )
+        second_own, second_halo, first_home = lax.optimization_barrier(
+            (second_own, second_halo, first_home)
+        )
+        second_home = grads_home(second_own, second_halo)
+        input_grad, odd_in, even_in = input_grads(
+            me, tokens, cosine, sine, first_home, second_home, extra, hidden_grad, project_pieces
+        )
+        in_sums = collect(odd_in, even_in)
+
+        out_shard = sum(term.astype(F32) for term in out_sums).astype(BF)
+        in_shard = sum(term.astype(F32) for term in in_sums).astype(BF)
+        shards = sum_shared(jnp.concatenate([in_shard, out_shard], axis=1))
+        return (output, input_grad, shards)
+
+    rounds = 1 + (documents[0] > 0).astype(jnp.int32)
+    output, input_grad, shards = lax.fori_loop(
+        0,
+        rounds,
+        finish,
+        (
+            jnp.zeros((512, 1024), BF),
+            jnp.zeros((512, 1024), BF),
+            jnp.zeros((128, 3328), BF),
+        ),
+    )
     in_shard, out_shard = shards[:, 0:2176], shards[:, 2176:3328]
-    while copies.flying:
-        copies.step(())
+    sums_of_parts = [
+        total[first : first + 3072] for total in sums_of_parts for first in (0, 3072)
+    ]
     stacked = [
-        jnp.stack([total[0:1024] for total in copies.sums]).astype(F32),
-        jnp.stack([total[1024:2048] for total in copies.sums]).astype(F32),
+        jnp.stack([total[0:1024] for total in sums_of_parts]).astype(F32),
+        jnp.stack([total[1024:2048] for total in sums_of_parts]).astype(F32),
         jnp.stack(
             [
                 jnp.concatenate([total[2048:2560], total[2560:3072]], axis=1)
-                for total in copies.sums
+                for total in sums_of_parts
             ]
         ).astype(F32),
     ]
@@ -1557,7 +1552,7 @@
         output,
         input_grad,
         in_shard[:, 2048].astype(F32),
-        swap_middle(in_shard[:, 0:1024]).astype(F32),
+        in_shard[:, 0:1024].astype(F32),
         in_shard[:, 1024:1536].astype(F32),
         in_shard[:, 1536:2048].astype(F32),
         out_shard[:, 0:1024].astype(F32),

time: 890 us -> 853 us (0.958)
  waiting for transfers between devices: 384 us -> 276 us
  blocking collectives: 0 us -> 33.2 us
  other arithmetic: 110 us -> 80.2 us
  loops' own time: 0 us -> 26.7 us
  local copies, waits for them, and re-layouts: 30.1 us -> 51 us
  between operations: 2 us -> 15.5 us
  Pallas kernels: 237 us -> 246 us
    ppermute x15 -> x0, waiting for transfers between devices: 148 us -> none  [the longest x12 124 us: step(): self.flying.append((phase, value, lax.ppermute(value, 'sp', pairs)))]
    all_to_all x6 -> x9, waiting for transfers between devices: 93.3 us -> 141 us  [across(): return lax.all_to_all(values, 'sp', split_axis=0, concat_axis=0, tiled=True)]
    ppermute x15 -> x0, starting transfers between devices: 46.2 us -> none  [the longest x12 42.6 us: step(): self.flying.append((phase, value, lax.ppermute(value, 'sp', pairs)))]
    convert_element_type x15 -> x5, other arithmetic: 45.5 us -> 8.79 us  [add_low(): return (left.astype(F32) + right.astype(F32)).astype(BF)]
    all_to_all x0 -> x1, blocking collectives: none -> 33.2 us  [across(): return lax.all_to_all(values, 'sp', split_axis=0, concat_axis=0, tiled=True)]
    ppermute x47, starting transfers between devices: 32.8 us -> 63.3 us  [flip(): lax.ppermute(value, 'fsdp', [(place, place ^ bit) for place in range(8)])]
    another operation x0 -> x1, loops' own time: none -> 26.7 us  [fast_local(): lax.fori_loop(0, rounds, finish, (jnp.zeros((512, 1024), BF), jnp.zeros((...]
    ppermute x47, waiting for transfers between devices: 142 us -> 117 us  [flip(): lax.ppermute(value, 'fsdp', [(place, place ^ bit) for place in range(8)])]
  transfers between devices with their start and end apart: 70 -> 61, of which waited for: 26 -> 28; matrix products, arithmetic and copies ran while one was open for 14% -> 12% of each run, Pallas kernels for 17% -> 21%
where the time goes in v3:
time: 853 us; the launch traced here: 843 us
  waiting for transfers between devices  276 us (32%)
  Pallas kernels  246 us (29%)
  starting transfers between devices  114 us (13%)
  other arithmetic  80.2 us (9%)
  local copies, waits for them, and re-layouts  51 us (6%)
  blocking collectives  33.2 us (4%)
  loops' own time  26.7 us (3%)
  between operations  15.5 us (2%)
    all_to_all x9, waiting for transfers between devices, across(): return lax.all_to_all(values, 'sp', split_axis=0, concat_axis=0, tiled=True)  141 us
    ppermute x47, waiting for transfers between devices, flip(): lax.ppermute(value, 'fsdp', [(place, place ^ bit) for place in range(8)])  117 us
    ppermute x47, starting transfers between devices, flip(): lax.ppermute(value, 'fsdp', [(place, place ^ bit) for place in range(8)])  63.3 us
    pallas_call x2, Pallas kernels, expert_grads(): pl.pallas_call(expert_grad_kernel, out_shape=(shaped((8, 144 * count, 102...  46.9 us
    pallas_call x2, Pallas kernels, attend_back(): pl.pallas_call(attend_back_kernel, out_shape=(shaped((2048, 256), F32), s...  43.8 us
    all_to_all x9, starting transfers between devices, across(): return lax.all_to_all(values, 'sp', split_axis=0, concat_axis=0, tiled=True)  39.4 us
    pallas_call x4, Pallas kernels, combine(): pl.pallas_call(functools.partial(combine_kernel, calls, weighted), out_sh...  33.9 us
    all_to_all x1, blocking collectives, across(): return lax.all_to_all(values, 'sp', split_axis=0, concat_axis=0, tiled=True)  33.2 us
  transfers between devices with their start and end apart: 61, of which 28 were waited for; matrix products, arithmetic and copies ran while one was open for 12% of the time, Pallas kernels for 21%

profile of v3, /device:TPU:0, one launch (start us, length us, event | category | flops | bytes accessed | tf_op | source)
XLA Modules:
  0.0 842.9 jit_solution(11387809758100320078)
XLA Ops:
  23.9 10.5 %collective-permute-done.25.refs_4_ = bf16[128,3200]{1,0:T(8,128)(2,1)S(1)} collective-permute-done((bf16[128,3200]{1,0:T(8,128)(2,1)S(1)}, bf16[128,3200]{1,0:T(8,128)(2,1)S(1)}, u32[]{:S(2)}, u32[]{:S(2)}) %collective-permute-start.25) | collective-permute-done | bytes 819232 | tf_op jit(solution)/shard_map/ppermute | solution.py:512
  49.6 8.3 project.1
  66.7 23.0 %collective-permute-done.32.refs_2_ = bf16[528,1024]{1,0:T(8,128)(2,1)S(1)} collective-permute-done((bf16[528,1024]{1,0:T(8,128)(2,1)S(1)}, bf16[528,1024]{1,0:T(8,128)(2,1)S(1)}, u32[]{:S(2)}, u32[]{:S(2)}) %collective-permute-start.32) | collective-permute-done | bytes 1081376 | tf_op jit(solution)/shard_map/ppermute | solution.py:512
  102.8 13.3 %attend.2 = (bf16[2048,128]{1,0:T(8,128)(2,1)}, f32[8,2048]{1,0:T(8,128)}) custom-call(s32[4]{0:T(128)} %get-tuple-element.978.low_ref, bf16[2048,256]{1,0:T(8,128)(2,1)} %bitcast.11.own_ref, bf16[2048,128]{1,0:T(8,128)(2,1)S(1)} %collective-permute-done.34.halo_ref, s32[4,1,512]{2,1,0:T(1,128)S(1)} %bitcast.229), custom_call_target="tpu_custom_call" | custom-call | flops 1500000000 | bytes 375000 | tf_op jit(solution)/shard_map/attend/pallas_call | solution.py:730
  147.5 13.4 %attend.3 = (bf16[2048,128]{1,0:T(8,128)(2,1)}, f32[8,2048]{1,0:T(8,128)}) custom-call(s32[4]{0:T(128)} %get-tuple-element.978.low_ref, bf16[2048,256]{1,0:T(8,128)(2,1)} %bitcast.12.own_ref, bf16[2048,128]{1,0:T(8,128)(2,1)} %collective-permute-done.35.halo_ref, s32[4,1,512]{2,1,0:T(1,128)S(1)} %bitcast.230), custom_call_target="tpu_custom_call" | custom-call | flops 1500000000 | bytes 375000 | tf_op jit(solution)/shard_map/attend/pallas_call | solution.py:730
  191.2 23.9 %collective-permute-done.43.refs_2_ = bf16[528,1024]{1,0:T(8,128)(2,1)S(1)} collective-permute-done((bf16[528,1024]{1,0:T(8,128)(2,1)}, bf16[528,1024]{1,0:T(8,128)(2,1)S(1)}, u32[]{:S(2)}, u32[]{:S(2)}) %collective-permute-start.43) | collective-permute-done | bytes 1081376 | tf_op jit(solution)/shard_map/ppermute | solution.py:512
  222.5 9.4 %pick_rows.2 = (bf16[6,576,1024]{2,1,0:T(8,128)(2,1)}, bf16[6,576,128]{2,1,0:T(8,128)(2,1)}, bf16[6,512,128]{2,1,0:T(8,128)(2,1)}) custom-call(s32[1]{0:T(128)} %bitcast.1.me_ref, f32[6,4,512]{2,1,0:T(4,128)} %get-tuple-element.666.slots_ref, bf16[528,1024]{1,0:T(8,128)(2,1)} %get-tuple-element.1393.refs_0_, bf16[528,1024]{1,0:T(8,128)(2,1)} %copy-done.31, ...), custom_call_target="tpu_custom_call" | custom-call | flops 452984832 | bytes 1800000 | tf_op jit(solution)/shard_map/pick_rows/pallas_call | solution.py:1014
  243.0 23.4 %expert_grads.2 = (bf16[8,288,1024]{2,1,0:T(8,128)(2,1)}, bf16[8,288,512]{2,1,0:T(8,128)(2,1)}, bf16[6144,512]{1,0:T(8,128)(2,1)}) custom-call(bf16[6,576,1024]{2,1,0:T(8,128)(2,1)} %get-tuple-element.674.refs_0_, bf16[2,576,1024]{2,1,0:T(8,128)(2,1)} %get-tuple-element.678.refs_1_, bf16[6,576,1024]{2,1,0:T(8,128)(2,1)} %get-tuple-element.1384.refs_2_, ...), custom_call_target="tpu_custom_call" | custom-call | flops 2000000000 | bytes 3750000 | tf_op jit(solution)/shard_map/expert_grads/pallas_call | solution.py:1080
  266.4 23.5 %expert_grads.3 = (bf16[8,288,1024]{2,1,0:T(8,128)(2,1)}, bf16[8,288,512]{2,1,0:T(8,128)(2,1)}, bf16[6144,512]{1,0:T(8,128)(2,1)}) custom-call(bf16[6,576,1024]{2,1,0:T(8,128)(2,1)} %get-tuple-element.674.refs_0_, bf16[2,576,1024]{2,1,0:T(8,128)(2,1)} %get-tuple-element.678.refs_1_, bf16[6,576,1024]{2,1,0:T(8,128)(2,1)} %get-tuple-element.1384.refs_2_, ...), custom_call_target="tpu_custom_call" | custom-call | flops 2000000000 | bytes 3750000 | tf_op jit(solution)/shard_map/expert_grads/pallas_call | solution.py:1080
  293.2 501.3 %while.17 = (s32[]{:T(128)}, bf16[512,1024]{1,0:T(8,128)(2,1)}, bf16[512,1024]{1,0:T(8,128)(2,1)}, bf16[128,3328]{1,0:T(8,128)(2,1)}, s32[]{:T(128)}, /*index=5*...) while((s32[]{:T(128)}, bf16[512,1024]{1,0:T(8,128)(2,1)}, ...), condition=%wide.region_6.7_spmd.clone, body=%wide.region_4.6_spmd.clone.sunk | while | flops 11965177856 | bytes 275651040 | solution.py:1527
  316.7 13.9 %expert_rows.8 = (bf16[8,288,1024]{2,1,0:T(8,128)(2,1)}, bf16[8,288,1024]{2,1,0:T(8,128)(2,1)}, bf16[8,288,128]{2,1,0:T(8,128)(2,1)}) custom-call(s32[1]{0:T(128)} %get-tuple-element.1327.me_ref, bf16[8,288,1024]{2,1,0:T(8,128)(2,1)} %get-tuple-element.1484.lin_ref, bf16[8,288,512]{2,1,0:T(8,128)(2,1)} %get-tuple-element.1485.inner_ref, ...), custom_call_target="tpu_custom_call" | custom-call | flops 1000000000 | bytes 3500000 | tf_op jit(solution)/shard_map/while/body/expert_rows/pallas_call | solution.py:1133
  330.6 13.9 %expert_rows.9 = (bf16[8,288,1024]{2,1,0:T(8,128)(2,1)}, bf16[8,288,1024]{2,1,0:T(8,128)(2,1)}, bf16[8,288,128]{2,1,0:T(8,128)(2,1)}) custom-call(s32[1]{0:T(128)} %get-tuple-element.1327.me_ref, bf16[8,288,1024]{2,1,0:T(8,128)(2,1)} %get-tuple-element.1491.lin_ref, bf16[8,288,512]{2,1,0:T(8,128)(2,1)} %get-tuple-element.1492.inner_ref, ...), custom_call_target="tpu_custom_call" | custom-call | flops 1000000000 | bytes 3500000 | tf_op jit(solution)/shard_map/while/body/expert_rows/pallas_call | solution.py:1133
  344.5 8.8 %combine.16 = bf16[4,528,1024]{2,1,0:T(8,128)(2,1)} custom-call(bf16[8,512,128]{2,1,0:T(8,128)(2,1)S(1)} %get-tuple-element.1326.refs_0_, bf16[8,288,1024]{2,1,0:T(8,128)(2,1)} %get-tuple-element.1330.refs_1_, bf16[8,288,1024]{2,1,0:T(8,128)(2,1)} %get-tuple-element.1331.refs_2_, bf16[8,288,128]{2,1,0:T(8,128)(2,1)} %get-tuple-element.1332.refs_3_, ...), custom_call_target="tpu_custom_call" | custom-call | flops 402653184 | bytes 1250000 | tf_op jit(solution)/shard_map/while/body/combine/pallas_call | solution.py:1195
  353.4 8.6 %combine.17 = bf16[4,528,1024]{2,1,0:T(8,128)(2,1)} custom-call(bf16[8,512,128]{2,1,0:T(8,128)(2,1)S(1)} %get-tuple-element.1326.refs_0_, bf16[8,288,1024]{2,1,0:T(8,128)(2,1)} %get-tuple-element.1330.refs_1_, bf16[8,288,1024]{2,1,0:T(8,128)(2,1)} %get-tuple-element.1331.refs_2_, bf16[8,288,128]{2,1,0:T(8,128)(2,1)} %get-tuple-element.1332.refs_3_, ...), custom_call_target="tpu_custom_call" | custom-call | flops 402653184 | bytes 1250000 | tf_op jit(solution)/shard_map/while/body/combine/pallas_call | solution.py:1195
  382.7 20.7 %collective-permute-done.2.sum_x_ref = bf16[528,1024]{1,0:T(8,128)(2,1)S(1)} collective-permute-done((bf16[528,1024]{1,0:T(8,128)(2,1)S(1)}, bf16[528,1024]{1,0:T(8,128)(2,1)S(1)}, u32[]{:S(2)}, u32[]{:S(2)}) %collective-permute-start.2) | collective-permute-done | bytes 1081376 | tf_op jit(solution)/shard_map/while/body/ppermute | solution.py:512
  414.0 33.2 %all_to_all.126 = bf16[4,512,128]{2,1,0:T(8,128)(2,1)} all-to-all(bf16[4,512,128]{2,1,0:T(8,128)(2,1)} %get-tuple-element.1337), channel_id=1, replica_groups=mesh['sp'=4,'fsdp'=8] {'sp'}, dimensions={0} | all-to-all | bytes 1048576 | tf_op jit(solution)/shard_map/while/body/all_to_all | solution.py:1370
  451.4 21.9 %attend_back.8 = (f32[2048,256]{1,0:T(8,128)}, bf16[2048,128]{1,0:T(8,128)(2,1)}) custom-call(s32[4]{0:T(128)S(1)} %get-tuple-element.1510.low_ref, bf16[2048,256]{1,0:T(8,128)(2,1)} %get-tuple-element.1511.own_ref, bf16[2048,128]{1,0:T(8,128)(2,1)} %get-tuple-element.1512.halo_ref, s32[4,1,512]{2,1,0:T(1,128)S(1)} %get-tuple-element.1513.start_ref, ...), custom_call_target="tpu_custom_call" | custom-call | flops 3750000128 | bytes 750000 | tf_op jit(solution)/shard_map/while/body/attend_back/pallas_call | solution.py:822
  507.7 21.9 %attend_back.9 = (f32[2048,256]{1,0:T(8,128)}, bf16[2048,128]{1,0:T(8,128)(2,1)}) custom-call(s32[4]{0:T(128)S(1)} %get-tuple-element.1510.low_ref, bf16[2048,256]{1,0:T(8,128)(2,1)} %get-tuple-element.1516.own_ref, bf16[2048,128]{1,0:T(8,128)(2,1)} %get-tuple-element.1517.halo_ref, s32[4,1,512]{2,1,0:T(1,128)S(1)} %get-tuple-element.1513.start_ref, ...), custom_call_target="tpu_custom_call" | custom-call | flops 3750000128 | bytes 750000 | tf_op jit(solution)/shard_map/while/body/attend_back/pallas_call | solution.py:822
  572.6 42.6 %all-to-all-done.3.second_ref = bf16[4,512,256]{2,1,0:T(8,128)(2,1)} async-done(((bf16[4,512,256]{2,1,0:T(8,128)(2,1)}), bf16[4,512,256]{2,1,0:T(8,128)(2,1)}, u32[]{:S(2)}, u32[]{:S(2)}) %all-to-all-start.3) | async-done | bytes 1048608 | tf_op jit(solution)/shard_map/while/body/all_to_all | solution.py:1370
  615.2 13.2 %input_grads.4 = (bf16[512,1024]{1,0:T(8,128)(2,1)}, bf16[4,128,2176]{2,1,0:T(8,128)(2,1)}, bf16[4,128,2176]{2,1,0:T(8,128)(2,1)}) custom-call(s32[1]{0:T(128)} %get-tuple-element.1327.me_ref, bf16[512,1024]{1,0:T(8,128)(2,1)} %get-tuple-element.1520.tokens_ref, f32[512,128]{1,0:T(8,128)} %copy.60.cos_ref, f32[512,128]{1,0:T(8,128)} %broadcast_multiply_fusion.3.sin_ref, ...), custom_call_target="tpu_custom_call" | custom-call | flops 536870912 | bytes 1875000 | tf_op jit(solution)/shard_map/while/body/input_grads/pallas_call | solution.py:1339
  659.0 13.0 %collective-permute-done.18 = bf16[64,2176]{1,0:T(8,128)(2,1)S(1)} collective-permute-done((bf16[64,2176]{1,0:T(8,128)(2,1)S(1)}, bf16[64,2176]{1,0:T(8,128)(2,1)S(1)}, u32[]{:S(2)}, u32[]{:S(2)}) %collective-permute-start.18) | collective-permute-done | bytes 278560 | tf_op jit(solution)/shard_map/while/body/ppermute | solution.py:512
  701.9 34.9 %all-to-all-done.4 = bf16[4,32,3328]{2,1,0:T(8,128)(2,1)} async-done(((bf16[4,32,3328]{2,1,0:T(8,128)(2,1)}), bf16[4,32,3328]{2,1,0:T(8,128)(2,1)}, u32[]{:S(2)}, u32[]{:S(2)}) %all-to-all-start.4) | async-done | bytes 852000 | tf_op jit(solution)/shard_map/while/body/all_to_all | solution.py:1370
  749.9 41.8 %all-to-all-done.5 = bf16[4,32,3328]{2,1,0:T(8,128)(2,1)} async-done(((bf16[4,32,3328]{2,1,0:T(8,128)(2,1)}), bf16[4,32,3328]{2,1,0:T(8,128)(2,1)}, u32[]{:S(2)}, u32[]{:S(2)}) %all-to-all-start.5) | async-done | bytes 852000 | tf_op jit(solution)/shard_map/while/body/all_to_all | solution.py:1370
  802.1 15.6 %all-reduce.5.cloned.1.call-done = (bf16[6144,512]{1,0:T(8,128)(2,1)}, bf16[6144,512]{1,0:T(8,128)(2,1)}) async-done(((bf16[6144,512]{1,0:T(8,128)(2,1)}, bf16[6144,512]{1,0:T(8,128)(2,1)}), (bf16[6144,512]{1,0:T(8,128)(2,1)}, bf16[6144,512]{1,0:T(8,128)(2,1)})) %all-reduce.5.cloned.1.call-update) | async-done | bytes 12582928 | tf_op jit(solution)/shard_map/psum | solution.py:1466
  (342 shorter events, 348.0 us)
Async XLA Ops:
  11.0 38.6 %collective-permute-start.22 = (bf16[128,3200]{1,0:T(8,128)(2,1)S(1)}, bf16[128,3200]{1,0:T(8,128)(2,1)S(1)}, u32[]{:S(2)}, u32[]{:S(2)}) collective-permute-start(bf16[128,3200]{1,0:T(8,128)(2,1)S(1)} %concatenate.96.refs_0_), channel_id=1, source_target_pairs={{0,1},{1,0},{2,3},{3,2},{4,5},{5,4},{6,7},{7,6},{8,9},{9,8},{10,11... | collective-permute-start | bytes 2457608 | tf_op jit(solution)/shard_map/ppermute | solution.py:512
  58.1 32.9 %all-to-all-start.6 = ((bf16[4,512,256]{2,1,0:T(8,128)(2,1)}), bf16[4,512,256]{2,1,0:T(8,128)(2,1)}, u32[]{:S(2)}, u32[]{:S(2)}) async-start(bf16[4,512,256]{2,1,0:T(8,128)(2,1)} %get-tuple-element.639), calls=%async_computation.6 | async-start | bytes 2097152 | tf_op jit(solution)/shard_map/all_to_all | solution.py:1370
  90.9 30.5 %all-to-all-start.7 = ((bf16[4,512,256]{2,1,0:T(8,128)(2,1)}), bf16[4,512,256]{2,1,0:T(8,128)(2,1)}, u32[]{:S(2)}, u32[]{:S(2)}) async-start(bf16[4,512,256]{2,1,0:T(8,128)(2,1)} %get-tuple-element.644), calls=%async_computation.7 | async-start | bytes 2097152 | tf_op jit(solution)/shard_map/all_to_all | solution.py:1370
  98.4 41.0 %collective-permute-start.36 = (bf16[528,1024]{1,0:T(8,128)(2,1)}, bf16[528,1024]{1,0:T(8,128)(2,1)}, u32[]{:S(2)}, u32[]{:S(2)}) collective-permute-start(bf16[528,1024]{1,0:T(8,128)(2,1)} %copy-done.27), channel_id=1, source_target_pairs={{0,1},{1,0},{2,3},{3,2},{4,5},{5,4},{6,7},{7,6},{8,9},{9,8},{10,11... | collective-permute-start | bytes 3244040 | tf_op jit(solution)/shard_map/ppermute | solution.py:512
  100.5 39.0 %collective-permute-start.37 = (bf16[528,1024]{1,0:T(8,128)(2,1)S(1)}, bf16[528,1024]{1,0:T(8,128)(2,1)}, u32[]{:S(2)}, u32[]{:S(2)}) collective-permute-start(bf16[528,1024]{1,0:T(8,128)(2,1)S(1)} %collective-permute-done.33.refs_4_), channel_id=1, source_target_pairs={{0,1},{1,0},{2,3},{3,2},{4,5},{5,4},{6,7},{7,6},{8,9},{9,8},{10,11... | collective-permute-start | bytes 3244040 | tf_op jit(solution)/shard_map/ppermute | solution.py:512
  121.5 39.5 %all-to-all-start.8 = ((bf16[4,512,128]{2,1,0:T(8,128)(2,1)}), bf16[4,512,128]{2,1,0:T(8,128)(2,1)S(1)}, u32[]{:S(2)}, u32[]{:S(2)}) async-start(bf16[4,512,128]{2,1,0:T(8,128)(2,1)} %bitcast.13), calls=%async_computation.8 | async-start | bytes 1048576 | tf_op jit(solution)/shard_map/all_to_all | solution.py:1370
  133.1 27.9 %collective-permute-start.38 = (bf16[272,1024]{1,0:T(8,128)(2,1)S(1)}, bf16[272,1024]{1,0:T(8,128)(2,1)S(1)}, u32[]{:S(2)}, u32[]{:S(2)}) collective-permute-start(bf16[272,1024]{1,0:T(8,128)(2,1)S(1)} %slice.552), channel_id=1, source_target_pairs={{0,2},{1,3},{2,0},{3,1},{4,6},{5,7},{6,4},{7,5},{8,10},{9,11},{10,... | collective-permute-start | bytes 1671176 | tf_op jit(solution)/shard_map/ppermute | solution.py:512
  165.8 651.8 %all-reduce.5.cloned.1.call-start = ((), (), s32[]{:S(2)}) async-start(), calls=%async_computation.10 | async-start | bytes 25165824 | tf_op jit(solution)/shard_map/psum | solution.py:1466
  187.0 28.1 %collective-permute-start.43 = (bf16[528,1024]{1,0:T(8,128)(2,1)}, bf16[528,1024]{1,0:T(8,128)(2,1)S(1)}, u32[]{:S(2)}, u32[]{:S(2)}) collective-permute-start(bf16[528,1024]{1,0:T(8,128)(2,1)} %get-tuple-element.1393.refs_0_), channel_id=1, source_target_pairs={{0,2},{1,3},{2,0},{3,1},{4,6},{5,7},{6,4},{7,5},{8,10},{9,11},{10,... | collective-permute-start | bytes 3244040 | tf_op jit(solution)/shard_map/ppermute | solution.py:512
  190.5 26.7 %collective-permute-start.45 = (bf16[528,1024]{1,0:T(8,128)(2,1)}, bf16[528,1024]{1,0:T(8,128)(2,1)S(1)}, u32[]{:S(2)}, u32[]{:S(2)}) collective-permute-start(bf16[528,1024]{1,0:T(8,128)(2,1)} %get-tuple-element.1393.refs_0_), channel_id=1, source_target_pairs={{0,4},{1,5},{2,6},{3,7},{4,0},{5,1},{6,2},{7,3},{8,12},{9,13},{10,... | collective-permute-start | bytes 3244040 | tf_op jit(solution)/shard_map/ppermute | solution.py:512
  190.8 29.7 %collective-permute-start.42 = (bf16[528,1024]{1,0:T(8,128)(2,1)}, bf16[528,1024]{1,0:T(8,128)(2,1)S(1)}, u32[]{:S(2)}, u32[]{:S(2)}) collective-permute-start(bf16[528,1024]{1,0:T(8,128)(2,1)} %get-tuple-element.1393.refs_0_), channel_id=1, source_target_pairs={{0,1},{1,0},{2,3},{3,2},{4,5},{5,4},{6,7},{7,6},{8,9},{9,8},{10,11... | collective-permute-start | bytes 3244040 | tf_op jit(solution)/shard_map/ppermute | solution.py:512
  447.2 32.7 %all-to-all-start.1 = ((bf16[4,512,128]{2,1,0:T(8,128)(2,1)}), bf16[4,512,128]{2,1,0:T(8,128)(2,1)}, u32[]{:S(2)}, u32[]{:S(2)}) async-start(bf16[4,512,128]{2,1,0:T(8,128)(2,1)} %get-tuple-element.1350), calls=%async_computation.1 | async-start | bytes 1048576 | tf_op jit(solution)/shard_map/while/body/all_to_all | solution.py:1370
  486.8 50.5 %all-to-all-start.2 = ((bf16[4,512,256]{2,1,0:T(8,128)(2,1)}), bf16[4,512,256]{2,1,0:T(8,128)(2,1)}, u32[]{:S(2)}, u32[]{:S(2)}) async-start(bf16[4,512,256]{2,1,0:T(8,128)(2,1)} %bitcast.217), calls=%async_computation.2 | async-start | bytes 2097152 | tf_op jit(solution)/shard_map/while/body/all_to_all | solution.py:1370
  501.3 61.6 %collective-permute-start.12 = (bf16[4,128,1152]{2,1,0:T(8,128)(2,1)}, bf16[4,128,1152]{2,1,0:T(8,128)(2,1)}, u32[]{:S(2)}, u32[]{:S(2)}) collective-permute-start(bf16[4,128,1152]{2,1,0:T(8,128)(2,1)} %get-tuple-element.1363), channel_id=1, source_target_pairs={{0,1},{1,0},{2,3},{3,2},{4,5},{5,4},{6,7},{7,6},{8,9},{9,8},{10,11... | collective-permute-start | bytes 3538952 | tf_op jit(solution)/shard_map/while/body/ppermute | solution.py:512
  551.3 97.9 %collective-permute-start.5 = (bf16[4,512,1024]{2,1,0:T(8,128)(2,1)}, bf16[4,512,1024]{2,1,0:T(8,128)(2,1)}, u32[]{:S(2)}, u32[]{:S(2)}) collective-permute-start(bf16[4,512,1024]{2,1,0:T(8,128)(2,1)} %combine.18), channel_id=1, source_target_pairs={{0,1},{1,0},{2,3},{3,2},{4,5},{5,4},{6,7},{7,6},{8,9},{9,8},{10,11... | collective-permute-start | bytes 12582920 | tf_op jit(solution)/shard_map/while/body/ppermute | solution.py:512
  558.6 56.6 %all-to-all-start.3 = ((bf16[4,512,256]{2,1,0:T(8,128)(2,1)}), bf16[4,512,256]{2,1,0:T(8,128)(2,1)}, u32[]{:S(2)}, u32[]{:S(2)}) async-start(bf16[4,512,256]{2,1,0:T(8,128)(2,1)} %bitcast.216), calls=%async_computation.3 | async-start | bytes 2097152 | tf_op jit(solution)/shard_map/while/body/all_to_all | solution.py:1370
  564.8 63.8 %collective-permute-start.13 = (bf16[64,1152]{1,0:T(8,128)(2,1)}, bf16[64,1152]{1,0:T(8,128)(2,1)}, u32[]{:S(2)}, u32[]{:S(2)}) collective-permute-start(bf16[64,1152]{1,0:T(8,128)(2,1)} %get-tuple-element.1366), channel_id=1, source_target_pairs={{0,2},{1,3},{2,0},{3,1},{4,6},{5,7},{6,4},{7,5},{8,10},{9,11},{10,... | collective-permute-start | bytes 442376 | tf_op jit(solution)/shard_map/while/body/ppermute | solution.py:512
  568.2 69.2 %collective-permute-start.15 = (bf16[64,1152]{1,0:T(8,128)(2,1)}, bf16[64,1152]{1,0:T(8,128)(2,1)}, u32[]{:S(2)}, u32[]{:S(2)}) collective-permute-start(bf16[64,1152]{1,0:T(8,128)(2,1)} %get-tuple-element.1368), channel_id=1, source_target_pairs={{0,4},{1,5},{2,6},{3,7},{4,0},{5,1},{6,2},{7,3},{8,12},{9,13},{10,... | collective-permute-start | bytes 442376 | tf_op jit(solution)/shard_map/while/body/ppermute | solution.py:512
  652.1 42.2 %collective-permute-start.6 = (bf16[256,1024]{1,0:T(8,128)(2,1)}, bf16[256,1024]{1,0:T(8,128)(2,1)}, u32[]{:S(2)}, u32[]{:S(2)}) collective-permute-start(bf16[256,1024]{1,0:T(8,128)(2,1)} %get-tuple-element.1345), channel_id=1, source_target_pairs={{0,2},{1,3},{2,0},{3,1},{4,6},{5,7},{6,4},{7,5},{8,10},{9,11},{10,... | collective-permute-start | bytes 1572872 | tf_op jit(solution)/shard_map/while/body/ppermute | solution.py:512
  653.3 45.0 %collective-permute-start.8 = (bf16[256,1024]{1,0:T(8,128)(2,1)}, bf16[256,1024]{1,0:T(8,128)(2,1)}, u32[]{:S(2)}, u32[]{:S(2)}) collective-permute-start(bf16[256,1024]{1,0:T(8,128)(2,1)} %get-tuple-element.1347), channel_id=1, source_target_pairs={{0,4},{1,5},{2,6},{3,7},{4,0},{5,1},{6,2},{7,3},{8,12},{9,13},{10,... | collective-permute-start | bytes 1572872 | tf_op jit(solution)/shard_map/while/body/ppermute | solution.py:512
  688.8 48.0 %all-to-all-start.4 = ((bf16[4,32,3328]{2,1,0:T(8,128)(2,1)}), bf16[4,32,3328]{2,1,0:T(8,128)(2,1)}, u32[]{:S(2)}, u32[]{:S(2)}) async-start(bf16[4,32,3328]{2,1,0:T(8,128)(2,1)} %bitcast.218), calls=%async_computation.4 | async-start | bytes 1703936 | tf_op jit(solution)/shard_map/while/body/all_to_all | solution.py:1370
  697.1 47.9 %collective-permute-start.7 = (bf16[512,1024]{1,0:T(8,128)(2,1)}, bf16[512,1024]{1,0:T(8,128)(2,1)}, u32[]{:S(2)}, u32[]{:S(2)}) collective-permute-start(bf16[512,1024]{1,0:T(8,128)(2,1)} %pad_maximum_fusion.21), channel_id=1, source_target_pairs={{0,4},{1,5},{2,6},{3,7},{4,0},{5,1},{6,2},{7,3},{8,12},{9,13},{10,... | collective-permute-start | bytes 3145736 | tf_op jit(solution)/shard_map/while/body/ppermute | solution.py:512
  700.6 44.4 %collective-permute-start.9 = (bf16[512,1024]{1,0:T(8,128)(2,1)}, bf16[512,1024]{1,0:T(8,128)(2,1)}, u32[]{:S(2)}, u32[]{:S(2)}) collective-permute-start(bf16[512,1024]{1,0:T(8,128)(2,1)} %pad_maximum_fusion.22), channel_id=1, source_target_pairs={{0,2},{1,3},{2,0},{3,1},{4,6},{5,7},{6,4},{7,5},{8,10},{9,11},{10,... | collective-permute-start | bytes 3145736 | tf_op jit(solution)/shard_map/while/body/ppermute | solution.py:512
  740.7 51.0 %all-to-all-start.5 = ((bf16[4,32,3328]{2,1,0:T(8,128)(2,1)}), bf16[4,32,3328]{2,1,0:T(8,128)(2,1)}, u32[]{:S(2)}, u32[]{:S(2)}) async-start(bf16[4,32,3328]{2,1,0:T(8,128)(2,1)} %tile.69), calls=%async_computation.5 | async-start | bytes 1703936 | tf_op jit(solution)/shard_map/while/body/all_to_all | solution.py:1370
  (91 other events, 1554.0 us)
Sparse Core Ops, SparseCore 0:
  290.1 527.5 all-reduce.4

commit v4 on v3

--- a/solution.py
+++ b/solution.py
@@ -1377,6 +1377,13 @@
     return across(jnp.tile(quarter, (4, 1)))
 
 
+def sum_line(value, seq):
+    outer = (seq == 0) | (seq == 3)
+    value = add_low(value, lax.ppermute(value, "sp", ((0, 1), (3, 2))))
+    value = add_low(value, lax.ppermute(value, "sp", ((1, 2), (2, 1))))
+    return jnp.where(outer, lax.ppermute(value, "sp", ((1, 0), (2, 3))), value)
+
+
 def fast_local(
     tokens, documents, expert_routes, drop_rank, norm1_gain, query_weight, key_weight,
     value_weight, out_weight, norm2_gain, router_weight, gate_weight, up_weight, down_weight,
@@ -1520,21 +1527,37 @@
 
         out_shard = sum(term.astype(F32) for term in out_sums).astype(BF)
         in_shard = sum(term.astype(F32) for term in in_sums).astype(BF)
-        shards = sum_shared(jnp.concatenate([in_shard, out_shard], axis=1))
-        return (output, input_grad, shards)
+        in_total = sum_shared(in_shard).astype(F32)
+        out_total = sum_line(out_shard, seq).astype(F32)
+        return (
+            output,
+            input_grad,
+            in_total[:, 2048],
+            in_total[:, 0:1024],
+            in_total[:, 1024:1536],
+            in_total[:, 1536:2048],
+            out_total[:, 0:1024],
+            out_total[:, 1056],
+            out_total[:, 1024:1056],
+        )
 
     rounds = 1 + (documents[0] > 0).astype(jnp.int32)
-    output, input_grad, shards = lax.fori_loop(
+    results = lax.fori_loop(
         0,
         rounds,
         finish,
         (
             jnp.zeros((512, 1024), BF),
             jnp.zeros((512, 1024), BF),
-            jnp.zeros((128, 3328), BF),
+            jnp.zeros((128,), F32),
+            jnp.zeros((128, 1024), F32),
+            jnp.zeros((128, 512), F32),
+            jnp.zeros((128, 512), F32),
+            jnp.zeros((128, 1024), F32),
+            jnp.zeros((128,), F32),
+            jnp.zeros((128, 32), F32),
         ),
     )
-    in_shard, out_shard = shards[:, 0:2176], shards[:, 2176:3328]
     sums_of_parts = [
         total[first : first + 3072] for total in sums_of_parts for first in (0, 3072)
     ]
@@ -1548,18 +1571,7 @@
             ]
         ).astype(F32),
     ]
-    return (
-        output,
-        input_grad,
-        in_shard[:, 2048].astype(F32),
-        in_shard[:, 0:1024].astype(F32),
-        in_shard[:, 1024:1536].astype(F32),
-        in_shard[:, 1536:2048].astype(F32),
-        out_shard[:, 0:1024].astype(F32),
-        out_shard[:, 1056].astype(F32),
-        out_shard[:, 1024:1056].astype(F32),
-        *stacked,
-    )
+    return (*results, *stacked)
 
 
 def solution(mesh):

time: 853 us -> 847 us (level)
  waiting for transfers between devices: 276 us -> 251 us
  loops' own time: 26.7 us -> 3.09 us
  starting transfers between devices: 114 us -> 137 us
  Pallas kernels: 246 us -> 259 us
    all_to_all x9, waiting for transfers between devices: 141 us -> 85.2 us  [across(): return lax.all_to_all(values, 'sp', split_axis=0, concat_axis=0, tiled=True)]
    psum x1, waiting for transfers between devices: 15.6 us -> 46.9 us  [fast_local(): sums_of_parts = lax.psum(parts, 'sp')]
    another operation x1, loops' own time: 26.7 us -> 3.09 us  [fast_local(): lax.fori_loop(0, rounds, finish, (jnp.zeros((512, 1024), BF), jnp.zeros((...]
    ppermute x47, starting transfers between devices: 63.3 us -> 75.3 us  [flip(): lax.ppermute(value, 'fsdp', [(place, place ^ bit) for place in range(8)])]
  transfers between devices with their start and end apart: 61 -> 64, of which waited for: 28 -> 25; matrix products, arithmetic and copies ran while one was open for 12% -> 13% of each run, Pallas kernels for 21% -> 23%
where the time goes in v4:
time: 847 us; the launch traced here: 838 us
  Pallas kernels  259 us (31%)
  waiting for transfers between devices  251 us (30%)
  starting transfers between devices  137 us (16%)
  other arithmetic  78.9 us (9%)
  local copies, waits for them, and re-layouts  58 us (7%)
  blocking collectives  35.8 us (4%)
  between operations  15.8 us (2%)
    ppermute x47, waiting for transfers between devices, flip(): lax.ppermute(value, 'fsdp', [(place, place ^ bit) for place in range(8)])  114 us
    all_to_all x9, waiting for transfers between devices, across(): return lax.all_to_all(values, 'sp', split_axis=0, concat_axis=0, tiled=True)  85.2 us
    ppermute x47, starting transfers between devices, flip(): lax.ppermute(value, 'fsdp', [(place, place ^ bit) for place in range(8)])  75.3 us
    pallas_call x2, Pallas kernels, attend_back(): pl.pallas_call(attend_back_kernel, out_shape=(shaped((2048, 256), F32), s...  51.9 us
    pallas_call x2, Pallas kernels, expert_grads(): pl.pallas_call(expert_grad_kernel, out_shape=(shaped((8, 144 * count, 102...  47.1 us
    psum x1, waiting for transfers between devices, fast_local(): sums_of_parts = lax.psum(parts, 'sp')  46.9 us
    all_to_all x9, starting transfers between devices, across(): return lax.all_to_all(values, 'sp', split_axis=0, concat_axis=0, tiled=True)  45.5 us
    all_to_all x1, blocking collectives, across(): return lax.all_to_all(values, 'sp', split_axis=0, concat_axis=0, tiled=True)  35.8 us
  transfers between devices with their start and end apart: 64, of which 25 were waited for; matrix products, arithmetic and copies ran while one was open for 13% of the time, Pallas kernels for 23%

profile of v4, /device:TPU:0, one launch (start us, length us, event | category | flops | bytes accessed | tf_op | source)
XLA Modules:
  0.0 837.9 jit_solution(4724005595424905985)
XLA Ops:
  23.9 10.5 %collective-permute-done.28.refs_4_ = bf16[128,3200]{1,0:T(8,128)(2,1)S(1)} collective-permute-done((bf16[128,3200]{1,0:T(8,128)(2,1)S(1)}, bf16[128,3200]{1,0:T(8,128)(2,1)S(1)}, u32[]{:S(2)}, u32[]{:S(2)}) %collective-permute-start.28) | collective-permute-done | bytes 819232 | tf_op jit(solution)/shard_map/ppermute | solution.py:512
  66.7 23.0 %collective-permute-done.35.refs_2_ = bf16[528,1024]{1,0:T(8,128)(2,1)S(1)} collective-permute-done((bf16[528,1024]{1,0:T(8,128)(2,1)S(1)}, bf16[528,1024]{1,0:T(8,128)(2,1)S(1)}, u32[]{:S(2)}, u32[]{:S(2)}) %collective-permute-start.35) | collective-permute-done | bytes 1081376 | tf_op jit(solution)/shard_map/ppermute | solution.py:512
  102.8 15.6 %attend.2 = (bf16[2048,128]{1,0:T(8,128)(2,1)}, f32[8,2048]{1,0:T(8,128)}) custom-call(s32[4]{0:T(128)} %get-tuple-element.1176.low_ref, bf16[2048,256]{1,0:T(8,128)(2,1)} %bitcast.11.own_ref, bf16[2048,128]{1,0:T(8,128)(2,1)S(1)} %collective-permute-done.37.halo_ref, s32[4,1,512]{2,1,0:T(1,128)S(1)} %bitcast.231), custom_call_target="tpu_custom_call" | custom-call | flops 1500000000 | bytes 375000 | tf_op jit(solution)/shard_map/attend/pallas_call | solution.py:730
  148.4 15.8 %attend.3 = (bf16[2048,128]{1,0:T(8,128)(2,1)}, f32[8,2048]{1,0:T(8,128)}) custom-call(s32[4]{0:T(128)} %get-tuple-element.1176.low_ref, bf16[2048,256]{1,0:T(8,128)(2,1)} %bitcast.12.own_ref, bf16[2048,128]{1,0:T(8,128)(2,1)} %collective-permute-done.38.halo_ref, s32[4,1,512]{2,1,0:T(1,128)S(1)} %bitcast.232), custom_call_target="tpu_custom_call" | custom-call | flops 1500000000 | bytes 375000 | tf_op jit(solution)/shard_map/attend/pallas_call | solution.py:730
  193.8 24.0 %collective-permute-done.46.refs_2_ = bf16[528,1024]{1,0:T(8,128)(2,1)S(1)} collective-permute-done((bf16[528,1024]{1,0:T(8,128)(2,1)}, bf16[528,1024]{1,0:T(8,128)(2,1)S(1)}, u32[]{:S(2)}, u32[]{:S(2)}) %collective-permute-start.46) | collective-permute-done | bytes 1081376 | tf_op jit(solution)/shard_map/ppermute | solution.py:512
  223.9 9.4 %pick_rows.2 = (bf16[6,576,1024]{2,1,0:T(8,128)(2,1)}, bf16[6,576,128]{2,1,0:T(8,128)(2,1)}, bf16[6,512,128]{2,1,0:T(8,128)(2,1)}) custom-call(s32[1]{0:T(128)} %bitcast.1.me_ref, f32[6,4,512]{2,1,0:T(4,128)} %get-tuple-element.736.slots_ref, bf16[528,1024]{1,0:T(8,128)(2,1)} %get-tuple-element.1631.refs_0_, bf16[528,1024]{1,0:T(8,128)(2,1)} %copy-done.24, ...), custom_call_target="tpu_custom_call" | custom-call | flops 452984832 | bytes 1800000 | tf_op jit(solution)/shard_map/pick_rows/pallas_call | solution.py:1014
  244.4 23.7 %expert_grads.2 = (bf16[8,288,1024]{2,1,0:T(8,128)(2,1)}, bf16[8,288,512]{2,1,0:T(8,128)(2,1)}, bf16[6144,512]{1,0:T(8,128)(2,1)}) custom-call(bf16[6,576,1024]{2,1,0:T(8,128)(2,1)} %get-tuple-element.744.refs_0_, bf16[2,576,1024]{2,1,0:T(8,128)(2,1)} %get-tuple-element.748.refs_1_, bf16[6,576,1024]{2,1,0:T(8,128)(2,1)} %get-tuple-element.1622.refs_2_, ...), custom_call_target="tpu_custom_call" | custom-call | flops 2000000000 | bytes 3750000 | tf_op jit(solution)/shard_map/expert_grads/pallas_call | solution.py:1080
  268.1 23.4 %expert_grads.3 = (bf16[8,288,1024]{2,1,0:T(8,128)(2,1)}, bf16[8,288,512]{2,1,0:T(8,128)(2,1)}, bf16[6144,512]{1,0:T(8,128)(2,1)}) custom-call(bf16[6,576,1024]{2,1,0:T(8,128)(2,1)} %get-tuple-element.744.refs_0_, bf16[2,576,1024]{2,1,0:T(8,128)(2,1)} %get-tuple-element.748.refs_1_, bf16[6,576,1024]{2,1,0:T(8,128)(2,1)} %get-tuple-element.1622.refs_2_, ...), custom_call_target="tpu_custom_call" | custom-call | flops 2000000000 | bytes 3750000 | tf_op jit(solution)/shard_map/expert_grads/pallas_call | solution.py:1080
  298.6 465.3 %while.29 = (s32[]{:T(128)}, bf16[512,1024]{1,0:T(8,128)(2,1)}, bf16[512,1024]{1,0:T(8,128)(2,1)}, f32[128]{0:T(128)}, f32[128,1024]{1,0:T(8,128)}, /*index=5*/f...) while((s32[]{:T(128)}, bf16[512,1024]{1,0:T(8,128)(2,1)}, ...), condition=%wide.region_6.7_spmd.clone, body=%wide.region_4.6_spmd.clone.sunk | while | flops 11965116416 | bytes 249158064 | solution.py:1545
  298.8 13.9 %expert_rows.8 = (bf16[8,288,1024]{2,1,0:T(8,128)(2,1)}, bf16[8,288,1024]{2,1,0:T(8,128)(2,1)}, bf16[8,288,128]{2,1,0:T(8,128)(2,1)}) custom-call(s32[1]{0:T(128)} %get-tuple-element.1557.me_ref, bf16[8,288,1024]{2,1,0:T(8,128)(2,1)} %get-tuple-element.1736.lin_ref, bf16[8,288,512]{2,1,0:T(8,128)(2,1)} %get-tuple-element.1737.inner_ref, ...), custom_call_target="tpu_custom_call" | custom-call | flops 1000000000 | bytes 3500000 | tf_op jit(solution)/shard_map/while/body/expert_rows/pallas_call | solution.py:1133
  312.7 13.9 %expert_rows.9 = (bf16[8,288,1024]{2,1,0:T(8,128)(2,1)}, bf16[8,288,1024]{2,1,0:T(8,128)(2,1)}, bf16[8,288,128]{2,1,0:T(8,128)(2,1)}) custom-call(s32[1]{0:T(128)} %get-tuple-element.1557.me_ref, bf16[8,288,1024]{2,1,0:T(8,128)(2,1)} %get-tuple-element.1743.lin_ref, bf16[8,288,512]{2,1,0:T(8,128)(2,1)} %get-tuple-element.1744.inner_ref, ...), custom_call_target="tpu_custom_call" | custom-call | flops 1000000000 | bytes 3500000 | tf_op jit(solution)/shard_map/while/body/expert_rows/pallas_call | solution.py:1133
  335.5 9.0 %combine.17 = bf16[4,528,1024]{2,1,0:T(8,128)(2,1)} custom-call(bf16[8,512,128]{2,1,0:T(8,128)(2,1)S(1)} %get-tuple-element.1556.refs_0_, bf16[8,288,1024]{2,1,0:T(8,128)(2,1)} %get-tuple-element.1560.refs_1_, bf16[8,288,1024]{2,1,0:T(8,128)(2,1)} %get-tuple-element.1561.refs_2_, bf16[8,288,128]{2,1,0:T(8,128)(2,1)} %get-tuple-element.1562.refs_3_, ...), custom_call_target="tpu_custom_call" | custom-call | flops 402653184 | bytes 1250000 | tf_op jit(solution)/shard_map/while/body/combine/pallas_call | solution.py:1195
  365.3 20.8 %collective-permute-done.2.sum_x_ref = bf16[528,1024]{1,0:T(8,128)(2,1)S(1)} collective-permute-done((bf16[528,1024]{1,0:T(8,128)(2,1)S(1)}, bf16[528,1024]{1,0:T(8,128)(2,1)S(1)}, u32[]{:S(2)}, u32[]{:S(2)}) %collective-permute-start.2) | collective-permute-done | bytes 1081376 | tf_op jit(solution)/shard_map/while/body/ppermute | solution.py:512
  396.5 35.8 %all_to_all.123 = bf16[4,512,128]{2,1,0:T(8,128)(2,1)} all-to-all(bf16[4,512,128]{2,1,0:T(8,128)(2,1)} %get-tuple-element.1567), channel_id=1, replica_groups=mesh['sp'=4,'fsdp'=8] {'sp'}, dimensions={0} | all-to-all | bytes 1048576 | tf_op jit(solution)/shard_map/while/body/all_to_all | solution.py:1370
  436.5 25.9 %attend_back.8 = (f32[2048,256]{1,0:T(8,128)}, bf16[2048,128]{1,0:T(8,128)(2,1)}) custom-call(s32[4]{0:T(128)S(1)} %get-tuple-element.1762.low_ref, bf16[2048,256]{1,0:T(8,128)(2,1)} %get-tuple-element.1763.own_ref, bf16[2048,128]{1,0:T(8,128)(2,1)} %get-tuple-element.1764.halo_ref, s32[4,1,512]{2,1,0:T(1,128)S(1)} %get-tuple-element.1765.start_ref, ...), custom_call_target="tpu_custom_call" | custom-call | flops 3750000128 | bytes 750000 | tf_op jit(solution)/shard_map/while/body/attend_back/pallas_call | solution.py:822
  501.4 26.0 %attend_back.9 = (f32[2048,256]{1,0:T(8,128)}, bf16[2048,128]{1,0:T(8,128)(2,1)}) custom-call(s32[4]{0:T(128)S(1)} %get-tuple-element.1762.low_ref, bf16[2048,256]{1,0:T(8,128)(2,1)} %get-tuple-element.1768.own_ref, bf16[2048,128]{1,0:T(8,128)(2,1)} %get-tuple-element.1769.halo_ref, s32[4,1,512]{2,1,0:T(1,128)S(1)} %get-tuple-element.1765.start_ref, ...), custom_call_target="tpu_custom_call" | custom-call | flops 3750000128 | bytes 750000 | tf_op jit(solution)/shard_map/while/body/attend_back/pallas_call | solution.py:822
  531.2 11.3 %collective-permute-start.18 = (bf16[64,1152]{1,0:T(8,128)(2,1)}, bf16[64,1152]{1,0:T(8,128)(2,1)}, u32[]{:S(2)}, u32[]{:S(2)}) collective-permute-start(bf16[64,1152]{1,0:T(8,128)(2,1)} %get-tuple-element.1604), channel_id=1, source_target_pairs={{0,2},{1,3},{2,0},{3,1},{4,6},{5,7},{6,4},{7,5},{8,10},{9,11},{10,... | collective-permute-start | bytes 442376 | tf_op jit(solution)/shard_map/while/body/ppermute | solution.py:512
  569.5 29.9 %all-to-all-done.3.second_ref = bf16[4,512,256]{2,1,0:T(8,128)(2,1)} async-done(((bf16[4,512,256]{2,1,0:T(8,128)(2,1)}), bf16[4,512,256]{2,1,0:T(8,128)(2,1)}, u32[]{:S(2)}, u32[]{:S(2)}) %all-to-all-start.3) | async-done | bytes 1048608 | tf_op jit(solution)/shard_map/while/body/all_to_all | solution.py:1370
  599.4 13.1 %input_grads.4 = (bf16[512,1024]{1,0:T(8,128)(2,1)}, bf16[4,128,2176]{2,1,0:T(8,128)(2,1)}, bf16[4,128,2176]{2,1,0:T(8,128)(2,1)}) custom-call(s32[1]{0:T(128)} %get-tuple-element.1557.me_ref, bf16[512,1024]{1,0:T(8,128)(2,1)} %get-tuple-element.1772.tokens_ref, f32[512,128]{1,0:T(8,128)} %copy.77.cos_ref, f32[512,128]{1,0:T(8,128)} %broadcast_multiply_fusion.3.sin_ref, ...), custom_call_target="tpu_custom_call" | custom-call | flops 536870912 | bytes 1875000 | tf_op jit(solution)/shard_map/while/body/input_grads/pallas_call | solution.py:1339
  655.6 8.8 %collective-permute-done.13 = bf16[64,2176]{1,0:T(8,128)(2,1)S(1)} collective-permute-done((bf16[64,2176]{1,0:T(8,128)(2,1)S(1)}, bf16[64,2176]{1,0:T(8,128)(2,1)S(1)}, u32[]{:S(2)}, u32[]{:S(2)}) %collective-permute-start.13) | collective-permute-done | bytes 278560 | tf_op jit(solution)/shard_map/while/body/ppermute | solution.py:512
  670.7 9.5 %collective-permute-done.14 = bf16[128,2176]{1,0:T(8,128)(2,1)S(1)} collective-permute-done((bf16[128,2176]{1,0:T(8,128)(2,1)S(1)}, bf16[128,2176]{1,0:T(8,128)(2,1)S(1)}, u32[]{:S(2)}, u32[]{:S(2)}) %collective-permute-start.14) | collective-permute-done | bytes 557088 | tf_op jit(solution)/shard_map/while/body/ppermute | solution.py:512
  697.4 23.8 %all-to-all-done.4 = bf16[4,32,2176]{2,1,0:T(8,128)(2,1)} async-done(((bf16[4,32,2176]{2,1,0:T(8,128)(2,1)}), bf16[4,32,2176]{2,1,0:T(8,128)(2,1)}, u32[]{:S(2)}, u32[]{:S(2)}) %all-to-all-start.4) | async-done | bytes 557088 | tf_op jit(solution)/shard_map/while/body/all_to_all | solution.py:1370
  734.9 23.1 %all-to-all-done.5 = bf16[4,32,2176]{2,1,0:T(8,128)(2,1)} async-done(((bf16[4,32,2176]{2,1,0:T(8,128)(2,1)}), bf16[4,32,2176]{2,1,0:T(8,128)(2,1)}, u32[]{:S(2)}, u32[]{:S(2)}) %all-to-all-start.5) | async-done | bytes 557088 | tf_op jit(solution)/shard_map/while/body/all_to_all | solution.py:1370
  765.5 46.9 %all-reduce.5.cloned.1.call-done = (bf16[6144,512]{1,0:T(8,128)(2,1)}, bf16[6144,512]{1,0:T(8,128)(2,1)}) async-done(((bf16[6144,512]{1,0:T(8,128)(2,1)}, bf16[6144,512]{1,0:T(8,128)(2,1)}), (bf16[6144,512]{1,0:T(8,128)(2,1)}, bf16[6144,512]{1,0:T(8,128)(2,1)})) %all-reduce.5.cloned.1.call-update) | async-done | bytes 12582928 | tf_op jit(solution)/shard_map/psum | solution.py:1473
  (339 shorter events, 361.7 us)
Async XLA Ops:
  11.0 38.6 %collective-permute-start.25 = (bf16[128,3200]{1,0:T(8,128)(2,1)S(1)}, bf16[128,3200]{1,0:T(8,128)(2,1)S(1)}, u32[]{:S(2)}, u32[]{:S(2)}) collective-permute-start(bf16[128,3200]{1,0:T(8,128)(2,1)S(1)} %concatenate.90.refs_0_), channel_id=1, source_target_pairs={{0,1},{1,0},{2,3},{3,2},{4,5},{5,4},{6,7},{7,6},{8,9},{9,8},{10,11... | collective-permute-start | bytes 2457608 | tf_op jit(solution)/shard_map/ppermute | solution.py:512
  58.1 32.9 %all-to-all-start.6 = ((bf16[4,512,256]{2,1,0:T(8,128)(2,1)}), bf16[4,512,256]{2,1,0:T(8,128)(2,1)}, u32[]{:S(2)}, u32[]{:S(2)}) async-start(bf16[4,512,256]{2,1,0:T(8,128)(2,1)} %get-tuple-element.709), calls=%async_computation.6 | async-start | bytes 2097152 | tf_op jit(solution)/shard_map/all_to_all | solution.py:1370
  90.9 30.5 %all-to-all-start.7 = ((bf16[4,512,256]{2,1,0:T(8,128)(2,1)}), bf16[4,512,256]{2,1,0:T(8,128)(2,1)}, u32[]{:S(2)}, u32[]{:S(2)}) async-start(bf16[4,512,256]{2,1,0:T(8,128)(2,1)} %get-tuple-element.714), calls=%async_computation.7 | async-start | bytes 2097152 | tf_op jit(solution)/shard_map/all_to_all | solution.py:1370
  98.4 41.9 %collective-permute-start.39 = (bf16[528,1024]{1,0:T(8,128)(2,1)}, bf16[528,1024]{1,0:T(8,128)(2,1)}, u32[]{:S(2)}, u32[]{:S(2)}) collective-permute-start(bf16[528,1024]{1,0:T(8,128)(2,1)} %copy-done.20), channel_id=1, source_target_pairs={{0,1},{1,0},{2,3},{3,2},{4,5},{5,4},{6,7},{7,6},{8,9},{9,8},{10,11... | collective-permute-start | bytes 3244040 | tf_op jit(solution)/shard_map/ppermute | solution.py:512
  100.5 39.9 %collective-permute-start.40 = (bf16[528,1024]{1,0:T(8,128)(2,1)S(1)}, bf16[528,1024]{1,0:T(8,128)(2,1)}, u32[]{:S(2)}, u32[]{:S(2)}) collective-permute-start(bf16[528,1024]{1,0:T(8,128)(2,1)S(1)} %collective-permute-done.36.refs_4_), channel_id=1, source_target_pairs={{0,1},{1,0},{2,3},{3,2},{4,5},{5,4},{6,7},{7,6},{8,9},{9,8},{10,11... | collective-permute-start | bytes 3244040 | tf_op jit(solution)/shard_map/ppermute | solution.py:512
  121.5 42.7 %all-to-all-start.8 = ((bf16[4,512,128]{2,1,0:T(8,128)(2,1)}), bf16[4,512,128]{2,1,0:T(8,128)(2,1)S(1)}, u32[]{:S(2)}, u32[]{:S(2)}) async-start(bf16[4,512,128]{2,1,0:T(8,128)(2,1)} %bitcast.13), calls=%async_computation.8 | async-start | bytes 1048576 | tf_op jit(solution)/shard_map/all_to_all | solution.py:1370
  133.0 31.2 %collective-permute-start.41 = (bf16[272,1024]{1,0:T(8,128)(2,1)S(1)}, bf16[272,1024]{1,0:T(8,128)(2,1)S(1)}, u32[]{:S(2)}, u32[]{:S(2)}) collective-permute-start(bf16[272,1024]{1,0:T(8,128)(2,1)S(1)} %slice.564), channel_id=1, source_target_pairs={{0,2},{1,3},{2,0},{3,1},{4,6},{5,7},{6,4},{7,5},{8,10},{9,11},{10,... | collective-permute-start | bytes 1671176 | tf_op jit(solution)/shard_map/ppermute | solution.py:512
  169.3 643.1 %all-reduce.5.cloned.1.call-start = ((), (), s32[]{:S(2)}) async-start(), calls=%async_computation.10 | async-start | bytes 25165824 | tf_op jit(solution)/shard_map/psum | solution.py:1473
  191.1 26.8 %collective-permute-start.46 = (bf16[528,1024]{1,0:T(8,128)(2,1)}, bf16[528,1024]{1,0:T(8,128)(2,1)S(1)}, u32[]{:S(2)}, u32[]{:S(2)}) collective-permute-start(bf16[528,1024]{1,0:T(8,128)(2,1)} %get-tuple-element.1631.refs_0_), channel_id=1, source_target_pairs={{0,2},{1,3},{2,0},{3,1},{4,6},{5,7},{6,4},{7,5},{8,10},{9,11},{10,... | collective-permute-start | bytes 3244040 | tf_op jit(solution)/shard_map/ppermute | solution.py:512
  193.8 28.1 %collective-permute-start.45 = (bf16[528,1024]{1,0:T(8,128)(2,1)}, bf16[528,1024]{1,0:T(8,128)(2,1)S(1)}, u32[]{:S(2)}, u32[]{:S(2)}) collective-permute-start(bf16[528,1024]{1,0:T(8,128)(2,1)} %get-tuple-element.1631.refs_0_), channel_id=1, source_target_pairs={{0,1},{1,0},{2,3},{3,2},{4,5},{5,4},{6,7},{7,6},{8,9},{9,8},{10,11... | collective-permute-start | bytes 3244040 | tf_op jit(solution)/shard_map/ppermute | solution.py:512
  432.4 30.1 %all-to-all-start.1 = ((bf16[4,512,128]{2,1,0:T(8,128)(2,1)}), bf16[4,512,128]{2,1,0:T(8,128)(2,1)}, u32[]{:S(2)}, u32[]{:S(2)}) async-start(bf16[4,512,128]{2,1,0:T(8,128)(2,1)} %get-tuple-element.1580), calls=%async_computation.1 | async-start | bytes 1048576 | tf_op jit(solution)/shard_map/while/body/all_to_all | solution.py:1370
  468.0 29.0 %collective-permute-start.17 = (bf16[4,128,1152]{2,1,0:T(8,128)(2,1)}, bf16[4,128,1152]{2,1,0:T(8,128)(2,1)}, u32[]{:S(2)}, u32[]{:S(2)}) collective-permute-start(bf16[4,128,1152]{2,1,0:T(8,128)(2,1)} %get-tuple-element.1601), channel_id=1, source_target_pairs={{0,1},{1,0},{2,3},{3,2},{4,5},{5,4},{6,7},{7,6},{8,9},{9,8},{10,11... | collective-permute-start | bytes 3538952 | tf_op jit(solution)/shard_map/while/body/ppermute | solution.py:512
  471.9 56.4 %all-to-all-start.2 = ((bf16[4,512,256]{2,1,0:T(8,128)(2,1)}), bf16[4,512,256]{2,1,0:T(8,128)(2,1)}, u32[]{:S(2)}, u32[]{:S(2)}) async-start(bf16[4,512,256]{2,1,0:T(8,128)(2,1)} %bitcast.219), calls=%async_computation.2 | async-start | bytes 2097152 | tf_op jit(solution)/shard_map/while/body/all_to_all | solution.py:1370
  490.2 149.4 %collective-permute-start.5 = (bf16[4,512,1024]{2,1,0:T(8,128)(2,1)}, bf16[4,512,1024]{2,1,0:T(8,128)(2,1)}, u32[]{:S(2)}, u32[]{:S(2)}) collective-permute-start(bf16[4,512,1024]{2,1,0:T(8,128)(2,1)} %combine.18), channel_id=1, source_target_pairs={{0,1},{1,0},{2,3},{3,2},{4,5},{5,4},{6,7},{7,6},{8,9},{9,8},{10,11... | collective-permute-start | bytes 12582920 | tf_op jit(solution)/shard_map/while/body/ppermute | solution.py:512
  547.1 52.3 %all-to-all-start.3 = ((bf16[4,512,256]{2,1,0:T(8,128)(2,1)}), bf16[4,512,256]{2,1,0:T(8,128)(2,1)}, u32[]{:S(2)}, u32[]{:S(2)}) async-start(bf16[4,512,256]{2,1,0:T(8,128)(2,1)} %bitcast.218), calls=%async_computation.3 | async-start | bytes 2097152 | tf_op jit(solution)/shard_map/while/body/all_to_all | solution.py:1370
  554.2 65.9 %collective-permute-start.19 = (bf16[128,1152]{1,0:T(8,128)(2,1)}, bf16[128,1152]{1,0:T(8,128)(2,1)}, u32[]{:S(2)}, u32[]{:S(2)}) collective-permute-start(bf16[128,1152]{1,0:T(8,128)(2,1)} %pad_maximum_fusion.23), channel_id=1, source_target_pairs={{0,4},{1,5},{2,6},{3,7},{4,0},{5,1},{6,2},{7,3},{8,12},{9,13},{10,... | collective-permute-start | bytes 884744 | tf_op jit(solution)/shard_map/while/body/ppermute | solution.py:512
  561.4 58.8 %collective-permute-start.21 = (bf16[128,1152]{1,0:T(8,128)(2,1)}, bf16[128,1152]{1,0:T(8,128)(2,1)}, u32[]{:S(2)}, u32[]{:S(2)}) collective-permute-start(bf16[128,1152]{1,0:T(8,128)(2,1)} %pad_maximum_fusion.24), channel_id=1, source_target_pairs={{0,2},{1,3},{2,0},{3,1},{4,6},{5,7},{6,4},{7,5},{8,10},{9,11},{10,... | collective-permute-start | bytes 884744 | tf_op jit(solution)/shard_map/while/body/ppermute | solution.py:512
  612.5 38.2 %collective-permute-start.12 = (bf16[4,128,2176]{2,1,0:T(8,128)(2,1)}, bf16[4,128,2176]{2,1,0:T(8,128)(2,1)}, u32[]{:S(2)}, u32[]{:S(2)}) collective-permute-start(bf16[4,128,2176]{2,1,0:T(8,128)(2,1)} %get-tuple-element.1591), channel_id=1, source_target_pairs={{0,1},{1,0},{2,3},{3,2},{4,5},{5,4},{6,7},{7,6},{8,9},{9,8},{10,11... | collective-permute-start | bytes 6684680 | tf_op jit(solution)/shard_map/while/body/ppermute | solution.py:512
  638.0 56.2 %collective-permute-start.23 = (bf16[128,1152]{1,0:T(8,128)(2,1)}, bf16[128,1152]{1,0:T(8,128)(2,1)}, u32[]{:S(2)}, u32[]{:S(2)}) collective-permute-start(bf16[128,1152]{1,0:T(8,128)(2,1)} %add_convert_fusion.22), channel_id=1, source_target_pairs={{8,16},{16,8},{9,17},{17,9},{10,18},{18,10},{11,19},{19,11},{12,20... | collective-permute-start | bytes 884744 | tf_op jit(solution)/shard_map/while/body/ppermute | solution.py:1383
  668.0 62.7 %collective-permute-start.7 = (bf16[512,1024]{1,0:T(8,128)(2,1)}, bf16[512,1024]{1,0:T(8,128)(2,1)}, u32[]{:S(2)}, u32[]{:S(2)}) collective-permute-start(bf16[512,1024]{1,0:T(8,128)(2,1)} %pad_maximum_fusion.19), channel_id=1, source_target_pairs={{0,4},{1,5},{2,6},{3,7},{4,0},{5,1},{6,2},{7,3},{8,12},{9,13},{10,... | collective-permute-start | bytes 3145736 | tf_op jit(solution)/shard_map/while/body/ppermute | solution.py:512
  682.3 38.9 %all-to-all-start.4 = ((bf16[4,32,2176]{2,1,0:T(8,128)(2,1)}), bf16[4,32,2176]{2,1,0:T(8,128)(2,1)}, u32[]{:S(2)}, u32[]{:S(2)}) async-start(bf16[4,32,2176]{2,1,0:T(8,128)(2,1)} %bitcast.220), calls=%async_computation.4 | async-start | bytes 1114112 | tf_op jit(solution)/shard_map/while/body/all_to_all | solution.py:1370
  692.5 38.2 %collective-permute-start.9 = (bf16[512,1024]{1,0:T(8,128)(2,1)}, bf16[512,1024]{1,0:T(8,128)(2,1)}, u32[]{:S(2)}, u32[]{:S(2)}) collective-permute-start(bf16[512,1024]{1,0:T(8,128)(2,1)} %pad_maximum_fusion.20), channel_id=1, source_target_pairs={{0,2},{1,3},{2,0},{3,1},{4,6},{5,7},{6,4},{7,5},{8,10},{9,11},{10,... | collective-permute-start | bytes 3145736 | tf_op jit(solution)/shard_map/while/body/ppermute | solution.py:512
  696.1 31.2 %collective-permute-start.24 = (bf16[128,1152]{1,0:T(8,128)(2,1)}, bf16[128,1152]{1,0:T(8,128)(2,1)}, u32[]{:S(2)}, u32[]{:S(2)}) collective-permute-start(bf16[128,1152]{1,0:T(8,128)(2,1)} %add_convert_fusion.23), channel_id=1, source_target_pairs={{8,0},{16,24},{9,1},{17,25},{10,2},{18,26},{11,3},{19,27},{12,4},{... | collective-permute-start | bytes 884744 | tf_op jit(solution)/shard_map/while/body/ppermute | solution.py:1384
  723.2 34.8 %all-to-all-start.5 = ((bf16[4,32,2176]{2,1,0:T(8,128)(2,1)}), bf16[4,32,2176]{2,1,0:T(8,128)(2,1)}, u32[]{:S(2)}, u32[]{:S(2)}) async-start(bf16[4,32,2176]{2,1,0:T(8,128)(2,1)} %tile.69), calls=%async_computation.5 | async-start | bytes 1114112 | tf_op jit(solution)/shard_map/while/body/all_to_all | solution.py:1370
  (84 other events, 1465.9 us)
Sparse Core Ops, SparseCore 0:
  291.7 520.6 all-reduce.4

commit v5 on v4

--- a/solution.py
+++ b/solution.py
@@ -492,7 +492,7 @@
 
 def cost(flops, moved, transcendentals=0):
     return pl.CostEstimate(
-        flops=int(flops) // 8, bytes_accessed=int(moved) // 8, transcendentals=int(transcendentals)
+        flops=int(flops), bytes_accessed=int(moved), transcendentals=int(transcendentals)
     )
 
 

time: 847 us -> 843 us (level)
  waiting for transfers between devices: 251 us -> 330 us
  blocking collectives: 35.8 us -> 0 us
  starting transfers between devices: 137 us -> 115 us
  Pallas kernels: 259 us -> 241 us
    all_to_all x9 -> x10, waiting for transfers between devices: 85.2 us -> 161 us  [across(): return lax.all_to_all(values, 'sp', split_axis=0, concat_axis=0, tiled=True)]
    all_to_all x1 -> x0, blocking collectives: 35.8 us -> none  [across(): return lax.all_to_all(values, 'sp', split_axis=0, concat_axis=0, tiled=True)]
    ppermute x47, starting transfers between devices: 75.3 us -> 52.1 us  [flip(): lax.ppermute(value, 'fsdp', [(place, place ^ bit) for place in range(8)])]
    pallas_call x2, Pallas kernels: 51.9 us -> 41.8 us  [attend_back(): pl.pallas_call(attend_back_kernel, out_shape=(shaped((2048, 256), F32), s...]
    all_to_all x9 -> x10, starting transfers between devices: 45.5 us -> 50.5 us  [across(): return lax.all_to_all(values, 'sp', split_axis=0, concat_axis=0, tiled=True)]
  transfers between devices with their start and end apart: 64 -> 65, of which waited for: 25 -> 29; matrix products, arithmetic and copies ran while one was open for 13% -> 12% of each run, Pallas kernels for 23% -> 21%
where the time goes in v5:
time: 843 us; the launch traced here: 833 us
  waiting for transfers between devices  330 us (39%)
  Pallas kernels  241 us (29%)
  starting transfers between devices  115 us (14%)
  other arithmetic  75.1 us (9%)
  local copies, waits for them, and re-layouts  53.8 us (6%)
  between operations  15.5 us (2%)
    all_to_all x10, waiting for transfers between devices, across(): return lax.all_to_all(values, 'sp', split_axis=0, concat_axis=0, tiled=True)  161 us
    ppermute x47, waiting for transfers between devices, flip(): lax.ppermute(value, 'fsdp', [(place, place ^ bit) for place in range(8)])  114 us
    ppermute x47, starting transfers between devices, flip(): lax.ppermute(value, 'fsdp', [(place, place ^ bit) for place in range(8)])  52.1 us
    all_to_all x10, starting transfers between devices, across(): return lax.all_to_all(values, 'sp', split_axis=0, concat_axis=0, tiled=True)  50.5 us
    psum x1, waiting for transfers between devices, fast_local(): sums_of_parts = lax.psum(parts, 'sp')  49.4 us
    pallas_call x2, Pallas kernels, expert_grads(): pl.pallas_call(expert_grad_kernel, out_shape=(shaped((8, 144 * count, 102...  47.4 us
    pallas_call x2, Pallas kernels, attend_back(): pl.pallas_call(attend_back_kernel, out_shape=(shaped((2048, 256), F32), s...  41.8 us
    pallas_call x4, Pallas kernels, combine(): pl.pallas_call(functools.partial(combine_kernel, calls, weighted), out_sh...  33.9 us
  transfers between devices with their start and end apart: 65, of which 29 were waited for; matrix products, arithmetic and copies ran while one was open for 12% of the time, Pallas kernels for 21%

profile of v5, /device:TPU:0, one launch (start us, length us, event | category | flops | bytes accessed | tf_op | source)
XLA Modules:
  0.0 832.9 jit_solution(12170510054659898879)
XLA Ops:
  23.9 10.5 %collective-permute-done.28.refs_4_ = bf16[128,3200]{1,0:T(8,128)(2,1)S(1)} collective-permute-done((bf16[128,3200]{1,0:T(8,128)(2,1)S(1)}, bf16[128,3200]{1,0:T(8,128)(2,1)S(1)}, u32[]{:S(2)}, u32[]{:S(2)}) %collective-permute-start.28) | collective-permute-done | bytes 819232 | tf_op jit(solution)/shard_map/ppermute | solution.py:512
  66.7 23.0 %collective-permute-done.35.refs_2_ = bf16[528,1024]{1,0:T(8,128)(2,1)S(1)} collective-permute-done((bf16[528,1024]{1,0:T(8,128)(2,1)S(1)}, bf16[528,1024]{1,0:T(8,128)(2,1)S(1)}, u32[]{:S(2)}, u32[]{:S(2)}) %collective-permute-start.35) | collective-permute-done | bytes 1081376 | tf_op jit(solution)/shard_map/ppermute | solution.py:512
  101.4 13.1 %attend.2 = (bf16[2048,128]{1,0:T(8,128)(2,1)}, f32[8,2048]{1,0:T(8,128)}) custom-call(s32[4]{0:T(128)} %get-tuple-element.1176.low_ref, bf16[2048,256]{1,0:T(8,128)(2,1)S(1)} %bitcast.228, bf16[2048,128]{1,0:T(8,128)(2,1)} %collective-permute-done.37.halo_ref, s32[4,1,512]{2,1,0:T(1,128)S(1)} %bitcast.236), custom_call_target="tpu_custom_call" | custom-call | flops 12000000000 | bytes 3000000 | tf_op jit(solution)/shard_map/attend/pallas_call | solution.py:730
  114.5 11.6 %all-to-all-done.7 = bf16[4,512,256]{2,1,0:T(8,128)(2,1)S(1)} async-done(((bf16[4,512,256]{2,1,0:T(8,128)(2,1)}), bf16[4,512,256]{2,1,0:T(8,128)(2,1)S(1)}, u32[]{:S(2)}, u32[]{:S(2)}) %all-to-all-start.7) | async-done | bytes 1048608 | tf_op jit(solution)/shard_map/all_to_all | solution.py:1370
  144.1 12.1 %attend.3 = (bf16[2048,128]{1,0:T(8,128)(2,1)}, f32[8,2048]{1,0:T(8,128)}) custom-call(s32[4]{0:T(128)} %get-tuple-element.1176.low_ref, bf16[2048,256]{1,0:T(8,128)(2,1)S(1)} %bitcast.231, bf16[2048,128]{1,0:T(8,128)(2,1)S(1)} %collective-permute-done.38.halo_ref, s32[4,1,512]{2,1,0:T(1,128)S(1)} %bitcast.237), custom_call_target="tpu_custom_call" | custom-call | flops 12000000000 | bytes 3000000 | tf_op jit(solution)/shard_map/attend/pallas_call | solution.py:730
  189.1 23.4 %collective-permute-done.46.refs_2_ = bf16[528,1024]{1,0:T(8,128)(2,1)S(1)} collective-permute-done((bf16[528,1024]{1,0:T(8,128)(2,1)}, bf16[528,1024]{1,0:T(8,128)(2,1)S(1)}, u32[]{:S(2)}, u32[]{:S(2)}) %collective-permute-start.46) | collective-permute-done | bytes 1081376 | tf_op jit(solution)/shard_map/ppermute | solution.py:512
  218.8 9.3 %pick_rows.2 = (bf16[6,576,1024]{2,1,0:T(8,128)(2,1)}, bf16[6,576,128]{2,1,0:T(8,128)(2,1)}, bf16[6,512,128]{2,1,0:T(8,128)(2,1)}) custom-call(s32[1]{0:T(128)} %bitcast.1.me_ref, f32[6,4,512]{2,1,0:T(4,128)} %get-tuple-element.736.slots_ref, bf16[528,1024]{1,0:T(8,128)(2,1)} %get-tuple-element.1631.refs_0_, bf16[528,1024]{1,0:T(8,128)(2,1)} %copy-done.37, ...), custom_call_target="tpu_custom_call" | custom-call | flops 3623878656 | bytes 14400000 | tf_op jit(solution)/shard_map/pick_rows/pallas_call | solution.py:1014
  238.2 23.6 %expert_grads.2 = (bf16[8,288,1024]{2,1,0:T(8,128)(2,1)}, bf16[8,288,512]{2,1,0:T(8,128)(2,1)}, bf16[6144,512]{1,0:T(8,128)(2,1)}) custom-call(bf16[6,576,1024]{2,1,0:T(8,128)(2,1)} %get-tuple-element.744.refs_0_, bf16[2,576,1024]{2,1,0:T(8,128)(2,1)} %get-tuple-element.748.refs_1_, bf16[6,576,1024]{2,1,0:T(8,128)(2,1)} %get-tuple-element.1622.refs_2_, ...), custom_call_target="tpu_custom_call" | custom-call | flops 16000000000 | bytes 30000000 | tf_op jit(solution)/shard_map/expert_grads/pallas_call | solution.py:1080
  261.8 23.8 %expert_grads.3 = (bf16[8,288,1024]{2,1,0:T(8,128)(2,1)}, bf16[8,288,512]{2,1,0:T(8,128)(2,1)}, bf16[6144,512]{1,0:T(8,128)(2,1)}) custom-call(bf16[6,576,1024]{2,1,0:T(8,128)(2,1)} %get-tuple-element.744.refs_0_, bf16[2,576,1024]{2,1,0:T(8,128)(2,1)} %get-tuple-element.748.refs_1_, bf16[6,576,1024]{2,1,0:T(8,128)(2,1)} %get-tuple-element.1622.refs_2_, ...), custom_call_target="tpu_custom_call" | custom-call | flops 16000000000 | bytes 30000000 | tf_op jit(solution)/shard_map/expert_grads/pallas_call | solution.py:1080
  292.6 464.2 %while.29 = (s32[]{:T(128)}, bf16[512,1024]{1,0:T(8,128)(2,1)}, bf16[512,1024]{1,0:T(8,128)(2,1)}, f32[128]{0:T(128)}, f32[128,1024]{1,0:T(8,128)}, /*index=5*/f...) while((s32[]{:T(128)}, bf16[512,1024]{1,0:T(8,128)(2,1)}, ...), condition=%wide.region_6.7_spmd.clone, body=%wide.region_4.6_spmd.clone.sunk | while | flops 95376556032 | bytes 373953760 | solution.py:1545
  292.7 14.1 %expert_rows.8 = (bf16[8,288,1024]{2,1,0:T(8,128)(2,1)}, bf16[8,288,1024]{2,1,0:T(8,128)(2,1)}, bf16[8,288,128]{2,1,0:T(8,128)(2,1)}) custom-call(s32[1]{0:T(128)} %get-tuple-element.1557.me_ref, bf16[8,288,1024]{2,1,0:T(8,128)(2,1)} %get-tuple-element.1736.lin_ref, bf16[8,288,512]{2,1,0:T(8,128)(2,1)} %get-tuple-element.1737.inner_ref, ...), custom_call_target="tpu_custom_call" | custom-call | flops 8000000000 | bytes 28000000 | tf_op jit(solution)/shard_map/while/body/expert_rows/pallas_call | solution.py:1133
  306.8 14.0 %expert_rows.9 = (bf16[8,288,1024]{2,1,0:T(8,128)(2,1)}, bf16[8,288,1024]{2,1,0:T(8,128)(2,1)}, bf16[8,288,128]{2,1,0:T(8,128)(2,1)}) custom-call(s32[1]{0:T(128)} %get-tuple-element.1557.me_ref, bf16[8,288,1024]{2,1,0:T(8,128)(2,1)} %get-tuple-element.1743.lin_ref, bf16[8,288,512]{2,1,0:T(8,128)(2,1)} %get-tuple-element.1744.inner_ref, ...), custom_call_target="tpu_custom_call" | custom-call | flops 8000000000 | bytes 28000000 | tf_op jit(solution)/shard_map/while/body/expert_rows/pallas_call | solution.py:1133
  358.6 22.0 %collective-permute-done.2.sum_x_ref = bf16[528,1024]{1,0:T(8,128)(2,1)S(1)} collective-permute-done((bf16[528,1024]{1,0:T(8,128)(2,1)S(1)}, bf16[528,1024]{1,0:T(8,128)(2,1)S(1)}, u32[]{:S(2)}, u32[]{:S(2)}) %collective-permute-start.2) | collective-permute-done | bytes 1081376 | tf_op jit(solution)/shard_map/while/body/ppermute | solution.py:512
  404.7 16.0 %all-to-all-done = bf16[4,512,128]{2,1,0:T(8,128)(2,1)} async-done(((bf16[4,512,128]{2,1,0:T(8,128)(2,1)}), bf16[4,512,128]{2,1,0:T(8,128)(2,1)}, u32[]{:S(2)}, u32[]{:S(2)}) %all-to-all-start) | async-done | bytes 524320 | tf_op jit(solution)/shard_map/while/body/all_to_all | solution.py:1370
  438.5 20.9 %attend_back.8 = (f32[2048,256]{1,0:T(8,128)}, bf16[2048,128]{1,0:T(8,128)(2,1)}) custom-call(s32[4]{0:T(128)S(1)} %copy-done.44, bf16[2048,256]{1,0:T(8,128)(2,1)} %get-tuple-element.1763.own_ref, bf16[2048,128]{1,0:T(8,128)(2,1)} %get-tuple-element.1764.halo_ref, s32[4,1,512]{2,1,0:T(1,128)S(1)} %copy-done.35, ...), custom_call_target="tpu_custom_call" | custom-call | flops 30000001024 | bytes 6000000 | tf_op jit(solution)/shard_map/while/body/attend_back/pallas_call | solution.py:822
  459.4 9.0 %all-to-all-done.1 = bf16[4,512,128]{2,1,0:T(8,128)(2,1)} async-done(((bf16[4,512,128]{2,1,0:T(8,128)(2,1)}), bf16[4,512,128]{2,1,0:T(8,128)(2,1)}, u32[]{:S(2)}, u32[]{:S(2)}) %all-to-all-start.1) | async-done | bytes 524320 | tf_op jit(solution)/shard_map/while/body/all_to_all | solution.py:1370
  477.9 20.9 %attend_back.9 = (f32[2048,256]{1,0:T(8,128)}, bf16[2048,128]{1,0:T(8,128)(2,1)}) custom-call(s32[4]{0:T(128)S(1)} %copy-done.44, bf16[2048,256]{1,0:T(8,128)(2,1)} %get-tuple-element.1768.own_ref, bf16[2048,128]{1,0:T(8,128)(2,1)} %get-tuple-element.1769.halo_ref, s32[4,1,512]{2,1,0:T(1,128)S(1)} %copy-done.35, ...), custom_call_target="tpu_custom_call" | custom-call | flops 30000001024 | bytes 6000000 | tf_op jit(solution)/shard_map/while/body/attend_back/pallas_call | solution.py:822
  498.8 30.8 %all-to-all-done.2.first_ref = bf16[4,512,256]{2,1,0:T(8,128)(2,1)} async-done(((bf16[4,512,256]{2,1,0:T(8,128)(2,1)}), bf16[4,512,256]{2,1,0:T(8,128)(2,1)}, u32[]{:S(2)}, u32[]{:S(2)}) %all-to-all-start.2) | async-done | bytes 1048608 | tf_op jit(solution)/shard_map/while/body/all_to_all | solution.py:1370
  561.0 41.7 %all-to-all-done.3.second_ref = bf16[4,512,256]{2,1,0:T(8,128)(2,1)} async-done(((bf16[4,512,256]{2,1,0:T(8,128)(2,1)}), bf16[4,512,256]{2,1,0:T(8,128)(2,1)}, u32[]{:S(2)}, u32[]{:S(2)}) %all-to-all-start.3) | async-done | bytes 1048608 | tf_op jit(solution)/shard_map/while/body/all_to_all | solution.py:1370
  602.8 11.6 %input_grads.4 = (bf16[512,1024]{1,0:T(8,128)(2,1)}, bf16[4,128,2176]{2,1,0:T(8,128)(2,1)}, bf16[4,128,2176]{2,1,0:T(8,128)(2,1)}) custom-call(s32[1]{0:T(128)} %get-tuple-element.1557.me_ref, bf16[512,1024]{1,0:T(8,128)(2,1)} %get-tuple-element.1772.tokens_ref, f32[512,128]{1,0:T(8,128)} %copy.77.cos_ref, f32[512,128]{1,0:T(8,128)} %broadcast_multiply_fusion.3.sin_ref, ...), custom_call_target="tpu_custom_call" | custom-call | flops 4294967296 | bytes 15000000 | tf_op jit(solution)/shard_map/while/body/input_grads/pallas_call | solution.py:1339
  666.4 9.7 %collective-permute-done.14 = bf16[128,2176]{1,0:T(8,128)(2,1)S(1)} collective-permute-done((bf16[128,2176]{1,0:T(8,128)(2,1)S(1)}, bf16[128,2176]{1,0:T(8,128)(2,1)S(1)}, u32[]{:S(2)}, u32[]{:S(2)}) %collective-permute-start.14) | collective-permute-done | bytes 557088 | tf_op jit(solution)/shard_map/while/body/ppermute | solution.py:512
  690.3 21.5 %all-to-all-done.4 = bf16[4,32,2176]{2,1,0:T(8,128)(2,1)} async-done(((bf16[4,32,2176]{2,1,0:T(8,128)(2,1)}), bf16[4,32,2176]{2,1,0:T(8,128)(2,1)}, u32[]{:S(2)}, u32[]{:S(2)}) %all-to-all-start.4) | async-done | bytes 557088 | tf_op jit(solution)/shard_map/while/body/all_to_all | solution.py:1370
  728.5 22.2 %all-to-all-done.5 = bf16[4,32,2176]{2,1,0:T(8,128)(2,1)} async-done(((bf16[4,32,2176]{2,1,0:T(8,128)(2,1)}), bf16[4,32,2176]{2,1,0:T(8,128)(2,1)}, u32[]{:S(2)}, u32[]{:S(2)}) %all-to-all-start.5) | async-done | bytes 557088 | tf_op jit(solution)/shard_map/while/body/all_to_all | solution.py:1370
  758.3 49.4 %all-reduce.5.cloned.1.call-done = (bf16[6144,512]{1,0:T(8,128)(2,1)}, bf16[6144,512]{1,0:T(8,128)(2,1)}) async-done(((bf16[6144,512]{1,0:T(8,128)(2,1)}, bf16[6144,512]{1,0:T(8,128)(2,1)}), (bf16[6144,512]{1,0:T(8,128)(2,1)}, bf16[6144,512]{1,0:T(8,128)(2,1)})) %all-reduce.5.cloned.1.call-update) | async-done | bytes 12582928 | tf_op jit(solution)/shard_map/psum | solution.py:1473
  (342 shorter events, 360.2 us)
Async XLA Ops:
  11.0 38.6 %collective-permute-start.25 = (bf16[128,3200]{1,0:T(8,128)(2,1)S(1)}, bf16[128,3200]{1,0:T(8,128)(2,1)S(1)}, u32[]{:S(2)}, u32[]{:S(2)}) collective-permute-start(bf16[128,3200]{1,0:T(8,128)(2,1)S(1)} %concatenate.90.refs_0_), channel_id=1, source_target_pairs={{0,1},{1,0},{2,3},{3,2},{4,5},{5,4},{6,7},{7,6},{8,9},{9,8},{10,11... | collective-permute-start | bytes 2457608 | tf_op jit(solution)/shard_map/ppermute | solution.py:512
  58.1 33.0 %all-to-all-start.6 = ((bf16[4,512,256]{2,1,0:T(8,128)(2,1)}), bf16[4,512,256]{2,1,0:T(8,128)(2,1)S(1)}, u32[]{:S(2)}, u32[]{:S(2)}) async-start(bf16[4,512,256]{2,1,0:T(8,128)(2,1)} %get-tuple-element.709), calls=%async_computation.6 | async-start | bytes 2097152 | tf_op jit(solution)/shard_map/all_to_all | solution.py:1370
  63.7 26.1 %collective-permute-start.35 = (bf16[528,1024]{1,0:T(8,128)(2,1)S(1)}, bf16[528,1024]{1,0:T(8,128)(2,1)S(1)}, u32[]{:S(2)}, u32[]{:S(2)}) collective-permute-start(bf16[528,1024]{1,0:T(8,128)(2,1)S(1)} %maximum_maximum_fusion.refs_0_), channel_id=1, source_target_pairs={{0,2},{1,3},{2,0},{3,1},{4,6},{5,7},{6,4},{7,5},{8,10},{9,11},{10,... | collective-permute-start | bytes 3244040 | tf_op jit(solution)/shard_map/ppermute | solution.py:512
  94.1 32.1 %all-to-all-start.7 = ((bf16[4,512,256]{2,1,0:T(8,128)(2,1)}), bf16[4,512,256]{2,1,0:T(8,128)(2,1)S(1)}, u32[]{:S(2)}, u32[]{:S(2)}) async-start(bf16[4,512,256]{2,1,0:T(8,128)(2,1)} %get-tuple-element.714), calls=%async_computation.7 | async-start | bytes 2097152 | tf_op jit(solution)/shard_map/all_to_all | solution.py:1370
  100.6 31.9 %collective-permute-start.39 = (bf16[528,1024]{1,0:T(8,128)(2,1)}, bf16[528,1024]{1,0:T(8,128)(2,1)}, u32[]{:S(2)}, u32[]{:S(2)}) collective-permute-start(bf16[528,1024]{1,0:T(8,128)(2,1)} %copy-done.26), channel_id=1, source_target_pairs={{0,1},{1,0},{2,3},{3,2},{4,5},{5,4},{6,7},{7,6},{8,9},{9,8},{10,11... | collective-permute-start | bytes 3244040 | tf_op jit(solution)/shard_map/ppermute | solution.py:512
  101.4 31.2 %collective-permute-start.40 = (bf16[528,1024]{1,0:T(8,128)(2,1)}, bf16[528,1024]{1,0:T(8,128)(2,1)}, u32[]{:S(2)}, u32[]{:S(2)}) collective-permute-start(bf16[528,1024]{1,0:T(8,128)(2,1)} %collective-permute-done.36.refs_4_), channel_id=1, source_target_pairs={{0,1},{1,0},{2,3},{3,2},{4,5},{5,4},{6,7},{7,6},{8,9},{9,8},{10,11... | collective-permute-start | bytes 3244040 | tf_op jit(solution)/shard_map/ppermute | solution.py:512
  165.7 642.0 %all-reduce.5.cloned.1.call-start = ((), (), s32[]{:S(2)}) async-start(), calls=%async_computation.10 | async-start | bytes 25165824 | tf_op jit(solution)/shard_map/psum | solution.py:1473
  189.1 27.7 %collective-permute-start.45 = (bf16[528,1024]{1,0:T(8,128)(2,1)}, bf16[528,1024]{1,0:T(8,128)(2,1)S(1)}, u32[]{:S(2)}, u32[]{:S(2)}) collective-permute-start(bf16[528,1024]{1,0:T(8,128)(2,1)} %get-tuple-element.1631.refs_0_), channel_id=1, source_target_pairs={{0,1},{1,0},{2,3},{3,2},{4,5},{5,4},{6,7},{7,6},{8,9},{9,8},{10,11... | collective-permute-start | bytes 3244040 | tf_op jit(solution)/shard_map/ppermute | solution.py:512
  354.3 26.4 %collective-permute-start.2 = (bf16[528,1024]{1,0:T(8,128)(2,1)S(1)}, bf16[528,1024]{1,0:T(8,128)(2,1)S(1)}, u32[]{:S(2)}, u32[]{:S(2)}) collective-permute-start(bf16[528,1024]{1,0:T(8,128)(2,1)S(1)} %pad_maximum_fusion.17), channel_id=1, source_target_pairs={{0,2},{1,3},{2,0},{3,1},{4,6},{5,7},{6,4},{7,5},{8,10},{9,11},{10,... | collective-permute-start | bytes 3244040 | tf_op jit(solution)/shard_map/while/body/ppermute | solution.py:512
  391.0 29.8 %all-to-all-start = ((bf16[4,512,128]{2,1,0:T(8,128)(2,1)}), bf16[4,512,128]{2,1,0:T(8,128)(2,1)}, u32[]{:S(2)}, u32[]{:S(2)}) async-start(bf16[4,512,128]{2,1,0:T(8,128)(2,1)} %get-tuple-element.1567), calls=%async_computation | async-start | bytes 1048576 | tf_op jit(solution)/shard_map/while/body/all_to_all | solution.py:1370
  404.7 65.1 %collective-permute-start.17 = (bf16[4,128,1152]{2,1,0:T(8,128)(2,1)}, bf16[4,128,1152]{2,1,0:T(8,128)(2,1)}, u32[]{:S(2)}, u32[]{:S(2)}) collective-permute-start(bf16[4,128,1152]{2,1,0:T(8,128)(2,1)} %get-tuple-element.1601), channel_id=1, source_target_pairs={{0,1},{1,0},{2,3},{3,2},{4,5},{5,4},{6,7},{7,6},{8,9},{9,8},{10,11... | collective-permute-start | bytes 3538952 | tf_op jit(solution)/shard_map/while/body/ppermute | solution.py:512
  431.8 206.1 %collective-permute-start.5 = (bf16[4,512,1024]{2,1,0:T(8,128)(2,1)}, bf16[4,512,1024]{2,1,0:T(8,128)(2,1)}, u32[]{:S(2)}, u32[]{:S(2)}) collective-permute-start(bf16[4,512,1024]{2,1,0:T(8,128)(2,1)} %combine.18), channel_id=1, source_target_pairs={{0,1},{1,0},{2,3},{3,2},{4,5},{5,4},{6,7},{7,6},{8,9},{9,8},{10,11... | collective-permute-start | bytes 12582920 | tf_op jit(solution)/shard_map/while/body/ppermute | solution.py:512
  431.9 36.5 %all-to-all-start.1 = ((bf16[4,512,128]{2,1,0:T(8,128)(2,1)}), bf16[4,512,128]{2,1,0:T(8,128)(2,1)}, u32[]{:S(2)}, u32[]{:S(2)}) async-start(bf16[4,512,128]{2,1,0:T(8,128)(2,1)} %get-tuple-element.1580), calls=%async_computation.1 | async-start | bytes 1048576 | tf_op jit(solution)/shard_map/while/body/all_to_all | solution.py:1370
  473.7 55.9 %all-to-all-start.2 = ((bf16[4,512,256]{2,1,0:T(8,128)(2,1)}), bf16[4,512,256]{2,1,0:T(8,128)(2,1)}, u32[]{:S(2)}, u32[]{:S(2)}) async-start(bf16[4,512,256]{2,1,0:T(8,128)(2,1)} %bitcast.219), calls=%async_computation.2 | async-start | bytes 2097152 | tf_op jit(solution)/shard_map/while/body/all_to_all | solution.py:1370
  546.0 56.8 %all-to-all-start.3 = ((bf16[4,512,256]{2,1,0:T(8,128)(2,1)}), bf16[4,512,256]{2,1,0:T(8,128)(2,1)}, u32[]{:S(2)}, u32[]{:S(2)}) async-start(bf16[4,512,256]{2,1,0:T(8,128)(2,1)} %bitcast.218), calls=%async_computation.3 | async-start | bytes 2097152 | tf_op jit(solution)/shard_map/while/body/all_to_all | solution.py:1370
  554.3 65.1 %collective-permute-start.19 = (bf16[128,1152]{1,0:T(8,128)(2,1)}, bf16[128,1152]{1,0:T(8,128)(2,1)}, u32[]{:S(2)}, u32[]{:S(2)}) collective-permute-start(bf16[128,1152]{1,0:T(8,128)(2,1)} %pad_maximum_fusion.23), channel_id=1, source_target_pairs={{0,4},{1,5},{2,6},{3,7},{4,0},{5,1},{6,2},{7,3},{8,12},{9,13},{10,... | collective-permute-start | bytes 884744 | tf_op jit(solution)/shard_map/while/body/ppermute | solution.py:512
  560.5 58.9 %collective-permute-start.21 = (bf16[128,1152]{1,0:T(8,128)(2,1)}, bf16[128,1152]{1,0:T(8,128)(2,1)}, u32[]{:S(2)}, u32[]{:S(2)}) collective-permute-start(bf16[128,1152]{1,0:T(8,128)(2,1)} %pad_maximum_fusion.24), channel_id=1, source_target_pairs={{0,2},{1,3},{2,0},{3,1},{4,6},{5,7},{6,4},{7,5},{8,10},{9,11},{10,... | collective-permute-start | bytes 884744 | tf_op jit(solution)/shard_map/while/body/ppermute | solution.py:512
  614.4 32.9 %collective-permute-start.12 = (bf16[4,128,2176]{2,1,0:T(8,128)(2,1)}, bf16[4,128,2176]{2,1,0:T(8,128)(2,1)}, u32[]{:S(2)}, u32[]{:S(2)}) collective-permute-start(bf16[4,128,2176]{2,1,0:T(8,128)(2,1)} %get-tuple-element.1591), channel_id=1, source_target_pairs={{0,1},{1,0},{2,3},{3,2},{4,5},{5,4},{6,7},{7,6},{8,9},{9,8},{10,11... | collective-permute-start | bytes 6684680 | tf_op jit(solution)/shard_map/while/body/ppermute | solution.py:512
  636.5 50.8 %collective-permute-start.23 = (bf16[128,1152]{1,0:T(8,128)(2,1)S(1)}, bf16[128,1152]{1,0:T(8,128)(2,1)}, u32[]{:S(2)}, u32[]{:S(2)}) collective-permute-start(bf16[128,1152]{1,0:T(8,128)(2,1)S(1)} %add_convert_fusion.22), channel_id=1, source_target_pairs={{8,16},{16,8},{9,17},{17,9},{10,18},{18,10},{11,19},{19,11},{12,20... | collective-permute-start | bytes 884744 | tf_op jit(solution)/shard_map/while/body/ppermute | solution.py:1383
  664.2 60.2 %collective-permute-start.7 = (bf16[512,1024]{1,0:T(8,128)(2,1)}, bf16[512,1024]{1,0:T(8,128)(2,1)}, u32[]{:S(2)}, u32[]{:S(2)}) collective-permute-start(bf16[512,1024]{1,0:T(8,128)(2,1)} %pad_maximum_fusion.19), channel_id=1, source_target_pairs={{0,4},{1,5},{2,6},{3,7},{4,0},{5,1},{6,2},{7,3},{8,12},{9,13},{10,... | collective-permute-start | bytes 3145736 | tf_op jit(solution)/shard_map/while/body/ppermute | solution.py:512
  678.2 33.6 %all-to-all-start.4 = ((bf16[4,32,2176]{2,1,0:T(8,128)(2,1)}), bf16[4,32,2176]{2,1,0:T(8,128)(2,1)}, u32[]{:S(2)}, u32[]{:S(2)}) async-start(bf16[4,32,2176]{2,1,0:T(8,128)(2,1)} %bitcast.220), calls=%async_computation.4 | async-start | bytes 1114112 | tf_op jit(solution)/shard_map/while/body/all_to_all | solution.py:1370
  686.0 38.4 %collective-permute-start.9 = (bf16[512,1024]{1,0:T(8,128)(2,1)}, bf16[512,1024]{1,0:T(8,128)(2,1)}, u32[]{:S(2)}, u32[]{:S(2)}) collective-permute-start(bf16[512,1024]{1,0:T(8,128)(2,1)} %pad_maximum_fusion.20), channel_id=1, source_target_pairs={{0,2},{1,3},{2,0},{3,1},{4,6},{5,7},{6,4},{7,5},{8,10},{9,11},{10,... | collective-permute-start | bytes 3145736 | tf_op jit(solution)/shard_map/while/body/ppermute | solution.py:512
  689.1 32.1 %collective-permute-start.24 = (bf16[128,1152]{1,0:T(8,128)(2,1)}, bf16[128,1152]{1,0:T(8,128)(2,1)}, u32[]{:S(2)}, u32[]{:S(2)}) collective-permute-start(bf16[128,1152]{1,0:T(8,128)(2,1)} %add_convert_fusion.23), channel_id=1, source_target_pairs={{8,0},{16,24},{9,1},{17,25},{10,2},{18,26},{11,3},{19,27},{12,4},{... | collective-permute-start | bytes 884744 | tf_op jit(solution)/shard_map/while/body/ppermute | solution.py:1384
  713.8 36.9 %all-to-all-start.5 = ((bf16[4,32,2176]{2,1,0:T(8,128)(2,1)}), bf16[4,32,2176]{2,1,0:T(8,128)(2,1)}, u32[]{:S(2)}, u32[]{:S(2)}) async-start(bf16[4,32,2176]{2,1,0:T(8,128)(2,1)} %tile.69), calls=%async_computation.5 | async-start | bytes 1114112 | tf_op jit(solution)/shard_map/while/body/all_to_all | solution.py:1370
  (86 other events, 1202.4 us)
Sparse Core Ops, SparseCore 0:
  285.7 521.9 all-reduce.4
